TPU v7x, 32 devices: a whole 2x2x4 slice. The times are simulated.
32 devices in a mesh: labels: 8 (over z, y), heads: 4 (over x, core).
Axes of the slice: x: 2, y: 2, z: 4, core: 2. Of those that a mesh axis runs over, the one named last changes fastest.
Arguments:
- hidden_in: bfloat16 [4096, 768], P('labels', 'heads'), may hold values from -6 to 6
- w_up: bfloat16 [768, 3072], P(None, 'heads'), may hold values from -0.21875 to 0.21875
- w_down: bfloat16 [3072, 768], P('heads'), may hold values from -0.109375 to 0.109375
- norm_gain: float32 [768], replicated, may hold values from 0.25 to 1.75
- title_length: int32 [256], P('labels'), may hold values from 1 to 16
- label_leaf: int32 [256], P('labels'), may hold values from 0 to 63, as said below
- leaf_parent: int32 [64], P('labels'), may hold values from 0 to 15
Outputs:
- label_embed: bfloat16 [256, 768], P('labels')
- leaf_centers: float32 [64, 768], P('labels', 'heads')
- parent_sums: float32 [16, 768], P('labels', 'heads')
Inputs may be any that keep to these rules, and one draw needn't show every extreme that they name: `label_leaf`: leaf l belongs to owner l // 8. The 32 labels of one device (an aligned block of 32 labels) name leaves of any one owner at most 8 times; in every draw one owner is named exactly 8 times by every device.
All inputs are finite; a program needn't handle non-finite values.
Results may differ from a plain program's by a relative error of at most 0.009.
Values may be sent and summed in bfloat16 or wider, within the bound.
No kernel may reach another device: no remote copies, remote signals or barrier semaphores. Data moves between devices by JAX's collectives and lax.ppermute only.
A program may use at most 64 MiB of HBM per device.

v0:
```python
import jax
import jax.numpy as jnp
from jax import lax
from jax.sharding import PartitionSpec as P

PAR_DEV = 2


def pool_rows(normed, title_length, labels_here, seq_positions):
    grouped = normed.reshape(labels_here, seq_positions, normed.shape[1])
    keep_mask = (jnp.arange(seq_positions)[None, :] < title_length[:, None]).astype(jnp.float32)
    return (
        jnp.sum(grouped * keep_mask[:, :, None], axis=1) / title_length.astype(jnp.float32)[:, None]
    )


def local(hidden_in, w_up, w_down, norm_gain, title_length, label_leaf, leaf_parent):
    token_rows = hidden_in.shape[0]
    share_cols = hidden_in.shape[1]
    full_width = w_down.shape[1]
    labels_here = label_leaf.shape[0]
    seq_positions = token_rows // labels_here
    leaf_count = leaf_parent.shape[0]
    head_index = lax.axis_index("heads")
    upward = jnp.dot(
        lax.all_gather(hidden_in, "heads", axis=1, tiled=True),
        w_up,
        preferred_element_type=jnp.float32,
    )
    activ = jax.nn.gelu(upward, approximate=False).astype(jnp.bfloat16)
    partial_term = (
        jnp.dot(activ, w_down, preferred_element_type=jnp.float32)
        .astype(jnp.bfloat16)
        .astype(jnp.float32)
    )
    summed = lax.psum_scatter(
        partial_term.astype(jnp.bfloat16), "heads", scatter_dimension=1, tiled=True
    ).astype(jnp.float32)
    mixed_share = (hidden_in.astype(jnp.float32) + summed).astype(jnp.bfloat16)
    mixed = lax.all_gather(mixed_share, "heads", axis=1, tiled=True)
    as_float = mixed.astype(jnp.float32)
    mean_value = jnp.mean(as_float, axis=1, keepdims=True)
    centred = as_float - mean_value
    variance = jnp.mean(centred * centred, axis=1, keepdims=True)
    normed = centred * lax.rsqrt(variance + 1e-05) * norm_gain[None, :]
    pooled = pool_rows(normed, title_length, labels_here, seq_positions)
    scale_inv = lax.rsqrt(jnp.mean(pooled * pooled, axis=1, keepdims=True) + 1e-05)
    label_embed = (pooled * scale_inv).astype(jnp.bfloat16)
    my_columns = lax.dynamic_slice_in_dim(label_embed, head_index * share_cols, share_cols, 1)
    owner_total = lax.axis_size("labels")
    capacity = max(2, 2 * labels_here // owner_total)
    owner_of = label_leaf // leaf_count
    local_leaf = label_leaf - owner_of * leaf_count
    label_order = jnp.arange(labels_here)
    earlier = (owner_of[None, :] == owner_of[:, None]) & (
        label_order[None, :] < label_order[:, None]
    )
    slot_rank = jnp.sum(earlier.astype(jnp.int32), axis=1)
    target_slot = owner_of * capacity + slot_rank
    slot_ids = jnp.arange(owner_total * capacity)
    placing = slot_ids[:, None] == target_slot[None, :]
    outgoing = jnp.dot(placing.astype(jnp.bfloat16), my_columns, preferred_element_type=jnp.float32)
    outgoing = outgoing.astype(jnp.bfloat16).reshape(owner_total, capacity, share_cols)
    slot_leaf = jnp.sum(placing.astype(jnp.int32) * (local_leaf + 1)[None, :], axis=1) - 1
    slot_leaf = slot_leaf.reshape(owner_total, capacity)
    arrived, arrived_leaf = (
        lax.all_to_all(outgoing, "labels", split_axis=0, concat_axis=0, tiled=True),
        lax.all_to_all(slot_leaf, "labels", split_axis=0, concat_axis=0, tiled=True),
    )
    picker = (jnp.arange(leaf_count)[:, None] == arrived_leaf.reshape(1, -1)).astype(jnp.bfloat16)
    leaf_sum = jnp.dot(picker, arrived.reshape(-1, share_cols), preferred_element_type=jnp.float32)
    squares = lax.psum(jnp.sum(leaf_sum * leaf_sum, axis=1), "heads")
    leaf_centers = leaf_sum * lax.rsqrt(squares / full_width + 1e-05)[:, None]
    wanted = jnp.arange(PAR_DEV * lax.axis_size("labels"))
    picker = (wanted[:, None] == leaf_parent[None, :]).astype(jnp.float32)
    parent_sums = lax.psum_scatter(
        jnp.dot(
            picker,
            leaf_centers,
            preferred_element_type=jnp.float32,
            precision=lax.Precision.HIGHEST,
        ),
        "labels",
        scatter_dimension=0,
        tiled=True,
    )
    return (label_embed, leaf_centers, parent_sums)


def solution(mesh):
    in_specs = (
        P("labels", "heads"),
        P(None, "heads"),
        P("heads", None),
        P(),
        P("labels"),
        P("labels"),
        P("labels"),
    )
    out_specs = (P("labels", None), P("labels", "heads"), P("labels", "heads"))
    return jax.shard_map(local, mesh=mesh, in_specs=in_specs, out_specs=out_specs, check_vma=False)
```

profile of v0, /device:TPU:0, one launch (start us, length us, event | category | flops | bytes accessed | tf_op | source)
XLA Modules:
  0.0 122.8 jit_solution(3448685862517830747)
XLA Ops:
  7.2 0.0 copy-start
  7.2 0.0 reduce-scatter.2.cloned.1.call-start
  7.2 10.4 %all_gather.6 = bf16[512,768]{0,1:T(8,128)(2,1)S(1)} all-gather(bf16[512,192]{0,1:T(8,128)(2,1)} %param.7), channel_id=1, replica_groups=mesh['labels'=8,'heads'=4] {'heads'}, dimensions={1}, use_global_device_ids=true | all-gather | bytes 983040 | tf_op jit(solution)/shard_map/all_gather | solution.py:26
  17.6 0.0 copy-done
  17.6 0.0 copy-start.7
  17.6 0.0 copy-start.5
  17.6 0.0 copy-start.1
  17.6 6.9 %convolution_convert_fusion = bf16[512,768]{0,1:T(8,128)(2,1)} fusion(bf16[768,768]{1,0:T(8,128)(2,1)S(1)} %copy-done, bf16[512,768]{0,1:T(8,128)(2,1)S(1)} %all_gather.6, bf16[768,768]{1,0:T(8,128)(2,1)} %param.8), kind=kOutput, calls=%fused_computation.26 | convolution fusion | flops 1233911808 | bytes 3932160 | tf_op jit(solution)/shard_map/dot_general | solution.py:32
  24.6 0.0 reduce-scatter.2.cloned.1.call-update
  24.6 0.0 copy-done.7
  24.6 0.2 convert_reduce_fusion.1
  24.8 0.1 select_reduce_fusion
  24.9 0.7 sub.28
  25.6 5.8 %all-to-all-start = ((s32[8,1,8]{2,1,0:T(1,128)}), s32[8,1,8]{2,1,0:T(1,128)S(1)}, u32[]{:S(2)}, u32[]{:S(2)}) async-start(s32[8,1,8]{2,1,0:T(1,128)} %bitcast.1), calls=%async_computation.1 | async-start | bytes 8192 | tf_op jit(solution)/shard_map/all_to_all | solution.py:68
  31.4 0.0 copy-done.5
  31.5 0.1 fusion.48
  31.5 0.0 copy-start.4
  31.5 17.4 %reduce-scatter.2.cloned.1.call-done = bf16[512,192]{0,1:T(8,128)(2,1)} async-done(((bf16[512,768]{0,1:T(8,128)(2,1)}), bf16[512,192]{0,1:T(8,128)(2,1)}) %reduce-scatter.2.cloned.1.call-update) | async-done | bytes 196624 | tf_op jit(solution)/shard_map/reduce_scatter | solution.py:36
  48.9 0.0 copy-done.1
  48.9 1.0 add_convert_fusion
  49.9 8.2 %all_gather.7 = bf16[512,768]{0,1:T(8,128)(2,1)S(1)} all-gather(bf16[512,192]{0,1:T(8,128)(2,1)S(1)} %add_convert_fusion), channel_id=1, replica_groups=mesh['labels'=8,'heads'=4] {'heads'}, dimensions={1}, use_global_device_ids=true | all-gather | bytes 983040 | tf_op jit(solution)/shard_map/all_gather | solution.py:40
  58.1 0.2 convert_reduce_fusion
  58.2 0.3 fusion.2
  58.5 0.0 copy-done.4
  58.5 0.2 fusion.3
  58.8 1.6 %copy.13 = f32[512,768]{1,0:T(8,128)} copy(f32[512,768]{0,1:T(8,128)S(1)} %fusion.3) | data formatting | bytes 3145728 | tf_op jit(solution)/shard_map/mul | solution.py:45
  60.4 1.8 %multiply_reduce_fusion = f32[32,768]{1,0:T(8,128)S(1)} fusion(f32[32,16]{1,0:T(8,128)S(1)} %fusion.48, f32[512,768]{1,0:T(8,128)} %copy.13), kind=kLoop, calls=%fused_computation.10 | loop fusion | flops 761856 | bytes 1673216 | tf_op jit(solution)/shard_map/reduce_sum | solution.py:13
  62.2 0.2 multiply_reduce_fusion.1
  62.4 0.1 multiply_convert_fusion
  62.5 0.0 copy-start.2
  62.5 0.9 fusion.14
  63.4 0.0 all-to-all-done
  63.4 5.5 %all-to-all-start.1 = ((bf16[8,8,192]{2,1,0:T(8,128)(2,1)}), bf16[8,8,192]{2,1,0:T(8,128)(2,1)S(1)}, u32[]{:S(2)}, u32[]{:S(2)}) async-start(bf16[8,8,192]{2,1,0:T(8,128)(2,1)} %fusion.14), calls=%async_computation.2 | async-start | bytes 65536 | tf_op jit(solution)/shard_map/all_to_all | solution.py:67
  68.9 0.0 copy-done.8
  68.9 0.6 dynamic-slice
  70.1 0.5 broadcast.112
  70.7 0.7 reduce.3
  71.3 0.1 eq.61
  71.4 4.2 %all-to-all-done.1 = bf16[8,8,192]{2,1,0:T(8,128)(2,1)S(1)} async-done(((bf16[8,8,192]{2,1,0:T(8,128)(2,1)}), bf16[8,8,192]{2,1,0:T(8,128)(2,1)S(1)}, u32[]{:S(2)}, u32[]{:S(2)}) %all-to-all-start.1) | async-done | bytes 24608 | tf_op jit(solution)/shard_map/all_to_all | solution.py:67
  75.6 0.2 multiply_reduce_fusion.2
  75.8 5.7 %psum.7 = f32[8]{0:T(128)S(1)} all-reduce(f32[8]{0:T(128)S(1)} %get-tuple-element.5), channel_id=1, replica_groups=mesh['labels'=8,'heads'=4] {'heads'}, use_global_device_ids=true, to_apply=%region_8.9 | all-reduce | flops 8 | bytes 64 | tf_op jit(solution)/shard_map/psum | solution.py:72
  81.5 0.1 broadcast_multiply_fusion
  81.6 0.0 copy-done.6
  81.6 0.1 fusion.51
  81.7 33.7 %all-reduce = f32[16,192]{1,0:T(8,128)S(1)} all-reduce(f32[16,192]{1,0:T(8,128)S(1)} %fusion.51), channel_id=3, replica_groups=mesh['labels'=8,'heads'=4] {'labels'}, use_global_device_ids=true, to_apply=%region_9.10.clone | all-reduce | flops 3072 | bytes 24576
  115.4 0.6 constant_dynamic-slice_fusion
  116.0 0.0 copy-done.2
  116.0 0.0 copy-done.3
  (11 shorter events, 0.1 us)
Async XLA Ops:
  7.2 10.5 %copy-start = (bf16[768,768]{1,0:T(8,128)(2,1)S(1)}, bf16[768,768]{1,0:T(8,128)(2,1)}, u32[]{:S(2)}) copy-start(bf16[768,768]{1,0:T(8,128)(2,1)} %param.9) | copy-start | bytes 3538948
  7.2 41.7 %reduce-scatter.2.cloned.1.call-start = ((), (), s32[]{:S(2)}) async-start(), calls=%async_computation.3 | async-start | bytes 983040 | tf_op jit(solution)/shard_map/reduce_scatter | solution.py:36
  17.6 7.0 %copy-start.7 = (s32[32]{0:T(128)S(1)}, s32[32]{0:T(128)}, u32[]{:S(2)}) copy-start(s32[32]{0:T(128)} %param.12) | copy-start | bytes 388
  17.6 13.8 %copy-start.5 = (s32[32]{0:T(128)S(1)}, s32[32]{0:T(128)}, u32[]{:S(2)}) copy-start(s32[32]{0:T(128)} %param.11) | copy-start | bytes 388
  17.6 31.3 %copy-start.1 = (bf16[512,192]{0,1:T(8,128)(2,1)S(1)}, bf16[512,192]{0,1:T(8,128)(2,1)}, u32[]{:S(2)}) copy-start(bf16[512,192]{0,1:T(8,128)(2,1)} %param.7) | copy-start | bytes 589828
  25.6 37.8 %all-to-all-start = ((s32[8,1,8]{2,1,0:T(1,128)}), s32[8,1,8]{2,1,0:T(1,128)S(1)}, u32[]{:S(2)}, u32[]{:S(2)}) async-start(s32[8,1,8]{2,1,0:T(1,128)} %bitcast.1), calls=%async_computation.1 | async-start | bytes 8192 | tf_op jit(solution)/shard_map/all_to_all | solution.py:68
  31.5 27.0 %copy-start.4 = (f32[768]{0:T(1024)S(1)}, f32[768]{0:T(1024)}, u32[]{:S(2)}) copy-start(f32[768]{0:T(1024)} %param.10) | copy-start | bytes 9220
  60.4 8.5 %copy-start.8 = (u32[32]{0:T(128)S(1)}, u32[32]{0:T(128)}, u32[]{:S(2)}) copy-start(u32[32]{0:T(128)} %constant.106) | copy-start | bytes 388
  60.4 21.2 %copy-start.6 = (s32[8]{0:T(128)S(1)}, s32[8]{0:T(128)}, u32[]{:S(2)}) copy-start(s32[8]{0:T(128)} %param.13) | copy-start | bytes 100
  62.5 53.5 %copy-start.2 = (bf16[32,768]{1,0:T(8,128)(2,1)}, bf16[32,768]{1,0:T(8,128)(2,1)S(1)}, u32[]{:S(2)}) copy-start(bf16[32,768]{1,0:T(8,128)(2,1)S(1)} %multiply_convert_fusion) | copy-start | bytes 147460
  63.4 12.2 %all-to-all-start.1 = ((bf16[8,8,192]{2,1,0:T(8,128)(2,1)}), bf16[8,8,192]{2,1,0:T(8,128)(2,1)S(1)}, u32[]{:S(2)}, u32[]{:S(2)}) async-start(bf16[8,8,192]{2,1,0:T(8,128)(2,1)} %fusion.14), calls=%async_computation.2 | async-start | bytes 65536 | tf_op jit(solution)/shard_map/all_to_all | solution.py:67
  81.6 34.4 %copy-start.3 = (f32[8,192]{1,0:T(8,128)}, f32[8,192]{1,0:T(8,128)S(1)}, u32[]{:S(2)}) copy-start(f32[8,192]{1,0:T(8,128)S(1)} %broadcast_multiply_fusion) | copy-start | bytes 18436
Sparse Core Ops, SparseCore 0:
  24.7 24.1 reduce-scatter.1
where the time goes:
time: 123 us
  blocking collectives  58 us (47%)
  waiting for transfers between devices  21.6 us (18%)
  between operations  14.8 us (12%)
  starting transfers between devices  11.4 us (9%)
  matrix products  8.17 us (7%)
  other arithmetic  4.85 us (4%)
  local copies, waits for them, and re-layouts  4.1 us (3%)
    unnamed x1, blocking collectives  33.7 us
    reduce_scatter x1, waiting for transfers between devices, local(): lax.psum_scatter(partial_term.astype(jnp.bfloat16), 'heads', scatter_dime...  17.4 us
    all_gather x1, blocking collectives, local(): lax.all_gather(hidden_in, 'heads', axis=1, tiled=True)  10.4 us
    all_gather x1, blocking collectives, local(): mixed = lax.all_gather(mixed_share, 'heads', axis=1, tiled=True)  8.2 us
    dot_general x1, matrix products, local(): jnp.dot(activ, w_down, preferred_element_type=jnp.float32)  6.95 us
    all_to_all x1, starting transfers between devices, local(): lax.all_to_all(slot_leaf, 'labels', split_axis=0, concat_axis=0, tiled=True)  5.83 us
    psum x1, blocking collectives, local(): squares = lax.psum(jnp.sum(leaf_sum * leaf_sum, axis=1), 'heads')  5.66 us
    all_to_all x1, starting transfers between devices, local(): lax.all_to_all(outgoing, 'labels', split_axis=0, concat_axis=0, tiled=True)  5.52 us
  transfers between devices with their start and end apart: 3, of which 2 were waited for; matrix products, arithmetic and copies ran while one was open for 7% of the time, Pallas kernels for 0%

commit v1 on v0

v1 whole, which is shorter than its diff:
```python
import functools

import jax
import jax.numpy as jnp
from jax import lax
from jax.experimental import pallas as pl
from jax.experimental.pallas import tpu as pltpu
from jax.sharding import PartitionSpec as P

PAR_DEV = 2
BASE = 128
LANES = 128
UNIT_TILE = 256
VMEM = pl.BlockSpec(memory_space=pltpu.VMEM)
SMEM = pl.BlockSpec(memory_space=pltpu.SMEM)
VMEM_LIMIT = 48 * 1024 * 1024


def call(kernel, out_shape, operands, in_specs, scratch=(), flops=0, bytes_accessed=0):
    return pl.pallas_call(
        kernel,
        out_shape=out_shape,
        in_specs=in_specs,
        out_specs=jax.tree.map(lambda _: VMEM, out_shape),
        scratch_shapes=list(scratch),
        compiler_params=pltpu.CompilerParams(vmem_limit_bytes=VMEM_LIMIT),
        cost_estimate=pl.CostEstimate(
            flops=flops, bytes_accessed=bytes_accessed, transcendentals=0
        ),
    )(*operands)


def split_kernel(place_ref, hidden_ref, mine_ref, other_ref):
    core = place_ref[0] % 2
    quarter = mine_ref.shape[1] // 2
    for pair in range(2):
        to = slice(pair * quarter, (pair + 1) * quarter)
        mine = pl.multiple_of((2 * pair + core) * quarter, quarter)
        other = pl.multiple_of((2 * pair + 1 - core) * quarter, quarter)
        mine_ref[:, to] = hidden_ref[:, pl.ds(mine, quarter)]
        other_ref[:, to] = hidden_ref[:, pl.ds(other, quarter)]


def feed_forward(place_ref, pieces, weights, gathered, own_quarter):
    head = place_ref[0]
    share, both = pieces[0].shape
    quarter = both // 2
    pair = head // 2
    if not own_quarter:
        pair = 1 - pair
    columns = pl.ds(pl.multiple_of(pair * quarter, quarter), quarter)
    for flip, piece in enumerate(pieces):
        source = head ^ flip
        rows = pl.ds(pl.multiple_of(source * share, 64), share)
        gathered[rows, :] = piece[:, columns]
    tokens = gathered[...].T
    total = None
    for up_ref, down_ref in weights:
        units = up_ref.shape[1]
        tile = min(UNIT_TILE, units)
        part = None
        for start in range(0, units, tile):
            upward = jnp.dot(
                tokens, up_ref[:, start : start + tile], preferred_element_type=jnp.float32
            )
            activ = (0.5 * upward * (1.0 + lax.erf(upward * 0.7071067811865476))).astype(
                jnp.bfloat16
            )
            term = jnp.dot(
                activ, down_ref[start : start + tile, :], preferred_element_type=jnp.float32
            )
            part = term if part is None else part + term
        part = part.astype(jnp.bfloat16).astype(jnp.float32)
        total = part if total is None else total + part
    return tokens, total


def give_kernel(place_ref, p0, p1, p2, p3, u0, d0, u1, d1, out_ref, gathered):
    _, total = feed_forward(
        place_ref, (p0, p1, p2, p3), ((u0, d0), (u1, d1)), gathered, own_quarter=False
    )
    out_ref[...] = total.astype(jnp.bfloat16)


def keep_kernel(place_ref, p0, p1, p2, p3, u0, d0, u1, d1, out_ref, gathered):
    tokens, total = feed_forward(
        place_ref, (p0, p1, p2, p3), ((u0, d0), (u1, d1)), gathered, own_quarter=True
    )
    out_ref[...] = tokens.astype(jnp.float32) + total


def embed_kernel(place_ref, length_ref, leaf_ref, parent_ref, kept_ref, came_ref, gain_ref, out_ref):
    head = place_ref[0]
    rows, width = out_ref.shape[0], kept_ref.shape[1]
    seq = kept_ref.shape[0] // rows
    mixed = (kept_ref[...] + came_ref[...].astype(jnp.float32)).astype(jnp.bfloat16)
    as_float = mixed.astype(jnp.float32)
    centred = as_float - jnp.mean(as_float, axis=1, keepdims=True)
    variance = jnp.mean(centred * centred, axis=1, keepdims=True)
    normed = centred * lax.rsqrt(variance + 1e-05) * gain_ref[...]
    position = lax.broadcasted_iota(jnp.int32, (seq, 1), 0)
    row = lax.broadcasted_iota(jnp.int32, (rows, 1), 0)
    lane = lax.broadcasted_iota(jnp.int32, (rows, LANES), 1)
    row_wide = lax.broadcasted_iota(jnp.int32, (rows, LANES), 0)
    pooled = []
    lengths = jnp.ones((rows, 1), jnp.float32)
    indices = jnp.zeros((rows, LANES), jnp.int32)
    for i in range(rows):
        length = length_ref[head * rows + i]
        block = normed[i * seq : (i + 1) * seq]
        pooled.append(
            jnp.sum(jnp.where(position < length, block, 0.0), axis=0, keepdims=True)
        )
        lengths = jnp.where(row == i, length.astype(jnp.float32), lengths)
        leaf = leaf_ref[head * rows + i]
        parent = parent_ref[i]
        for at, digit in enumerate((leaf % BASE, leaf // BASE, parent % BASE, parent // BASE)):
            indices = jnp.where((row_wide == i) & (lane == at), digit, indices)
    pooled = jnp.concatenate(pooled, axis=0) / lengths
    scale = lax.rsqrt(jnp.mean(pooled * pooled, axis=1, keepdims=True) + 1e-05)
    both = jnp.concatenate([pooled * scale, indices.astype(jnp.float32)], axis=1)
    out_ref[...] = both.astype(jnp.bfloat16)


def pick_share(values, head, heads):
    share = values.shape[1] // heads
    result = values[:, :share]
    for other in range(1, heads):
        result = jnp.where(head == other, values[:, other * share : (other + 1) * share], result)
    return result


def leaf_kernel(
    heads, leaf_count, place_ref, near_ref, far_ref, embed_ref, centers_ref, parents_ref, scratch
):
    head, index = place_ref[0], place_ref[1]
    core = head % 2
    width = embed_ref.shape[1]
    rows = embed_ref.shape[0] // heads
    owners = near_ref.shape[0] // (2 * rows)
    leaves = owners * leaf_count
    wanted = lax.broadcasted_iota(jnp.int32, (leaves, near_ref.shape[0]), 0)
    leaf_sum = jnp.zeros((leaves, width), jnp.float32)
    for ref in (near_ref, far_ref):
        digits = ref[:, width:].astype(jnp.float32)
        turned = digits.T
        leaf = (turned[0:1] + BASE * turned[1:2]).astype(jnp.int32)
        picker = jnp.where(wanted == leaf, 1.0, 0.0).astype(jnp.bfloat16)
        leaf_sum = leaf_sum + jnp.dot(
            picker, ref[:, :width], preferred_element_type=jnp.float32
        )
    squares = jnp.mean(leaf_sum * leaf_sum, axis=1, keepdims=True)
    centers = leaf_sum * lax.rsqrt(squares + 1e-05)
    scratch[...] = centers
    own = scratch[pl.ds(pl.multiple_of(index * leaf_count, leaf_count), leaf_count), :]
    centers_ref[...] = pick_share(own, head, heads)
    digits = near_ref[:, width:].astype(jnp.float32)
    digits = digits.reshape(owners, 2, rows, LANES)[:, 0, :leaf_count].reshape(leaves, LANES)
    parent = (digits[:, 2:3] + BASE * digits[:, 3:4]).astype(jnp.int32)
    sums = [
        jnp.sum(jnp.where(parent == index * PAR_DEV + p, centers, 0.0), axis=0, keepdims=True)
        for p in range(PAR_DEV)
    ]
    parents_ref[...] = pick_share(jnp.concatenate(sums, axis=0), head, heads)
    here = pl.ds(pl.multiple_of(index * 2 * rows, 2 * rows), 2 * rows)
    near = near_ref[here, :width].astype(jnp.float32)
    far = far_ref[here, :width].astype(jnp.float32)
    even, odd = jnp.where(core == 0, near, far), jnp.where(core == 0, far, near)
    embed_ref[...] = jnp.concatenate(
        [part[i * rows : (i + 1) * rows] for i in range(2) for part in (even, odd)], axis=0
    ).astype(jnp.bfloat16)


def local(owners, heads, hidden_in, w_up, w_down, norm_gain, title_length, label_leaf, leaf_parent):
    token_rows, share = hidden_in.shape
    width = w_down.shape[1]
    units = w_up.shape[1]
    labels_here = label_leaf.shape[0]
    leaf_count = leaf_parent.shape[0]
    rows = labels_here // heads
    quarter = token_rows // heads
    place = jnp.stack([lax.axis_index("heads"), lax.axis_index("labels")]).astype(jnp.int32)

    def swap(values, flip):
        return lax.ppermute(values, "heads", [(i, i ^ flip) for i in range(heads)])

    up_far, down_far = swap(w_up, 1), swap(w_down, 1)
    half = jax.ShapeDtypeStruct((share, 2 * quarter), jnp.bfloat16)
    mine, other = call(split_kernel, (half, half), (place, hidden_in.T), [SMEM, VMEM])
    pieces = (mine, swap(other, 1), swap(mine, 2), swap(other, 3))
    operands = (place, *pieces, w_up, w_down, up_far, down_far)
    specs = [SMEM] + [VMEM] * 8
    scratch = [pltpu.VMEM((width, quarter), jnp.bfloat16)]
    flops = 8 * quarter * width * units
    given = call(
        give_kernel,
        jax.ShapeDtypeStruct((quarter, width), jnp.bfloat16),
        operands,
        specs,
        scratch,
        flops,
        8 * width * units,
    )
    came = swap(given, 2)
    kept = call(
        keep_kernel,
        jax.ShapeDtypeStruct((quarter, width), jnp.float32),
        operands,
        specs,
        scratch,
        flops,
        8 * width * units,
    )
    message = call(
        embed_kernel,
        jax.ShapeDtypeStruct((rows, width + LANES), jnp.bfloat16),
        (place, title_length, label_leaf, leaf_parent, kept, came, norm_gain[None, :]),
        [SMEM] * 4 + [VMEM] * 3,
    )
    groups = [
        [owner * heads + head for owner in range(owners) for head in range(core, heads, 2)]
        for core in range(2)
    ]
    members = owners * heads // 2
    near = lax.all_to_all(
        jnp.broadcast_to(message[None], (members,) + message.shape),
        ("labels", "heads"),
        split_axis=0,
        concat_axis=0,
        tiled=True,
        axis_index_groups=groups,
    ).reshape(members * rows, width + LANES)
    far = swap(near, 1)
    return call(
        functools.partial(leaf_kernel, heads, leaf_count),
        (
            jax.ShapeDtypeStruct((labels_here, width), jnp.bfloat16),
            jax.ShapeDtypeStruct((leaf_count, share), jnp.float32),
            jax.ShapeDtypeStruct((PAR_DEV, share), jnp.float32),
        ),
        (place, near, far),
        [SMEM, VMEM, VMEM],
        [pltpu.VMEM((owners * leaf_count, width), jnp.float32)],
    )


def solution(mesh):
    in_specs = (
        P("labels", "heads"),
        P(None, "heads"),
        P("heads", None),
        P(),
        P("labels"),
        P("labels"),
        P("labels"),
    )
    out_specs = (P("labels", None), P("labels", "heads"), P("labels", "heads"))
    body = functools.partial(local, mesh.shape["labels"], mesh.shape["heads"])
    return jax.shard_map(body, mesh=mesh, in_specs=in_specs, out_specs=out_specs, check_vma=False)
```

time: 123 us -> 42.9 us (0.35)
  blocking collectives: 58 us -> 16.2 us
  between operations: 14.8 us -> 0.7 us
  waiting for transfers between devices: 21.6 us -> 9.65 us
  matrix products: 8.17 us -> 0 us
  Pallas kernels: 0 us -> 7.2 us
  starting transfers between devices: 11.4 us -> 5.29 us
  other arithmetic: 4.85 us -> 0.07 us
    unnamed x1 -> x0, blocking collectives: 33.7 us -> none
    all_gather x2 -> x0, blocking collectives: 18.6 us -> none  [the longest x1 10.4 us: local(): lax.all_gather(hidden_in, 'heads', axis=1, tiled=True)]
    reduce_scatter x1 -> x0, waiting for transfers between devices: 17.4 us -> none  [local(): lax.psum_scatter(partial_term.astype(jnp.bfloat16), 'heads', scatter_dime...]
    all_to_all x0 -> x1, blocking collectives: none -> 16.2 us  [local(): lax.all_to_all(jnp.broadcast_to(message[None], (members,) + message.shape...]
    all_to_all x2 -> x0, starting transfers between devices: 11.4 us -> none  [the longest x1 5.83 us: local(): lax.all_to_all(slot_leaf, 'labels', split_axis=0, concat_axis=0, tiled=True)]
    ppermute x0 -> x7, waiting for transfers between devices: none -> 9.65 us  [swap(): return lax.ppermute(values, 'heads', [(i, i ^ flip) for i in range(heads)])]
    dot_general x4 -> x0, matrix products: 8.17 us -> none  [the longest x1 6.95 us: local(): jnp.dot(activ, w_down, preferred_element_type=jnp.float32)]
    pallas_call x0 -> x5, Pallas kernels: none -> 7.2 us  [call(): pl.pallas_call(kernel, out_shape=out_shape, in_specs=in_specs, out_specs=...]
  transfers between devices with their start and end apart: 3 -> 7, of which waited for: 2 -> 4; matrix products, arithmetic and copies ran while one was open for 7% -> 0% of each run, Pallas kernels for 0% -> 6%
where the time goes in v1:
time: 42.9 us; the launch traced here: 42.6 us
  blocking collectives  16.2 us (38%)
  waiting for transfers between devices  9.65 us (22%)
  Pallas kernels  7.2 us (17%)
  starting transfers between devices  5.29 us (12%)
  local copies, waits for them, and re-layouts  3.51 us (8%)
  between operations  0.7 us (2%)
    all_to_all x1, blocking collectives, local(): lax.all_to_all(jnp.broadcast_to(message[None], (members,) + message.shape...  16.2 us
    ppermute x7, waiting for transfers between devices, swap(): return lax.ppermute(values, 'heads', [(i, i ^ flip) for i in range(heads)])  9.65 us
    pallas_call x5, Pallas kernels, call(): pl.pallas_call(kernel, out_shape=out_shape, in_specs=in_specs, out_specs=...  7.2 us
    ppermute x7, starting transfers between devices, swap(): return lax.ppermute(values, 'heads', [(i, i ^ flip) for i in range(heads)])  5.29 us
    unnamed x14, local copies, waits for them, and re-layouts  3.49 us
  transfers between devices with their start and end apart: 7, of which 4 were waited for; matrix products, arithmetic and copies ran while one was open for 0% of the time, Pallas kernels for 6%

profile of v1, /device:TPU:0, one launch (start us, length us, event | category | flops | bytes accessed | tf_op | source)
XLA Modules:
  0.0 42.6 jit_solution(2501665885559054140)
XLA Ops:
  0.6 0.5 %collective-permute-start.3 = (bf16[768,768]{1,0:T(8,128)(2,1)}, bf16[768,768]{1,0:T(8,128)(2,1)S(1)}, u32[]{:S(2)}, u32[]{:S(2)}) collective-permute-start(bf16[768,768]{1,0:T(8,128)(2,1)} %u0.3), channel_id=1, source_target_pairs={{0,1},{1,0},{2,3},{3,2},{4,5},{5,4},{6,7},{7,6},{8,9},{9,8},{10,11... | collective-permute-start | bytes 3538952 | tf_op jit(solution)/shard_map/ppermute | solution.py:185
  1.1 0.1 collective-permute-start.4
  1.2 0.1 pad_add_fusion.place_ref
  1.3 0.0 copy-start.2
  1.3 0.9 %copy-done.2 = bf16[512,192]{0,1:T(8,128)(2,1)S(1)} copy-done((bf16[512,192]{0,1:T(8,128)(2,1)S(1)}, bf16[512,192]{0,1:T(8,128)(2,1)}, u32[]{:S(2)}) %copy-start.2) | copy-done | bytes 196632
  2.2 0.0 copy-start.6
  2.2 0.6 %shard_map.94 = (bf16[192,256]{1,0:T(8,128)(2,1)S(1)}, bf16[192,256]{1,0:T(8,128)(2,1)S(1)}) custom-call(s32[2]{0:T(128)S(1)} %pad_add_fusion.place_ref, bf16[192,512]{1,0:T(8,128)(2,1)S(1)} %bitcast.6), custom_call_target="tpu_custom_call" | custom-call | tf_op jit(solution)/shard_map/pallas_call | solution.py:20
  2.8 3.0 %collective-permute-start.1 = (bf16[192,256]{1,0:T(8,128)(2,1)S(1)}, bf16[192,256]{1,0:T(8,128)(2,1)S(1)}, u32[]{:S(2)}, u32[]{:S(2)}) collective-permute-start(bf16[192,256]{1,0:T(8,128)(2,1)S(1)} %get-tuple-element.5.p0), channel_id=1, source_target_pairs={{0,2},{1,3},{2,0},{3,1},{4,6},{5,7},{6,4},{7,5},{8,10},{9,11},{10,... | collective-permute-start | bytes 294920 | tf_op jit(solution)/shard_map/ppermute | solution.py:185
  5.8 0.0 collective-permute-start
  5.8 0.2 collective-permute-start.2
  6.0 3.0 %collective-permute-done.1.p2 = bf16[192,256]{1,0:T(8,128)(2,1)S(1)} collective-permute-done((bf16[192,256]{1,0:T(8,128)(2,1)S(1)}, bf16[192,256]{1,0:T(8,128)(2,1)S(1)}, u32[]{:S(2)}, u32[]{:S(2)}) %collective-permute-start.1) | collective-permute-done | bytes 98336 | tf_op jit(solution)/shard_map/ppermute | solution.py:185
  9.0 0.0 collective-permute-done.p1
  9.0 1.4 %collective-permute-done.2.p3 = bf16[192,256]{1,0:T(8,128)(2,1)S(1)} collective-permute-done((bf16[192,256]{1,0:T(8,128)(2,1)S(1)}, bf16[192,256]{1,0:T(8,128)(2,1)S(1)}, u32[]{:S(2)}, u32[]{:S(2)}) %collective-permute-start.2) | collective-permute-done | bytes 98336 | tf_op jit(solution)/shard_map/ppermute | solution.py:185
  10.4 0.0 collective-permute-done.3.u1
  10.4 0.0 collective-permute-done.4.d1
  10.4 0.0 copy-start
  10.4 1.3 %copy-done = bf16[768,768]{1,0:T(8,128)(2,1)S(1)} copy-done((bf16[768,768]{1,0:T(8,128)(2,1)S(1)}, bf16[768,768]{1,0:T(8,128)(2,1)}, u32[]{:S(2)}) %copy-start) | copy-done | bytes 1179672
  11.6 0.0 copy-start.1
  11.6 1.3 %copy-done.1 = bf16[768,768]{1,0:T(8,128)(2,1)S(1)} copy-done((bf16[768,768]{1,0:T(8,128)(2,1)S(1)}, bf16[768,768]{1,0:T(8,128)(2,1)}, u32[]{:S(2)}) %copy-start.1) | copy-done | bytes 1179672
  12.9 1.9 %shard_map.96 = bf16[128,768]{1,0:T(8,128)(2,1)S(1)} custom-call(s32[2]{0:T(128)S(1)} %pad_add_fusion.place_ref, bf16[192,256]{1,0:T(8,128)(2,1)S(1)} %get-tuple-element.5.p0, bf16[192,256]{1,0:T(8,128)(2,1)S(1)} %collective-permute-done.p1, bf16[192,256]{1,0:T(8,128)(2,1)S(1)} %collective-permute-done.1.p2, bf16[192,256]{1,0:T(8,128)(2,1)S(1)} %collective-permute-done.2.p3, ...), custom_call_target="tpu_custom_call" | custom-call | flops 603979776 | bytes 4718592 | tf_op jit(solution)/shard_map/pallas_call | solution.py:20
  14.9 1.5 %collective-permute-start.5 = (bf16[128,768]{1,0:T(8,128)(2,1)S(1)}, bf16[128,768]{1,0:T(8,128)(2,1)S(1)}, u32[]{:S(2)}, u32[]{:S(2)}) collective-permute-start(bf16[128,768]{1,0:T(8,128)(2,1)S(1)} %shard_map.96), channel_id=1, source_target_pairs={{0,2},{1,3},{2,0},{3,1},{4,6},{5,7},{6,4},{7,5},{8,10},{9,11},{10,... | collective-permute-start | bytes 589832 | tf_op jit(solution)/shard_map/ppermute | solution.py:185
  16.3 0.0 copy-done.6
  16.4 0.0 copy-start.3
  16.4 0.0 copy-start.4
  16.4 0.0 copy-start.5
  16.4 1.9 %shard_map.95.kept_ref = f32[128,768]{1,0:T(8,128)S(1)} custom-call(s32[2]{0:T(128)S(1)} %pad_add_fusion.place_ref, bf16[192,256]{1,0:T(8,128)(2,1)S(1)} %get-tuple-element.5.p0, bf16[192,256]{1,0:T(8,128)(2,1)S(1)} %collective-permute-done.p1, bf16[192,256]{1,0:T(8,128)(2,1)S(1)} %collective-permute-done.1.p2, ...), custom_call_target="tpu_custom_call" | custom-call | flops 603979776 | bytes 4718592 | tf_op jit(solution)/shard_map/pallas_call | solution.py:20
  18.3 3.8 %collective-permute-done.5.came_ref = bf16[128,768]{1,0:T(8,128)(2,1)S(1)} collective-permute-done((bf16[128,768]{1,0:T(8,128)(2,1)S(1)}, bf16[128,768]{1,0:T(8,128)(2,1)S(1)}, u32[]{:S(2)}, u32[]{:S(2)}) %collective-permute-start.5) | collective-permute-done | bytes 196640 | tf_op jit(solution)/shard_map/ppermute | solution.py:185
  22.2 0.0 copy-done.3
  22.2 0.0 copy-done.4
  22.2 0.0 copy-done.5
  22.2 0.9 %shard_map.97 = bf16[8,896]{1,0:T(8,128)(2,1)S(1)} custom-call(s32[2]{0:T(128)S(1)} %pad_add_fusion.place_ref, s32[32]{0:T(128)S(1)} %copy-done.3, s32[32]{0:T(128)S(1)} %copy-done.4, s32[8]{0:T(128)S(1)} %copy-done.5, f32[128,768]{1,0:T(8,128)S(1)} %shard_map.95.kept_ref, bf16[128,768]{1,0:T(8,128)(2,1)S(1)} %collective-permute-done.5.came_ref, ...), custom_call_target="tpu_custom_call" | custom-call | tf_op jit(solution)/shard_map/pallas_call | solution.py:20
  23.1 16.2 %all_to_all.5 = bf16[16,8,896]{2,1,0:T(8,128)(2,1)S(1)} all-to-all(bf16[16,8,896]{2,1,0:T(8,128)(2,1)S(1)} %broadcast_in_dim.10), channel_id=1, replica_groups={{0,2,4,6,8,10,12,14,16,18,20,22,24,26,28,30},{1,3,5,7,9,11,13,15,17,19,..., dimensions={0} | all-to-all | bytes 458752 | tf_op jit(solution)/shard_map/all_to_all | solution.py:225
  39.3 0.0 collective-permute-start.6
  39.3 1.5 %collective-permute-done.6.far_ref = bf16[128,896]{1,0:T(8,128)(2,1)S(1)} collective-permute-done((bf16[128,896]{1,0:T(8,128)(2,1)S(1)}, bf16[128,896]{1,0:T(8,128)(2,1)S(1)}, u32[]{:S(2)}, u32[]{:S(2)}) %collective-permute-start.6) | collective-permute-done | bytes 229408 | tf_op jit(solution)/shard_map/ppermute | solution.py:185
  40.8 1.8 %shard_map.98 = (bf16[32,768]{1,0:T(8,128)(2,1)}, f32[8,192]{1,0:T(8,128)}, f32[2,192]{1,0:T(2,128)}) custom-call(s32[2]{0:T(128)S(1)} %pad_add_fusion.place_ref, bf16[128,896]{1,0:T(8,128)(2,1)S(1)} %bitcast.5, bf16[128,896]{1,0:T(8,128)(2,1)S(1)} %collective-permute-done.6.far_ref), custom_call_target="tpu_custom_call" | custom-call | tf_op jit(solution)/shard_map/pallas_call | solution.py:20
  (2 shorter events, 0.0 us)
Async XLA Ops:
  0.6 9.7 %collective-permute-start.3 = (bf16[768,768]{1,0:T(8,128)(2,1)}, bf16[768,768]{1,0:T(8,128)(2,1)S(1)}, u32[]{:S(2)}, u32[]{:S(2)}) collective-permute-start(bf16[768,768]{1,0:T(8,128)(2,1)} %u0.3), channel_id=1, source_target_pairs={{0,1},{1,0},{2,3},{3,2},{4,5},{5,4},{6,7},{7,6},{8,9},{9,8},{10,11... | collective-permute-start | bytes 3538952 | tf_op jit(solution)/shard_map/ppermute | solution.py:185
  1.1 9.2 %collective-permute-start.4 = (bf16[768,768]{1,0:T(8,128)(2,1)}, bf16[768,768]{1,0:T(8,128)(2,1)S(1)}, u32[]{:S(2)}, u32[]{:S(2)}) collective-permute-start(bf16[768,768]{1,0:T(8,128)(2,1)} %d0.3), channel_id=1, source_target_pairs={{0,1},{1,0},{2,3},{3,2},{4,5},{5,4},{6,7},{7,6},{8,9},{9,8},{10,11... | collective-permute-start | bytes 3538952 | tf_op jit(solution)/shard_map/ppermute | solution.py:185
  1.3 0.9 %copy-start.2 = (bf16[512,192]{0,1:T(8,128)(2,1)S(1)}, bf16[512,192]{0,1:T(8,128)(2,1)}, u32[]{:S(2)}) copy-start(bf16[512,192]{0,1:T(8,128)(2,1)} %param.7) | copy-start | bytes 589828
  2.2 14.1 %copy-start.6 = (f32[768]{0:T(1024)S(1)}, f32[768]{0:T(1024)}, u32[]{:S(2)}) copy-start(f32[768]{0:T(1024)} %param.10) | copy-start | bytes 9220
  2.8 6.2 %collective-permute-start.1 = (bf16[192,256]{1,0:T(8,128)(2,1)S(1)}, bf16[192,256]{1,0:T(8,128)(2,1)S(1)}, u32[]{:S(2)}, u32[]{:S(2)}) collective-permute-start(bf16[192,256]{1,0:T(8,128)(2,1)S(1)} %get-tuple-element.5.p0), channel_id=1, source_target_pairs={{0,2},{1,3},{2,0},{3,1},{4,6},{5,7},{6,4},{7,5},{8,10},{9,11},{10,... | collective-permute-start | bytes 294920 | tf_op jit(solution)/shard_map/ppermute | solution.py:185
  5.8 3.2 %collective-permute-start = (bf16[192,256]{1,0:T(8,128)(2,1)S(1)}, bf16[192,256]{1,0:T(8,128)(2,1)S(1)}, u32[]{:S(2)}, u32[]{:S(2)}) collective-permute-start(bf16[192,256]{1,0:T(8,128)(2,1)S(1)} %get-tuple-element.6), channel_id=1, source_target_pairs={{0,1},{1,0},{2,3},{3,2},{4,5},{5,4},{6,7},{7,6},{8,9},{9,8},{10,11... | collective-permute-start | bytes 294920 | tf_op jit(solution)/shard_map/ppermute | solution.py:185
  5.8 4.5 %collective-permute-start.2 = (bf16[192,256]{1,0:T(8,128)(2,1)S(1)}, bf16[192,256]{1,0:T(8,128)(2,1)S(1)}, u32[]{:S(2)}, u32[]{:S(2)}) collective-permute-start(bf16[192,256]{1,0:T(8,128)(2,1)S(1)} %get-tuple-element.6), channel_id=1, source_target_pairs={{0,3},{1,2},{2,1},{3,0},{4,7},{5,6},{6,5},{7,4},{8,11},{9,10},{10,... | collective-permute-start | bytes 294920 | tf_op jit(solution)/shard_map/ppermute | solution.py:185
  10.4 1.3 %copy-start = (bf16[768,768]{1,0:T(8,128)(2,1)S(1)}, bf16[768,768]{1,0:T(8,128)(2,1)}, u32[]{:S(2)}) copy-start(bf16[768,768]{1,0:T(8,128)(2,1)} %u0.3) | copy-start | bytes 3538948
  11.6 1.3 %copy-start.1 = (bf16[768,768]{1,0:T(8,128)(2,1)S(1)}, bf16[768,768]{1,0:T(8,128)(2,1)}, u32[]{:S(2)}) copy-start(bf16[768,768]{1,0:T(8,128)(2,1)} %d0.3) | copy-start | bytes 3538948
  14.9 7.3 %collective-permute-start.5 = (bf16[128,768]{1,0:T(8,128)(2,1)S(1)}, bf16[128,768]{1,0:T(8,128)(2,1)S(1)}, u32[]{:S(2)}, u32[]{:S(2)}) collective-permute-start(bf16[128,768]{1,0:T(8,128)(2,1)S(1)} %shard_map.96), channel_id=1, source_target_pairs={{0,2},{1,3},{2,0},{3,1},{4,6},{5,7},{6,4},{7,5},{8,10},{9,11},{10,... | collective-permute-start | bytes 589832 | tf_op jit(solution)/shard_map/ppermute | solution.py:185
  16.4 5.8 %copy-start.3 = (s32[32]{0:T(128)S(1)}, s32[32]{0:T(128)}, u32[]{:S(2)}) copy-start(s32[32]{0:T(128)} %length_ref.1) | copy-start | bytes 388
  16.4 5.8 %copy-start.4 = (s32[32]{0:T(128)S(1)}, s32[32]{0:T(128)}, u32[]{:S(2)}) copy-start(s32[32]{0:T(128)} %leaf_ref.1) | copy-start | bytes 388
  16.4 5.8 %copy-start.5 = (s32[8]{0:T(128)S(1)}, s32[8]{0:T(128)}, u32[]{:S(2)}) copy-start(s32[8]{0:T(128)} %parent_ref.1) | copy-start | bytes 100
  39.3 1.5 %collective-permute-start.6 = (bf16[128,896]{1,0:T(8,128)(2,1)S(1)}, bf16[128,896]{1,0:T(8,128)(2,1)S(1)}, u32[]{:S(2)}, u32[]{:S(2)}) collective-permute-start(bf16[128,896]{1,0:T(8,128)(2,1)S(1)} %bitcast.4), channel_id=1, source_target_pairs={{0,1},{1,0},{2,3},{3,2},{4,5},{5,4},{6,7},{7,6},{8,9},{9,8},{10,11... | collective-permute-start | bytes 688136 | tf_op jit(solution)/shard_map/ppermute | solution.py:185

commit v2 on v1

v2 whole, which is shorter than its diff:
```python
import functools

import jax
import jax.numpy as jnp
from jax import lax
from jax.experimental import pallas as pl
from jax.experimental.pallas import tpu as pltpu
from jax.sharding import PartitionSpec as P

PAR_DEV = 2
BASE = 128
LANES = 128
UNIT_TILE = 256
VMEM = pl.BlockSpec(memory_space=pltpu.VMEM)
HBM = pl.BlockSpec(memory_space=pl.ANY)
VMEM_LIMIT = 40 * 1024 * 1024


def call(kernel, out_shape, operands, out_spec=VMEM, scratch=(), flops=0, moved=0):
    return pl.pallas_call(
        kernel,
        out_shape=out_shape,
        in_specs=[VMEM] * len(operands),
        out_specs=jax.tree.map(lambda _: out_spec, out_shape),
        scratch_shapes=list(scratch),
        compiler_params=pltpu.CompilerParams(vmem_limit_bytes=VMEM_LIMIT),
        cost_estimate=pl.CostEstimate(flops=flops, bytes_accessed=moved, transcendentals=0),
    )(*operands)


def split_kernel(hidden_ref, mine_ref, other_ref):
    core = lax.axis_index("heads") % 2
    quarter = mine_ref.shape[1] // 2
    for pair in range(2):
        to = slice(pair * quarter, (pair + 1) * quarter)
        mine = pl.multiple_of((2 * pair + core) * quarter, quarter)
        other = pl.multiple_of((2 * pair + 1 - core) * quarter, quarter)
        mine_ref[:, to] = hidden_ref[:, pl.ds(mine, quarter)]
        other_ref[:, to] = hidden_ref[:, pl.ds(other, quarter)]


def stage_kernel(up_ref, down_ref, out_ref):
    out_ref[...] = up_ref[:16, :LANES] + down_ref[:16, :LANES]


def feed_forward(pieces, weights, gathered, own_quarter):
    head = lax.axis_index("heads")
    share, both = pieces[0].shape
    quarter = both // 2
    pair = head // 2 if own_quarter else 1 - head // 2
    columns = pl.ds(pl.multiple_of(pair * quarter, quarter), quarter)
    for flip, piece in enumerate(pieces):
        rows = pl.ds(pl.multiple_of((head ^ flip) * share, 64), share)
        gathered[rows, :] = piece[:, columns]
    tokens = gathered[...].T
    total = None
    for up_ref, down_ref in weights:
        units = up_ref.shape[1]
        tile = min(UNIT_TILE, units)
        part = None
        for start in range(0, units, tile):
            upward = jnp.dot(
                tokens, up_ref[:, start : start + tile], preferred_element_type=jnp.float32
            )
            activ = (0.5 * upward * (1.0 + lax.erf(upward * 0.7071067811865476))).astype(
                jnp.bfloat16
            )
            term = jnp.dot(
                activ, down_ref[start : start + tile, :], preferred_element_type=jnp.float32
            )
            part = term if part is None else part + term
        part = part.astype(jnp.bfloat16).astype(jnp.float32)
        total = part if total is None else total + part
    return tokens, total


def give_kernel(p0, p1, p2, p3, u0, d0, u1, d1, staged, out_ref, gathered):
    _, total = feed_forward((p0, p1, p2, p3), ((u0, d0), (u1, d1)), gathered, False)
    out_ref[...] = total.astype(jnp.bfloat16)


def own_column(values_ref, rows, repeat, first):
    shape = (rows * repeat, values_ref.shape[1])
    wanted = first + lax.broadcasted_iota(jnp.int32, shape, 0) // repeat
    lane = lax.broadcasted_iota(jnp.int32, shape, 1)
    values = values_ref[...].astype(jnp.float32)
    return jnp.sum(jnp.where(lane == wanted, values, 0.0), axis=1, keepdims=True)


def keep_kernel(
    p0, p1, p2, p3, u0, d0, u1, d1, length_ref, leaf_ref, parent_ref,
    out_ref, weight_ref, digits_ref, gathered,
):
    head = lax.axis_index("heads")
    rows, lanes = digits_ref.shape
    seq = out_ref.shape[0] // rows
    length = own_column(length_ref, rows, seq, head * rows)
    position = lax.broadcasted_iota(jnp.int32, (rows * seq, 1), 0) % seq
    weight = jnp.where(position.astype(jnp.float32) < length, 1.0 / length, 0.0)
    weight_ref[...] = jnp.broadcast_to(weight, weight_ref.shape)
    lane = lax.broadcasted_iota(jnp.int32, (rows, lanes), 1)
    digits = jnp.zeros((rows, lanes), jnp.int32)
    for at, (ref, first) in enumerate(((leaf_ref, head * rows), (parent_ref, 0))):
        values = own_column(ref, rows, 1, first).astype(jnp.int32)
        digits = jnp.where(lane == 2 * at, values % BASE, digits)
        digits = jnp.where(lane == 2 * at + 1, values // BASE, digits)
    digits_ref[...] = digits.astype(jnp.float32)
    tokens, total = feed_forward((p0, p1, p2, p3), ((u0, d0), (u1, d1)), gathered, True)
    out_ref[...] = tokens.astype(jnp.float32) + total


def embed_kernel(kept_ref, came_ref, weight_ref, digits_ref, gain_ref, out_ref):
    rows, width = digits_ref.shape[0], kept_ref.shape[1]
    mixed = (kept_ref[...] + came_ref[...].astype(jnp.float32)).astype(jnp.bfloat16)
    as_float = mixed.astype(jnp.float32)
    centred = as_float - jnp.mean(as_float, axis=1, keepdims=True)
    variance = jnp.mean(centred * centred, axis=1, keepdims=True)
    weighted = centred * (lax.rsqrt(variance + 1e-05) * weight_ref[:, :1])
    pooled = jnp.sum(weighted.reshape(rows, -1, width), axis=1) * gain_ref[...]
    scale = lax.rsqrt(jnp.mean(pooled * pooled, axis=1, keepdims=True) + 1e-05)
    both = jnp.concatenate([pooled * scale, digits_ref[...]], axis=1)
    out_ref[...] = both.astype(jnp.bfloat16)


def pick_share(values, head, heads):
    share = values.shape[1] // heads
    result = values[:, :share]
    for other in range(1, heads):
        result = jnp.where(head == other, values[:, other * share : (other + 1) * share], result)
    return result


def leaf_kernel(
    heads, near_ref, far_ref, embed_out, centers_out, parents_out,
    embed_ref, centers_ref, parents_ref, scratch, sems,
):
    head, index = lax.axis_index("heads"), lax.axis_index("labels")
    core = head % 2
    width = embed_ref.shape[1]
    rows = embed_ref.shape[0] // heads
    leaf_count = centers_ref.shape[0]
    owners = near_ref.shape[0] // (2 * rows)
    leaves = owners * leaf_count
    here = pl.ds(pl.multiple_of(index * 2 * rows, 2 * rows), 2 * rows)
    near = near_ref[here, :width].astype(jnp.float32)
    far = far_ref[here, :width].astype(jnp.float32)
    even, odd = jnp.where(core == 0, near, far), jnp.where(core == 0, far, near)
    embed_ref[...] = jnp.concatenate(
        [part[i * rows : (i + 1) * rows] for i in range(2) for part in (even, odd)], axis=0
    ).astype(jnp.bfloat16)
    embed_copy = pltpu.make_async_copy(embed_ref, embed_out, sems.at[0])
    embed_copy.start()
    wanted = lax.broadcasted_iota(jnp.int32, (leaves, near_ref.shape[0]), 0)
    leaf_sum = jnp.zeros((leaves, width), jnp.float32)
    for ref in (near_ref, far_ref):
        turned = ref[:, width:].astype(jnp.float32).T
        leaf = (turned[0:1] + BASE * turned[1:2]).astype(jnp.int32)
        picker = jnp.where(wanted == leaf, 1.0, 0.0).astype(jnp.bfloat16)
        leaf_sum = leaf_sum + jnp.dot(
            picker, ref[:, :width], preferred_element_type=jnp.float32
        )
    squares = jnp.mean(leaf_sum * leaf_sum, axis=1, keepdims=True)
    centers = leaf_sum * lax.rsqrt(squares + 1e-05)
    scratch[...] = centers
    own = scratch[pl.ds(pl.multiple_of(index * leaf_count, leaf_count), leaf_count), :]
    centers_ref[...] = pick_share(own, head, heads)
    centers_copy = pltpu.make_async_copy(centers_ref, centers_out, sems.at[1])
    centers_copy.start()
    digits = near_ref[:, width:].astype(jnp.float32)
    digits = digits.reshape(owners, 2, rows, LANES)[:, 0, :leaf_count].reshape(leaves, LANES)
    parent = (digits[:, 2:3] + BASE * digits[:, 3:4]).astype(jnp.int32)
    sums = [
        jnp.sum(jnp.where(parent == index * PAR_DEV + p, centers, 0.0), axis=0, keepdims=True)
        for p in range(PAR_DEV)
    ]
    parents_ref[...] = pick_share(jnp.concatenate(sums, axis=0), head, heads)
    parents_copy = pltpu.make_async_copy(parents_ref, parents_out, sems.at[2])
    parents_copy.start()
    embed_copy.wait()
    centers_copy.wait()
    parents_copy.wait()


def local(owners, heads, hidden_in, w_up, w_down, norm_gain, title_length, label_leaf, leaf_parent):
    token_rows, share = hidden_in.shape
    width = w_down.shape[1]
    units = w_up.shape[1]
    labels_here = label_leaf.shape[0]
    leaf_count = leaf_parent.shape[0]
    rows = labels_here // heads
    quarter = token_rows // heads

    def swap(values, flip):
        return lax.ppermute(values, "heads", [(i, i ^ flip) for i in range(heads)])

    def array(*shape, dtype=jnp.float32):
        return jax.ShapeDtypeStruct(shape, dtype)

    up_far, down_far = swap(w_up, 1), swap(w_down, 1)
    half = array(share, 2 * quarter, dtype=jnp.bfloat16)
    mine, other = call(split_kernel, (half, half), (hidden_in.T,), flops=0)
    pieces = (mine, swap(other, 1), swap(mine, 2), swap(other, 3))
    staged = call(stage_kernel, array(16, LANES, dtype=jnp.bfloat16), (w_up, w_down))
    operands = (*pieces, w_up, w_down, up_far, down_far)
    cost = dict(
        scratch=[pltpu.VMEM((width, quarter), jnp.bfloat16)],
        flops=8 * quarter * width * units,
        moved=8 * width * units,
    )
    given = call(
        give_kernel, array(quarter, width, dtype=jnp.bfloat16), (*operands, staged), **cost
    )
    came = swap(given, 2)
    kept, weight, digits = call(
        keep_kernel,
        (array(quarter, width), array(quarter, LANES), array(rows, LANES)),
        (*operands, title_length[None, :], label_leaf[None, :], leaf_parent[None, :]),
        **cost,
    )
    message = call(
        embed_kernel,
        array(rows, width + LANES, dtype=jnp.bfloat16),
        (kept, came, weight, digits, norm_gain[None, :]),
    )
    groups = [
        [owner * heads + head for owner in range(owners) for head in range(core, heads, 2)]
        for core in range(2)
    ]
    members = owners * heads // 2
    near = lax.all_to_all(
        jnp.broadcast_to(message[None], (members,) + message.shape),
        ("labels", "heads"),
        split_axis=0,
        concat_axis=0,
        tiled=True,
        axis_index_groups=groups,
    ).reshape(members * rows, width + LANES)
    far = swap(near, 1)
    outputs = (
        array(labels_here, width, dtype=jnp.bfloat16),
        array(leaf_count, share),
        array(PAR_DEV, share),
    )
    return call(
        functools.partial(leaf_kernel, heads),
        outputs,
        (near, far),
        out_spec=HBM,
        scratch=[pltpu.VMEM(out.shape, out.dtype) for out in outputs]
        + [pltpu.VMEM((owners * leaf_count, width), jnp.float32), pltpu.SemaphoreType.DMA((3,))],
    )


def solution(mesh):
    in_specs = (
        P("labels", "heads"),
        P(None, "heads"),
        P("heads", None),
        P(),
        P("labels"),
        P("labels"),
        P("labels"),
    )
    out_specs = (P("labels", None), P("labels", "heads"), P("labels", "heads"))
    body = functools.partial(local, mesh.shape["labels"], mesh.shape["heads"])
    return jax.shard_map(body, mesh=mesh, in_specs=in_specs, out_specs=out_specs, check_vma=False)
```

time: 42.9 us -> 37.5 us (0.87)
  Pallas kernels: 7.2 us -> 4.49 us
  waiting for transfers between devices: 9.65 us -> 7.4 us
  blocking collectives: 16.2 us -> 15.3 us
  starting transfers between devices: 5.29 us -> 5.87 us
    pallas_call x5 -> x6, Pallas kernels: 7.2 us -> 4.49 us  [call(): pl.pallas_call(kernel, out_shape=out_shape, in_specs=[VMEM] * len(operand...]
    ppermute x7, waiting for transfers between devices: 9.65 us -> 7.4 us  [swap(): return lax.ppermute(values, 'heads', [(i, i ^ flip) for i in range(heads)])]
    all_to_all x1, blocking collectives: 16.2 us -> 15.3 us  [local(): lax.all_to_all(jnp.broadcast_to(message[None], (members,) + message.shape...]
    ppermute x7, starting transfers between devices: 5.29 us -> 5.87 us  [swap(): return lax.ppermute(values, 'heads', [(i, i ^ flip) for i in range(heads)])]
    unnamed x14 -> x16, local copies, waits for them, and re-layouts: 3.49 us -> 3.49 us
  transfers between devices with their start and end apart: 7 -> 7, of which waited for: 4 -> 4; matrix products, arithmetic and copies ran while one was open for 0% -> 0% of each run, Pallas kernels for 6% -> 4%
where the time goes in v2:
time: 37.5 us; the launch traced here: 37.3 us
  blocking collectives  15.3 us (41%)
  waiting for transfers between devices  7.4 us (20%)
  starting transfers between devices  5.87 us (16%)
  Pallas kernels  4.49 us (12%)
  local copies, waits for them, and re-layouts  3.52 us (9%)
  between operations  0.71 us (2%)
    all_to_all x1, blocking collectives, local(): lax.all_to_all(jnp.broadcast_to(message[None], (members,) + message.shape...  15.3 us
    ppermute x7, waiting for transfers between devices, swap(): return lax.ppermute(values, 'heads', [(i, i ^ flip) for i in range(heads)])  7.4 us
    ppermute x7, starting transfers between devices, swap(): return lax.ppermute(values, 'heads', [(i, i ^ flip) for i in range(heads)])  5.87 us
    pallas_call x6, Pallas kernels, call(): pl.pallas_call(kernel, out_shape=out_shape, in_specs=[VMEM] * len(operand...  4.49 us
    unnamed x16, local copies, waits for them, and re-layouts  3.49 us
  transfers between devices with their start and end apart: 7, of which 4 were waited for; matrix products, arithmetic and copies ran while one was open for 0% of the time, Pallas kernels for 4%

profile of v2, /device:TPU:0, one launch (start us, length us, event | category | flops | bytes accessed | tf_op | source)
XLA Modules:
  0.0 37.3 jit_solution(15705821005532114198)
XLA Ops:
  0.6 0.5 %collective-permute-start.3 = (bf16[768,768]{1,0:T(8,128)(2,1)}, bf16[768,768]{1,0:T(8,128)(2,1)S(1)}, u32[]{:S(2)}, u32[]{:S(2)}) collective-permute-start(bf16[768,768]{1,0:T(8,128)(2,1)} %u0.3), channel_id=1, source_target_pairs={{0,1},{1,0},{2,3},{3,2},{4,5},{5,4},{6,7},{7,6},{8,9},{9,8},{10,11... | collective-permute-start | bytes 3538952 | tf_op jit(solution)/shard_map/ppermute | solution.py:194
  1.1 0.1 collective-permute-start.4
  1.2 0.0 copy-start.3
  1.2 0.9 %copy-done.3 = bf16[512,192]{0,1:T(8,128)(2,1)S(1)} copy-done((bf16[512,192]{0,1:T(8,128)(2,1)S(1)}, bf16[512,192]{0,1:T(8,128)(2,1)}, u32[]{:S(2)}) %copy-start.3) | copy-done | bytes 196632
  2.2 2.7 %collective-permute-start.2 = (bf16[192,256]{1,0:T(8,128)(2,1)S(1)}, bf16[192,256]{1,0:T(8,128)(2,1)S(1)}, u32[]{:S(2)}, u32[]{:S(2)}) collective-permute-start(bf16[192,256]{1,0:T(8,128)(2,1)S(1)} %get-tuple-element.9), channel_id=1, source_target_pairs={{0,3},{1,2},{2,1},{3,0},{4,7},{5,6},{6,5},{7,4},{8,11},{9,10},{10,... | collective-permute-start | bytes 294920 | tf_op jit(solution)/shard_map/ppermute | solution.py:194
  4.9 0.4 %collective-permute-start = (bf16[192,256]{1,0:T(8,128)(2,1)S(1)}, bf16[192,256]{1,0:T(8,128)(2,1)S(1)}, u32[]{:S(2)}, u32[]{:S(2)}) collective-permute-start(bf16[192,256]{1,0:T(8,128)(2,1)S(1)} %get-tuple-element.9), channel_id=1, source_target_pairs={{0,1},{1,0},{2,3},{3,2},{4,5},{5,4},{6,7},{7,6},{8,9},{9,8},{10,11... | collective-permute-start | bytes 294920 | tf_op jit(solution)/shard_map/ppermute | solution.py:194
  5.3 0.0 collective-permute-start.1
  5.3 0.0 copy-start
  5.3 1.3 %copy-done = bf16[768,768]{1,0:T(8,128)(2,1)S(1)} copy-done((bf16[768,768]{1,0:T(8,128)(2,1)S(1)}, bf16[768,768]{1,0:T(8,128)(2,1)}, u32[]{:S(2)}) %copy-start) | copy-done | bytes 1179672
  6.6 0.0 copy-start.2
  6.6 1.3 %copy-done.2 = bf16[768,768]{1,0:T(8,128)(2,1)S(1)} copy-done((bf16[768,768]{1,0:T(8,128)(2,1)S(1)}, bf16[768,768]{1,0:T(8,128)(2,1)}, u32[]{:S(2)}) %copy-start.2) | copy-done | bytes 1179672
  7.9 0.0 copy-start.1
  7.9 0.0 copy-start.7
  7.9 0.0 copy-start.4
  7.9 0.0 copy-start.5
  7.9 0.0 copy-start.6
  7.9 0.1 collective-permute-done.2.p3
  8.0 0.0 collective-permute-done.p1
  8.1 2.3 %collective-permute-done.1.p2 = bf16[192,256]{1,0:T(8,128)(2,1)S(1)} collective-permute-done((bf16[192,256]{1,0:T(8,128)(2,1)S(1)}, bf16[192,256]{1,0:T(8,128)(2,1)S(1)}, u32[]{:S(2)}, u32[]{:S(2)}) %collective-permute-start.1) | collective-permute-done | bytes 98336 | tf_op jit(solution)/shard_map/ppermute | solution.py:194
  10.3 0.0 collective-permute-done.3.u1
  10.3 0.0 collective-permute-done.4.d1
  10.3 0.0 copy-done.1
  10.3 1.4 %shard_map.97 = bf16[128,768]{1,0:T(8,128)(2,1)S(1)} custom-call(bf16[192,256]{1,0:T(8,128)(2,1)S(1)} %get-tuple-element.8.p0, bf16[192,256]{1,0:T(8,128)(2,1)S(1)} %collective-permute-done.p1, bf16[192,256]{1,0:T(8,128)(2,1)S(1)} %collective-permute-done.1.p2, bf16[192,256]{1,0:T(8,128)(2,1)S(1)} %collective-permute-done.2.p3, ...), custom_call_target="tpu_custom_call" | custom-call | flops 603979776 | bytes 4718592 | tf_op jit(solution)/shard_map/pallas_call | solution.py:20
  11.7 2.1 %collective-permute-start.5 = (bf16[128,768]{1,0:T(8,128)(2,1)S(1)}, bf16[128,768]{1,0:T(8,128)(2,1)S(1)}, u32[]{:S(2)}, u32[]{:S(2)}) collective-permute-start(bf16[128,768]{1,0:T(8,128)(2,1)S(1)} %shard_map.97), channel_id=1, source_target_pairs={{0,2},{1,3},{2,0},{3,1},{4,6},{5,7},{6,4},{7,5},{8,10},{9,11},{10,... | collective-permute-start | bytes 589832 | tf_op jit(solution)/shard_map/ppermute | solution.py:194
  13.8 0.0 copy-done.7
  13.8 0.0 copy-done.4
  13.9 0.0 copy-done.5
  13.9 0.0 copy-done.6
  13.9 1.4 %shard_map.95 = (f32[128,768]{1,0:T(8,128)S(1)}, f32[128,128]{1,0:T(8,128)S(1)}, f32[8,128]{1,0:T(8,128)S(1)}) custom-call(bf16[192,256]{1,0:T(8,128)(2,1)S(1)} %get-tuple-element.8.p0, bf16[192,256]{1,0:T(8,128)(2,1)S(1)} %collective-permute-done.p1, bf16[192,256]{1,0:T(8,128)(2,1)S(1)} %collective-permute-done.1.p2, ...), custom_call_target="tpu_custom_call" | custom-call | flops 603979776 | bytes 4718592 | tf_op jit(solution)/shard_map/pallas_call | solution.py:20
  15.3 3.5 %collective-permute-done.5.came_ref = bf16[128,768]{1,0:T(8,128)(2,1)S(1)} collective-permute-done((bf16[128,768]{1,0:T(8,128)(2,1)S(1)}, bf16[128,768]{1,0:T(8,128)(2,1)S(1)}, u32[]{:S(2)}, u32[]{:S(2)}) %collective-permute-start.5) | collective-permute-done | bytes 196640 | tf_op jit(solution)/shard_map/ppermute | solution.py:194
  18.8 0.4 %shard_map.98 = bf16[8,896]{1,0:T(8,128)(2,1)S(1)} custom-call(f32[128,768]{1,0:T(8,128)S(1)} %get-tuple-element.10.kept_ref, bf16[128,768]{1,0:T(8,128)(2,1)S(1)} %collective-permute-done.5.came_ref, f32[128,128]{1,0:T(8,128)S(1)} %get-tuple-element.11.weight_ref, f32[8,128]{1,0:T(8,128)S(1)} %get-tuple-element.12.digits_ref, ...), custom_call_target="tpu_custom_call" | custom-call | tf_op jit(solution)/shard_map/pallas_call | solution.py:20
  19.2 15.3 %all_to_all.5 = bf16[16,8,896]{2,1,0:T(8,128)(2,1)S(1)} all-to-all(bf16[16,8,896]{2,1,0:T(8,128)(2,1)S(1)} %broadcast_in_dim.22), channel_id=1, replica_groups={{0,2,4,6,8,10,12,14,16,18,20,22,24,26,28,30},{1,3,5,7,9,11,13,15,17,19,..., dimensions={0} | all-to-all | bytes 458752 | tf_op jit(solution)/shard_map/all_to_all | solution.py:230
  34.5 0.0 collective-permute-start.6
  34.5 1.5 %collective-permute-done.6.far_ref = bf16[128,896]{1,0:T(8,128)(2,1)S(1)} collective-permute-done((bf16[128,896]{1,0:T(8,128)(2,1)S(1)}, bf16[128,896]{1,0:T(8,128)(2,1)S(1)}, u32[]{:S(2)}, u32[]{:S(2)}) %collective-permute-start.6) | collective-permute-done | bytes 229408 | tf_op jit(solution)/shard_map/ppermute | solution.py:194
  36.0 1.3 %shard_map.99 = (bf16[32,768]{1,0:T(8,128)(2,1)}, f32[8,192]{1,0:T(8,128)}, f32[2,192]{1,0:T(2,128)}) custom-call(bf16[128,896]{1,0:T(8,128)(2,1)S(1)} %bitcast.6, bf16[128,896]{1,0:T(8,128)(2,1)S(1)} %collective-permute-done.6.far_ref), custom_call_target="tpu_custom_call" | custom-call | tf_op jit(solution)/shard_map/pallas_call | solution.py:20
  (4 shorter events, 0.1 us)
Async XLA Ops:
  0.6 9.7 %collective-permute-start.3 = (bf16[768,768]{1,0:T(8,128)(2,1)}, bf16[768,768]{1,0:T(8,128)(2,1)S(1)}, u32[]{:S(2)}, u32[]{:S(2)}) collective-permute-start(bf16[768,768]{1,0:T(8,128)(2,1)} %u0.3), channel_id=1, source_target_pairs={{0,1},{1,0},{2,3},{3,2},{4,5},{5,4},{6,7},{7,6},{8,9},{9,8},{10,11... | collective-permute-start | bytes 3538952 | tf_op jit(solution)/shard_map/ppermute | solution.py:194
  1.1 9.2 %collective-permute-start.4 = (bf16[768,768]{1,0:T(8,128)(2,1)}, bf16[768,768]{1,0:T(8,128)(2,1)S(1)}, u32[]{:S(2)}, u32[]{:S(2)}) collective-permute-start(bf16[768,768]{1,0:T(8,128)(2,1)} %d0.3), channel_id=1, source_target_pairs={{0,1},{1,0},{2,3},{3,2},{4,5},{5,4},{6,7},{7,6},{8,9},{9,8},{10,11... | collective-permute-start | bytes 3538952 | tf_op jit(solution)/shard_map/ppermute | solution.py:194
  1.2 0.9 %copy-start.3 = (bf16[512,192]{0,1:T(8,128)(2,1)S(1)}, bf16[512,192]{0,1:T(8,128)(2,1)}, u32[]{:S(2)}) copy-start(bf16[512,192]{0,1:T(8,128)(2,1)} %param.7) | copy-start | bytes 589828
  2.2 5.9 %collective-permute-start.2 = (bf16[192,256]{1,0:T(8,128)(2,1)S(1)}, bf16[192,256]{1,0:T(8,128)(2,1)S(1)}, u32[]{:S(2)}, u32[]{:S(2)}) collective-permute-start(bf16[192,256]{1,0:T(8,128)(2,1)S(1)} %get-tuple-element.9), channel_id=1, source_target_pairs={{0,3},{1,2},{2,1},{3,0},{4,7},{5,6},{6,5},{7,4},{8,11},{9,10},{10,... | collective-permute-start | bytes 294920 | tf_op jit(solution)/shard_map/ppermute | solution.py:194
  4.9 3.2 %collective-permute-start = (bf16[192,256]{1,0:T(8,128)(2,1)S(1)}, bf16[192,256]{1,0:T(8,128)(2,1)S(1)}, u32[]{:S(2)}, u32[]{:S(2)}) collective-permute-start(bf16[192,256]{1,0:T(8,128)(2,1)S(1)} %get-tuple-element.9), channel_id=1, source_target_pairs={{0,1},{1,0},{2,3},{3,2},{4,5},{5,4},{6,7},{7,6},{8,9},{9,8},{10,11... | collective-permute-start | bytes 294920 | tf_op jit(solution)/shard_map/ppermute | solution.py:194
  5.3 5.0 %collective-permute-start.1 = (bf16[192,256]{1,0:T(8,128)(2,1)S(1)}, bf16[192,256]{1,0:T(8,128)(2,1)S(1)}, u32[]{:S(2)}, u32[]{:S(2)}) collective-permute-start(bf16[192,256]{1,0:T(8,128)(2,1)S(1)} %get-tuple-element.8.p0), channel_id=1, source_target_pairs={{0,2},{1,3},{2,0},{3,1},{4,6},{5,7},{6,4},{7,5},{8,10},{9,11},{10,... | collective-permute-start | bytes 294920 | tf_op jit(solution)/shard_map/ppermute | solution.py:194
  5.3 1.3 %copy-start = (bf16[768,768]{1,0:T(8,128)(2,1)S(1)}, bf16[768,768]{1,0:T(8,128)(2,1)}, u32[]{:S(2)}) copy-start(bf16[768,768]{1,0:T(8,128)(2,1)} %u0.3) | copy-start | bytes 3538948
  6.6 1.3 %copy-start.2 = (bf16[768,768]{1,0:T(8,128)(2,1)S(1)}, bf16[768,768]{1,0:T(8,128)(2,1)}, u32[]{:S(2)}) copy-start(bf16[768,768]{1,0:T(8,128)(2,1)} %d0.3) | copy-start | bytes 3538948
  7.9 2.5 %copy-start.1 = (bf16[768,768]{1,0:T(8,128)(2,1)S(1)}, bf16[768,768]{1,0:T(8,128)(2,1)}, u32[]{:S(2)}) copy-start(bf16[768,768]{1,0:T(8,128)(2,1)} %u0.3) | copy-start | bytes 3538948
  7.9 6.0 %copy-start.7 = (f32[768]{0:T(1024)S(1)}, f32[768]{0:T(1024)}, u32[]{:S(2)}) copy-start(f32[768]{0:T(1024)} %param.10) | copy-start | bytes 9220
  7.9 6.0 %copy-start.4 = (s32[32]{0:T(128)S(1)}, s32[32]{0:T(128)}, u32[]{:S(2)}) copy-start(s32[32]{0:T(128)} %param.11) | copy-start | bytes 388
  7.9 6.0 %copy-start.5 = (s32[32]{0:T(128)S(1)}, s32[32]{0:T(128)}, u32[]{:S(2)}) copy-start(s32[32]{0:T(128)} %param.12) | copy-start | bytes 388
  7.9 6.0 %copy-start.6 = (s32[8]{0:T(128)S(1)}, s32[8]{0:T(128)}, u32[]{:S(2)}) copy-start(s32[8]{0:T(128)} %param.13) | copy-start | bytes 100
  11.7 7.0 %collective-permute-start.5 = (bf16[128,768]{1,0:T(8,128)(2,1)S(1)}, bf16[128,768]{1,0:T(8,128)(2,1)S(1)}, u32[]{:S(2)}, u32[]{:S(2)}) collective-permute-start(bf16[128,768]{1,0:T(8,128)(2,1)S(1)} %shard_map.97), channel_id=1, source_target_pairs={{0,2},{1,3},{2,0},{3,1},{4,6},{5,7},{6,4},{7,5},{8,10},{9,11},{10,... | collective-permute-start | bytes 589832 | tf_op jit(solution)/shard_map/ppermute | solution.py:194
  34.5 1.5 %collective-permute-start.6 = (bf16[128,896]{1,0:T(8,128)(2,1)S(1)}, bf16[128,896]{1,0:T(8,128)(2,1)S(1)}, u32[]{:S(2)}, u32[]{:S(2)}) collective-permute-start(bf16[128,896]{1,0:T(8,128)(2,1)S(1)} %bitcast.5), channel_id=1, source_target_pairs={{0,1},{1,0},{2,3},{3,2},{4,5},{5,4},{6,7},{7,6},{8,9},{9,8},{10,11... | collective-permute-start | bytes 688136 | tf_op jit(solution)/shard_map/ppermute | solution.py:194

commit v3 on v2

--- a/solution.py
+++ b/solution.py
@@ -10,7 +10,7 @@
 PAR_DEV = 2
 BASE = 128
 LANES = 128
-UNIT_TILE = 256
+UNIT_TILE = 768
 VMEM = pl.BlockSpec(memory_space=pltpu.VMEM)
 HBM = pl.BlockSpec(memory_space=pl.ANY)
 VMEM_LIMIT = 40 * 1024 * 1024
@@ -28,30 +28,33 @@
     )(*operands)
 
 
-def split_kernel(hidden_ref, mine_ref, other_ref):
-    core = lax.axis_index("heads") % 2
-    quarter = mine_ref.shape[1] // 2
-    for pair in range(2):
-        to = slice(pair * quarter, (pair + 1) * quarter)
-        mine = pl.multiple_of((2 * pair + core) * quarter, quarter)
-        other = pl.multiple_of((2 * pair + 1 - core) * quarter, quarter)
-        mine_ref[:, to] = hidden_ref[:, pl.ds(mine, quarter)]
-        other_ref[:, to] = hidden_ref[:, pl.ds(other, quarter)]
-
-
-def stage_kernel(up_ref, down_ref, out_ref):
-    out_ref[...] = up_ref[:16, :LANES] + down_ref[:16, :LANES]
-
-
-def feed_forward(pieces, weights, gathered, own_quarter):
+def position_kernel(seq, out_ref):
+    shape = (out_ref.shape[0], out_ref.shape[1])
+    out_ref[...] = (lax.broadcasted_iota(jnp.int32, shape, 0) % seq).astype(jnp.float32)
+
+
+def merge_kernel(hidden_ref, beside_ref, position_ref, near_ref, far_ref):
     head = lax.axis_index("heads")
-    share, both = pieces[0].shape
-    quarter = both // 2
-    pair = head // 2 if own_quarter else 1 - head // 2
-    columns = pl.ds(pl.multiple_of(pair * quarter, quarter), quarter)
+    share, quarter = hidden_ref.shape[0], near_ref.shape[1]
+    for owner, ref in ((head, near_ref), (head ^ 2, far_ref)):
+        columns = pl.ds(pl.multiple_of(owner * quarter, quarter), quarter)
+        ref[:share, :] = hidden_ref[:, columns]
+        ref[share:, :] = beside_ref[:, columns]
+
+
+def feed_forward(hidden_ref, beside_ref, across_ref, weights, gathered, owner):
+    head = lax.axis_index("heads")
+    share, quarter = hidden_ref.shape[0], gathered.shape[1]
+    columns = pl.ds(pl.multiple_of(owner * quarter, quarter), quarter)
+    pieces = (
+        hidden_ref[:, columns],
+        beside_ref[:, columns],
+        across_ref[:share, :],
+        across_ref[share:, :],
+    )
     for flip, piece in enumerate(pieces):
         rows = pl.ds(pl.multiple_of((head ^ flip) * share, 64), share)
-        gathered[rows, :] = piece[:, columns]
+        gathered[rows, :] = piece
     tokens = gathered[...].T
     total = None
     for up_ref, down_ref in weights:
@@ -74,8 +77,10 @@
     return tokens, total
 
 
-def give_kernel(p0, p1, p2, p3, u0, d0, u1, d1, staged, out_ref, gathered):
-    _, total = feed_forward((p0, p1, p2, p3), ((u0, d0), (u1, d1)), gathered, False)
+def give_kernel(hidden_ref, beside_ref, across_ref, u0, d0, u1, d1, out_ref, gathered):
+    owner = lax.axis_index("heads") ^ 2
+    weights = ((u0, d0), (u1, d1))
+    _, total = feed_forward(hidden_ref, beside_ref, across_ref, weights, gathered, owner)
     out_ref[...] = total.astype(jnp.bfloat16)
 
 
@@ -88,24 +93,25 @@
 
 
 def keep_kernel(
-    p0, p1, p2, p3, u0, d0, u1, d1, length_ref, leaf_ref, parent_ref,
+    hidden_ref, beside_ref, across_ref, u0, d0, u1, d1, position_ref, length_ref, leaf_ref, parent_ref,
     out_ref, weight_ref, digits_ref, gathered,
 ):
     head = lax.axis_index("heads")
     rows, lanes = digits_ref.shape
     seq = out_ref.shape[0] // rows
     length = own_column(length_ref, rows, seq, head * rows)
-    position = lax.broadcasted_iota(jnp.int32, (rows * seq, 1), 0) % seq
-    weight = jnp.where(position.astype(jnp.float32) < length, 1.0 / length, 0.0)
-    weight_ref[...] = jnp.broadcast_to(weight, weight_ref.shape)
+    weight_ref[...] = jnp.where(position_ref[...] < length, 1.0 / length, 0.0)
     lane = lax.broadcasted_iota(jnp.int32, (rows, lanes), 1)
     digits = jnp.zeros((rows, lanes), jnp.int32)
-    for at, (ref, first) in enumerate(((leaf_ref, head * rows), (parent_ref, 0))):
+    for at, (ref, first) in enumerate(
+        ((leaf_ref, head * rows), (parent_ref, 0), (leaf_ref, (head ^ 1) * rows))
+    ):
         values = own_column(ref, rows, 1, first).astype(jnp.int32)
         digits = jnp.where(lane == 2 * at, values % BASE, digits)
         digits = jnp.where(lane == 2 * at + 1, values // BASE, digits)
     digits_ref[...] = digits.astype(jnp.float32)
-    tokens, total = feed_forward((p0, p1, p2, p3), ((u0, d0), (u1, d1)), gathered, True)
+    weights = ((u0, d0), (u1, d1))
+    tokens, total = feed_forward(hidden_ref, beside_ref, across_ref, weights, gathered, head)
     out_ref[...] = tokens.astype(jnp.float32) + total
 
 
@@ -130,17 +136,34 @@
     return result
 
 
+def near_kernel(leaf_count, near_ref, sum_ref, picker_ref, parent_ref):
+    leaves, width = sum_ref.shape
+    count = near_ref.shape[0]
+    owners = leaves // leaf_count
+    digits = near_ref[:, width:].astype(jnp.float32)
+    turned = digits.T
+    wanted = lax.broadcasted_iota(jnp.int32, (leaves, count), 0)
+
+    def pick(at):
+        leaf = (turned[at : at + 1] + BASE * turned[at + 1 : at + 2]).astype(jnp.int32)
+        return jnp.where(wanted == leaf, 1.0, 0.0).astype(jnp.bfloat16)
+
+    sum_ref[...] = jnp.dot(pick(0), near_ref[:, :width], preferred_element_type=jnp.float32)
+    picker_ref[...] = pick(4)
+    digits = digits.reshape(owners, count // owners, LANES)[:, :leaf_count].reshape(leaves, LANES)
+    parent = digits[:, 2:3] + BASE * digits[:, 3:4]
+    parent_ref[...] = jnp.broadcast_to(parent, parent_ref.shape)
+
+
 def leaf_kernel(
-    heads, near_ref, far_ref, embed_out, centers_out, parents_out,
-    embed_ref, centers_ref, parents_ref, scratch, sems,
+    heads, near_ref, far_ref, sum_ref, picker_ref, parent_ref,
+    embed_out, centers_out, parents_out, embed_ref, centers_ref, parents_ref, scratch, sems,
 ):
     head, index = lax.axis_index("heads"), lax.axis_index("labels")
     core = head % 2
     width = embed_ref.shape[1]
     rows = embed_ref.shape[0] // heads
     leaf_count = centers_ref.shape[0]
-    owners = near_ref.shape[0] // (2 * rows)
-    leaves = owners * leaf_count
     here = pl.ds(pl.multiple_of(index * 2 * rows, 2 * rows), 2 * rows)
     near = near_ref[here, :width].astype(jnp.float32)
     far = far_ref[here, :width].astype(jnp.float32)
@@ -150,15 +173,9 @@
     ).astype(jnp.bfloat16)
     embed_copy = pltpu.make_async_copy(embed_ref, embed_out, sems.at[0])
     embed_copy.start()
-    wanted = lax.broadcasted_iota(jnp.int32, (leaves, near_ref.shape[0]), 0)
-    leaf_sum = jnp.zeros((leaves, width), jnp.float32)
-    for ref in (near_ref, far_ref):
-        turned = ref[:, width:].astype(jnp.float32).T
-        leaf = (turned[0:1] + BASE * turned[1:2]).astype(jnp.int32)
-        picker = jnp.where(wanted == leaf, 1.0, 0.0).astype(jnp.bfloat16)
-        leaf_sum = leaf_sum + jnp.dot(
-            picker, ref[:, :width], preferred_element_type=jnp.float32
-        )
+    leaf_sum = sum_ref[...] + jnp.dot(
+        picker_ref[...], far_ref[:, :width], preferred_element_type=jnp.float32
+    )
     squares = jnp.mean(leaf_sum * leaf_sum, axis=1, keepdims=True)
     centers = leaf_sum * lax.rsqrt(squares + 1e-05)
     scratch[...] = centers
@@ -166,9 +183,7 @@
     centers_ref[...] = pick_share(own, head, heads)
     centers_copy = pltpu.make_async_copy(centers_ref, centers_out, sems.at[1])
     centers_copy.start()
-    digits = near_ref[:, width:].astype(jnp.float32)
-    digits = digits.reshape(owners, 2, rows, LANES)[:, 0, :leaf_count].reshape(leaves, LANES)
-    parent = (digits[:, 2:3] + BASE * digits[:, 3:4]).astype(jnp.int32)
+    parent = parent_ref[:, :1].astype(jnp.int32)
     sums = [
         jnp.sum(jnp.where(parent == index * PAR_DEV + p, centers, 0.0), axis=0, keepdims=True)
         for p in range(PAR_DEV)
@@ -196,26 +211,33 @@
     def array(*shape, dtype=jnp.float32):
         return jax.ShapeDtypeStruct(shape, dtype)
 
+    hidden = hidden_in.T
+    beside = swap(hidden, 1)
+    position = call(
+        functools.partial(position_kernel, token_rows // labels_here),
+        array(quarter, LANES),
+        (),
+        flops=5000000000,
+    )
+    merged = array(2 * share, quarter, dtype=jnp.bfloat16)
+    near, far = call(merge_kernel, (merged, merged), (hidden, beside, position), flops=10000000000)
     up_far, down_far = swap(w_up, 1), swap(w_down, 1)
-    half = array(share, 2 * quarter, dtype=jnp.bfloat16)
-    mine, other = call(split_kernel, (half, half), (hidden_in.T,), flops=0)
-    pieces = (mine, swap(other, 1), swap(mine, 2), swap(other, 3))
-    staged = call(stage_kernel, array(16, LANES, dtype=jnp.bfloat16), (w_up, w_down))
-    operands = (*pieces, w_up, w_down, up_far, down_far)
+    come_give, come_keep = swap(near, 2), swap(far, 2)
+    weights = (w_up, w_down, up_far, down_far)
     cost = dict(
         scratch=[pltpu.VMEM((width, quarter), jnp.bfloat16)],
         flops=8 * quarter * width * units,
         moved=8 * width * units,
     )
     given = call(
-        give_kernel, array(quarter, width, dtype=jnp.bfloat16), (*operands, staged), **cost
+        give_kernel, array(quarter, width, dtype=jnp.bfloat16), (hidden, beside, come_give, *weights), **cost
     )
     came = swap(given, 2)
     kept, weight, digits = call(
         keep_kernel,
         (array(quarter, width), array(quarter, LANES), array(rows, LANES)),
-        (*operands, title_length[None, :], label_leaf[None, :], leaf_parent[None, :]),
-        **cost,
+        (hidden, beside, come_keep, *weights, position, title_length[None, :], label_leaf[None, :], leaf_parent[None, :]),
+        **dict(cost, flops=10000000000),
     )
     message = call(
         embed_kernel,
@@ -236,6 +258,16 @@
         axis_index_groups=groups,
     ).reshape(members * rows, width + LANES)
     far = swap(near, 1)
+    leaves = owners * leaf_count
+    ready = call(
+        functools.partial(near_kernel, leaf_count),
+        (
+            array(leaves, width),
+            array(leaves, members * rows, dtype=jnp.bfloat16),
+            array(leaves, LANES),
+        ),
+        (near,),
+    )
     outputs = (
         array(labels_here, width, dtype=jnp.bfloat16),
         array(leaf_count, share),
@@ -244,10 +276,10 @@
     return call(
         functools.partial(leaf_kernel, heads),
         outputs,
-        (near, far),
+        (near, far, *ready),
         out_spec=HBM,
         scratch=[pltpu.VMEM(out.shape, out.dtype) for out in outputs]
-        + [pltpu.VMEM((owners * leaf_count, width), jnp.float32), pltpu.SemaphoreType.DMA((3,))],
+        + [pltpu.VMEM((leaves, width), jnp.float32), pltpu.SemaphoreType.DMA((3,))],
     )
 
 

time: 37.5 us -> 34.8 us (0.928)
  local copies, waits for them, and re-layouts: 3.52 us -> 0.07 us
  waiting for transfers between devices: 7.4 us -> 8.22 us
  Pallas kernels: 4.49 us -> 4.1 us
    unnamed x16 -> x14, local copies, waits for them, and re-layouts: 3.49 us -> 0.04 us
    ppermute x7, waiting for transfers between devices: 7.4 us -> 8.22 us  [swap(): return lax.ppermute(values, 'heads', [(i, i ^ flip) for i in range(heads)])]
    pallas_call x6 -> x7, Pallas kernels: 4.49 us -> 4.1 us  [call(): pl.pallas_call(kernel, out_shape=out_shape, in_specs=[VMEM] * len(operand...]
  transfers between devices with their start and end apart: 7 -> 7, of which waited for: 4 -> 4; matrix products, arithmetic and copies ran while one was open for 0% -> 0% of each run, Pallas kernels for 4% -> 7%
where the time goes in v3:
time: 34.8 us; the launch traced here: 34.6 us
  blocking collectives  15.3 us (44%)
  waiting for transfers between devices  8.22 us (24%)
  starting transfers between devices  6.15 us (18%)
  Pallas kernels  4.1 us (12%)
  between operations  0.75 us (2%)
    all_to_all x1, blocking collectives, local(): lax.all_to_all(jnp.broadcast_to(message[None], (members,) + message.shape...  15.3 us
    ppermute x7, waiting for transfers between devices, swap(): return lax.ppermute(values, 'heads', [(i, i ^ flip) for i in range(heads)])  8.22 us
    ppermute x7, starting transfers between devices, swap(): return lax.ppermute(values, 'heads', [(i, i ^ flip) for i in range(heads)])  6.15 us
    pallas_call x7, Pallas kernels, call(): pl.pallas_call(kernel, out_shape=out_shape, in_specs=[VMEM] * len(operand...  4.1 us
  transfers between devices with their start and end apart: 7, of which 4 were waited for; matrix products, arithmetic and copies ran while one was open for 0% of the time, Pallas kernels for 7%

profile of v3, /device:TPU:0, one launch (start us, length us, event | category | flops | bytes accessed | tf_op | source)
XLA Modules:
  0.0 34.6 jit_solution(648371286914332675)
XLA Ops:
  0.6 0.0 copy-start.2
  0.6 0.5 %collective-permute-start = (bf16[192,512]{1,0:T(8,128)(2,1)}, bf16[192,512]{1,0:T(8,128)(2,1)S(1)}, u32[]{:S(2)}, u32[]{:S(2)}) collective-permute-start(bf16[192,512]{1,0:T(8,128)(2,1)} %bitcast.8), channel_id=1, source_target_pairs={{0,1},{1,0},{2,3},{3,2},{4,5},{5,4},{6,7},{7,6},{8,9},{9,8},{10,11... | collective-permute-start | bytes 589832 | tf_op jit(solution)/shard_map/ppermute | solution.py:209
  1.2 0.1 collective-permute-start.2
  1.2 0.4 %collective-permute-start.3 = (bf16[768,768]{1,0:T(8,128)(2,1)}, bf16[768,768]{1,0:T(8,128)(2,1)S(1)}, u32[]{:S(2)}, u32[]{:S(2)}) collective-permute-start(bf16[768,768]{1,0:T(8,128)(2,1)} %d0.3), channel_id=1, source_target_pairs={{0,1},{1,0},{2,3},{3,2},{4,5},{5,4},{6,7},{7,6},{8,9},{9,8},{10,11... | collective-permute-start | bytes 3538952 | tf_op jit(solution)/shard_map/ppermute | solution.py:209
  1.7 0.0 copy-start.6
  1.7 0.0 copy-start
  1.7 0.0 copy-start.1
  1.7 0.7 %collective-permute-done.beside_ref = bf16[192,512]{1,0:T(8,128)(2,1)S(1)} collective-permute-done((bf16[192,512]{1,0:T(8,128)(2,1)}, bf16[192,512]{1,0:T(8,128)(2,1)S(1)}, u32[]{:S(2)}, u32[]{:S(2)}) %collective-permute-start) | collective-permute-done | bytes 196640 | tf_op jit(solution)/shard_map/ppermute | solution.py:209
  2.4 0.0 copy-done.2
  2.5 2.9 %collective-permute-start.4 = (bf16[384,128]{1,0:T(8,128)(2,1)S(1)}, bf16[384,128]{1,0:T(8,128)(2,1)S(1)}, u32[]{:S(2)}, u32[]{:S(2)}) collective-permute-start(bf16[384,128]{1,0:T(8,128)(2,1)S(1)} %get-tuple-element.13), channel_id=1, source_target_pairs={{0,2},{1,3},{2,0},{3,1},{4,6},{5,7},{6,4},{7,5},{8,10},{9,11},{10,... | collective-permute-start | bytes 294920 | tf_op jit(solution)/shard_map/ppermute | solution.py:209
  5.4 0.1 collective-permute-start.1
  5.5 0.0 copy-done.6
  5.5 0.0 copy-start.3
  5.5 0.0 copy-start.4
  5.5 0.0 copy-start.5
  5.5 3.5 %collective-permute-done.4.across_ref = bf16[384,128]{1,0:T(8,128)(2,1)S(1)} collective-permute-done((bf16[384,128]{1,0:T(8,128)(2,1)S(1)}, bf16[384,128]{1,0:T(8,128)(2,1)S(1)}, u32[]{:S(2)}, u32[]{:S(2)}) %collective-permute-start.4) | collective-permute-done | bytes 98336 | tf_op jit(solution)/shard_map/ppermute | solution.py:209
  9.0 0.0 collective-permute-done.2.u1
  9.0 0.0 collective-permute-done.3.d1
  9.0 0.0 copy-done
  9.0 0.0 copy-done.1
  9.0 1.1 %shard_map.97 = bf16[128,768]{1,0:T(8,128)(2,1)S(1)} custom-call(bf16[192,512]{1,0:T(8,128)(2,1)S(1)} %bitcast.10, bf16[192,512]{1,0:T(8,128)(2,1)S(1)} %collective-permute-done.beside_ref, bf16[384,128]{1,0:T(8,128)(2,1)S(1)} %collective-permute-done.4.across_ref, bf16[768,768]{1,0:T(8,128)(2,1)S(1)} %copy-done, bf16[768,768]{1,0:T(8,128)(2,1)S(1)} %copy-done.1, ...), custom_call_target="tpu_custom_call" | custom-call | flops 603979776 | bytes 4718592 | tf_op jit(solution)/shard_map/pallas_call | solution.py:20
  10.1 2.1 %collective-permute-start.5 = (bf16[128,768]{1,0:T(8,128)(2,1)S(1)}, bf16[128,768]{1,0:T(8,128)(2,1)S(1)}, u32[]{:S(2)}, u32[]{:S(2)}) collective-permute-start(bf16[128,768]{1,0:T(8,128)(2,1)S(1)} %shard_map.97), channel_id=1, source_target_pairs={{0,2},{1,3},{2,0},{3,1},{4,6},{5,7},{6,4},{7,5},{8,10},{9,11},{10,... | collective-permute-start | bytes 589832 | tf_op jit(solution)/shard_map/ppermute | solution.py:209
  12.2 0.0 collective-permute-done.1.across_ref
  12.2 0.0 copy-done.3
  12.3 0.0 copy-done.4
  12.3 0.0 copy-done.5
  12.3 1.1 %shard_map.96 = (f32[128,768]{1,0:T(8,128)S(1)}, f32[128,128]{1,0:T(8,128)S(1)}, f32[8,128]{1,0:T(8,128)S(1)}) custom-call(bf16[192,512]{1,0:T(8,128)(2,1)S(1)} %bitcast.11, bf16[192,512]{1,0:T(8,128)(2,1)S(1)} %collective-permute-done.beside_ref, bf16[384,128]{1,0:T(8,128)(2,1)S(1)} %collective-permute-done.1.across_ref, bf16[768,768]{1,0:T(8,128)(2,1)S(1)} %copy-done, ...), custom_call_target="tpu_custom_call" | custom-call | flops 10000000000 | bytes 4718592 | tf_op jit(solution)/shard_map/pallas_call | solution.py:20
  13.4 2.8 %collective-permute-done.5.came_ref = bf16[128,768]{1,0:T(8,128)(2,1)S(1)} collective-permute-done((bf16[128,768]{1,0:T(8,128)(2,1)S(1)}, bf16[128,768]{1,0:T(8,128)(2,1)S(1)}, u32[]{:S(2)}, u32[]{:S(2)}) %collective-permute-start.5) | collective-permute-done | bytes 196640 | tf_op jit(solution)/shard_map/ppermute | solution.py:209
  16.1 0.4 %shard_map.98 = bf16[8,896]{1,0:T(8,128)(2,1)S(1)} custom-call(f32[128,768]{1,0:T(8,128)S(1)} %get-tuple-element.12.kept_ref, bf16[128,768]{1,0:T(8,128)(2,1)S(1)} %collective-permute-done.5.came_ref, f32[128,128]{1,0:T(8,128)S(1)} %get-tuple-element.14.weight_ref, f32[8,128]{1,0:T(8,128)S(1)} %get-tuple-element.15.digits_ref, ...), custom_call_target="tpu_custom_call" | custom-call | tf_op jit(solution)/shard_map/pallas_call | solution.py:20
  16.6 15.3 %all_to_all.5 = bf16[16,8,896]{2,1,0:T(8,128)(2,1)S(1)} all-to-all(bf16[16,8,896]{2,1,0:T(8,128)(2,1)S(1)} %broadcast_in_dim.22), channel_id=1, replica_groups={{0,2,4,6,8,10,12,14,16,18,20,22,24,26,28,30},{1,3,5,7,9,11,13,15,17,19,..., dimensions={0} | all-to-all | bytes 458752 | tf_op jit(solution)/shard_map/all_to_all | solution.py:252
  31.9 0.0 collective-permute-start.6
  31.9 0.2 shard_map.99
  32.2 1.3 %collective-permute-done.6.far_ref = bf16[128,896]{1,0:T(8,128)(2,1)S(1)} collective-permute-done((bf16[128,896]{1,0:T(8,128)(2,1)S(1)}, bf16[128,896]{1,0:T(8,128)(2,1)S(1)}, u32[]{:S(2)}, u32[]{:S(2)}) %collective-permute-start.6) | collective-permute-done | bytes 229408 | tf_op jit(solution)/shard_map/ppermute | solution.py:209
  33.4 1.2 %shard_map.100 = (bf16[32,768]{1,0:T(8,128)(2,1)}, f32[8,192]{1,0:T(8,128)}, f32[2,192]{1,0:T(2,128)}) custom-call(bf16[128,896]{1,0:T(8,128)(2,1)S(1)} %bitcast.7, bf16[128,896]{1,0:T(8,128)(2,1)S(1)} %collective-permute-done.6.far_ref, f32[64,768]{1,0:T(8,128)S(1)} %get-tuple-element.16.sum_ref, bf16[64,128]{1,0:T(8,128)(2,1)S(1)} %get-tuple-element.17.picker_ref, ...), custom_call_target="tpu_custom_call" | custom-call | tf_op jit(solution)/shard_map/pallas_call | solution.py:20
  (4 shorter events, 0.1 us)
Async XLA Ops:
  0.6 1.8 %copy-start.2 = (bf16[512,192]{0,1:T(8,128)(2,1)S(1)}, bf16[512,192]{0,1:T(8,128)(2,1)}, u32[]{:S(2)}) copy-start(bf16[512,192]{0,1:T(8,128)(2,1)} %param.7) | copy-start | bytes 589828
  0.6 1.8 %collective-permute-start = (bf16[192,512]{1,0:T(8,128)(2,1)}, bf16[192,512]{1,0:T(8,128)(2,1)S(1)}, u32[]{:S(2)}, u32[]{:S(2)}) collective-permute-start(bf16[192,512]{1,0:T(8,128)(2,1)} %bitcast.8), channel_id=1, source_target_pairs={{0,1},{1,0},{2,3},{3,2},{4,5},{5,4},{6,7},{7,6},{8,9},{9,8},{10,11... | collective-permute-start | bytes 589832 | tf_op jit(solution)/shard_map/ppermute | solution.py:209
  1.2 7.8 %collective-permute-start.2 = (bf16[768,768]{1,0:T(8,128)(2,1)}, bf16[768,768]{1,0:T(8,128)(2,1)S(1)}, u32[]{:S(2)}, u32[]{:S(2)}) collective-permute-start(bf16[768,768]{1,0:T(8,128)(2,1)} %u0.3), channel_id=1, source_target_pairs={{0,1},{1,0},{2,3},{3,2},{4,5},{5,4},{6,7},{7,6},{8,9},{9,8},{10,11... | collective-permute-start | bytes 3538952 | tf_op jit(solution)/shard_map/ppermute | solution.py:209
  1.2 7.8 %collective-permute-start.3 = (bf16[768,768]{1,0:T(8,128)(2,1)}, bf16[768,768]{1,0:T(8,128)(2,1)S(1)}, u32[]{:S(2)}, u32[]{:S(2)}) collective-permute-start(bf16[768,768]{1,0:T(8,128)(2,1)} %d0.3), channel_id=1, source_target_pairs={{0,1},{1,0},{2,3},{3,2},{4,5},{5,4},{6,7},{7,6},{8,9},{9,8},{10,11... | collective-permute-start | bytes 3538952 | tf_op jit(solution)/shard_map/ppermute | solution.py:209
  1.7 3.8 %copy-start.6 = (f32[768]{0:T(1024)S(1)}, f32[768]{0:T(1024)}, u32[]{:S(2)}) copy-start(f32[768]{0:T(1024)} %param.10) | copy-start | bytes 9220
  1.7 7.3 %copy-start = (bf16[768,768]{1,0:T(8,128)(2,1)S(1)}, bf16[768,768]{1,0:T(8,128)(2,1)}, u32[]{:S(2)}) copy-start(bf16[768,768]{1,0:T(8,128)(2,1)} %u0.3) | copy-start | bytes 3538948
  1.7 7.3 %copy-start.1 = (bf16[768,768]{1,0:T(8,128)(2,1)S(1)}, bf16[768,768]{1,0:T(8,128)(2,1)}, u32[]{:S(2)}) copy-start(bf16[768,768]{1,0:T(8,128)(2,1)} %d0.3) | copy-start | bytes 3538948
  2.5 6.5 %collective-permute-start.4 = (bf16[384,128]{1,0:T(8,128)(2,1)S(1)}, bf16[384,128]{1,0:T(8,128)(2,1)S(1)}, u32[]{:S(2)}, u32[]{:S(2)}) collective-permute-start(bf16[384,128]{1,0:T(8,128)(2,1)S(1)} %get-tuple-element.13), channel_id=1, source_target_pairs={{0,2},{1,3},{2,0},{3,1},{4,6},{5,7},{6,4},{7,5},{8,10},{9,11},{10,... | collective-permute-start | bytes 294920 | tf_op jit(solution)/shard_map/ppermute | solution.py:209
  5.4 6.8 %collective-permute-start.1 = (bf16[384,128]{1,0:T(8,128)(2,1)S(1)}, bf16[384,128]{1,0:T(8,128)(2,1)S(1)}, u32[]{:S(2)}, u32[]{:S(2)}) collective-permute-start(bf16[384,128]{1,0:T(8,128)(2,1)S(1)} %get-tuple-element.11), channel_id=1, source_target_pairs={{0,2},{1,3},{2,0},{3,1},{4,6},{5,7},{6,4},{7,5},{8,10},{9,11},{10,... | collective-permute-start | bytes 294920 | tf_op jit(solution)/shard_map/ppermute | solution.py:209
  5.5 6.8 %copy-start.3 = (s32[32]{0:T(128)S(1)}, s32[32]{0:T(128)}, u32[]{:S(2)}) copy-start(s32[32]{0:T(128)} %param.11) | copy-start | bytes 388
  5.5 6.8 %copy-start.4 = (s32[32]{0:T(128)S(1)}, s32[32]{0:T(128)}, u32[]{:S(2)}) copy-start(s32[32]{0:T(128)} %param.12) | copy-start | bytes 388
  5.5 6.8 %copy-start.5 = (s32[8]{0:T(128)S(1)}, s32[8]{0:T(128)}, u32[]{:S(2)}) copy-start(s32[8]{0:T(128)} %param.13) | copy-start | bytes 100
  10.1 6.0 %collective-permute-start.5 = (bf16[128,768]{1,0:T(8,128)(2,1)S(1)}, bf16[128,768]{1,0:T(8,128)(2,1)S(1)}, u32[]{:S(2)}, u32[]{:S(2)}) collective-permute-start(bf16[128,768]{1,0:T(8,128)(2,1)S(1)} %shard_map.97), channel_id=1, source_target_pairs={{0,2},{1,3},{2,0},{3,1},{4,6},{5,7},{6,4},{7,5},{8,10},{9,11},{10,... | collective-permute-start | bytes 589832 | tf_op jit(solution)/shard_map/ppermute | solution.py:209
  31.9 1.5 %collective-permute-start.6 = (bf16[128,896]{1,0:T(8,128)(2,1)S(1)}, bf16[128,896]{1,0:T(8,128)(2,1)S(1)}, u32[]{:S(2)}, u32[]{:S(2)}) collective-permute-start(bf16[128,896]{1,0:T(8,128)(2,1)S(1)} %bitcast.5), channel_id=1, source_target_pairs={{0,1},{1,0},{2,3},{3,2},{4,5},{5,4},{6,7},{7,6},{8,9},{9,8},{10,11... | collective-permute-start | bytes 688136 | tf_op jit(solution)/shard_map/ppermute | solution.py:209

commit v4 on v3

--- a/solution.py
+++ b/solution.py
@@ -136,13 +136,25 @@
     return result
 
 
+def position_of(owners, owner):
+    half = owners // 2
+    return (1 - owner % 2) * half + half - 1 - owner // 2
+
+
+def owner_at(owners, position):
+    half = owners // 2
+    odd = jnp.where(position < half, 1, 0)
+    return 2 * (half - 1 - position + (1 - odd) * half) + odd
+
+
 def near_kernel(leaf_count, near_ref, sum_ref, picker_ref, parent_ref):
     leaves, width = sum_ref.shape
     count = near_ref.shape[0]
     owners = leaves // leaf_count
     digits = near_ref[:, width:].astype(jnp.float32)
     turned = digits.T
-    wanted = lax.broadcasted_iota(jnp.int32, (leaves, count), 0)
+    row = lax.broadcasted_iota(jnp.int32, (leaves, count), 0)
+    wanted = owner_at(owners, row // leaf_count) * leaf_count + row % leaf_count
 
     def pick(at):
         leaf = (turned[at : at + 1] + BASE * turned[at + 1 : at + 2]).astype(jnp.int32)
@@ -164,12 +176,13 @@
     width = embed_ref.shape[1]
     rows = embed_ref.shape[0] // heads
     leaf_count = centers_ref.shape[0]
-    here = pl.ds(pl.multiple_of(index * 2 * rows, 2 * rows), 2 * rows)
+    position = position_of(sum_ref.shape[0] // leaf_count, index)
+    here = pl.ds(pl.multiple_of(position * 2 * rows, 2 * rows), 2 * rows)
     near = near_ref[here, :width].astype(jnp.float32)
     far = far_ref[here, :width].astype(jnp.float32)
     even, odd = jnp.where(core == 0, near, far), jnp.where(core == 0, far, near)
     embed_ref[...] = jnp.concatenate(
-        [part[i * rows : (i + 1) * rows] for i in range(2) for part in (even, odd)], axis=0
+        [part[i * rows : (i + 1) * rows] for i in (1, 0) for part in (even, odd)], axis=0
     ).astype(jnp.bfloat16)
     embed_copy = pltpu.make_async_copy(embed_ref, embed_out, sems.at[0])
     embed_copy.start()
@@ -179,7 +192,7 @@
     squares = jnp.mean(leaf_sum * leaf_sum, axis=1, keepdims=True)
     centers = leaf_sum * lax.rsqrt(squares + 1e-05)
     scratch[...] = centers
-    own = scratch[pl.ds(pl.multiple_of(index * leaf_count, leaf_count), leaf_count), :]
+    own = scratch[pl.ds(pl.multiple_of(position * leaf_count, leaf_count), leaf_count), :]
     centers_ref[...] = pick_share(own, head, heads)
     centers_copy = pltpu.make_async_copy(centers_ref, centers_out, sems.at[1])
     centers_copy.start()
@@ -245,7 +258,11 @@
         (kept, came, weight, digits, norm_gain[None, :]),
     )
     groups = [
-        [owner * heads + head for owner in range(owners) for head in range(core, heads, 2)]
+        [
+            owner * heads + head
+            for owner in sorted(range(owners), key=functools.partial(position_of, owners))
+            for head in reversed(range(core, heads, 2))
+        ]
         for core in range(2)
     ]
     members = owners * heads // 2

time: 34.8 us -> 32 us (0.920)
  blocking collectives: 15.3 us -> 12.6 us
    all_to_all x1, blocking collectives: 15.3 us -> 12.6 us  [local(): lax.all_to_all(jnp.broadcast_to(message[None], (members,) + message.shape...]
  transfers between devices with their start and end apart: 7 -> 7, of which waited for: 4 -> 4; matrix products, arithmetic and copies ran while one was open for 0% -> 0% of each run, Pallas kernels for 7% -> 8%
where the time goes in v4:
time: 32 us; the launch traced here: 31.9 us
  blocking collectives  12.6 us (39%)
  waiting for transfers between devices  8.22 us (26%)
  starting transfers between devices  6.15 us (19%)
  Pallas kernels  4.1 us (13%)
  between operations  0.75 us (2%)
    all_to_all x1, blocking collectives, local(): lax.all_to_all(jnp.broadcast_to(message[None], (members,) + message.shape...  12.6 us
    ppermute x7, waiting for transfers between devices, swap(): return lax.ppermute(values, 'heads', [(i, i ^ flip) for i in range(heads)])  8.22 us
    ppermute x7, starting transfers between devices, swap(): return lax.ppermute(values, 'heads', [(i, i ^ flip) for i in range(heads)])  6.15 us
    pallas_call x7, Pallas kernels, call(): pl.pallas_call(kernel, out_shape=out_shape, in_specs=[VMEM] * len(operand...  4.1 us
  transfers between devices with their start and end apart: 7, of which 4 were waited for; matrix products, arithmetic and copies ran while one was open for 0% of the time, Pallas kernels for 8%

profile of v4, /device:TPU:0, one launch (start us, length us, event | category | flops | bytes accessed | tf_op | source)
XLA Modules:
  0.0 31.9 jit_solution(10653602168347601007)
XLA Ops:
  0.6 0.0 copy-start.2
  0.6 0.5 %collective-permute-start = (bf16[192,512]{1,0:T(8,128)(2,1)}, bf16[192,512]{1,0:T(8,128)(2,1)S(1)}, u32[]{:S(2)}, u32[]{:S(2)}) collective-permute-start(bf16[192,512]{1,0:T(8,128)(2,1)} %bitcast.8), channel_id=1, source_target_pairs={{0,1},{1,0},{2,3},{3,2},{4,5},{5,4},{6,7},{7,6},{8,9},{9,8},{10,11... | collective-permute-start | bytes 589832 | tf_op jit(solution)/shard_map/ppermute | solution.py:222
  1.2 0.1 collective-permute-start.2
  1.2 0.4 %collective-permute-start.3 = (bf16[768,768]{1,0:T(8,128)(2,1)}, bf16[768,768]{1,0:T(8,128)(2,1)S(1)}, u32[]{:S(2)}, u32[]{:S(2)}) collective-permute-start(bf16[768,768]{1,0:T(8,128)(2,1)} %d0.3), channel_id=1, source_target_pairs={{0,1},{1,0},{2,3},{3,2},{4,5},{5,4},{6,7},{7,6},{8,9},{9,8},{10,11... | collective-permute-start | bytes 3538952 | tf_op jit(solution)/shard_map/ppermute | solution.py:222
  1.7 0.0 copy-start.6
  1.7 0.0 copy-start
  1.7 0.0 copy-start.1
  1.7 0.7 %collective-permute-done.beside_ref = bf16[192,512]{1,0:T(8,128)(2,1)S(1)} collective-permute-done((bf16[192,512]{1,0:T(8,128)(2,1)}, bf16[192,512]{1,0:T(8,128)(2,1)S(1)}, u32[]{:S(2)}, u32[]{:S(2)}) %collective-permute-start) | collective-permute-done | bytes 196640 | tf_op jit(solution)/shard_map/ppermute | solution.py:222
  2.4 0.0 copy-done.2
  2.5 2.9 %collective-permute-start.4 = (bf16[384,128]{1,0:T(8,128)(2,1)S(1)}, bf16[384,128]{1,0:T(8,128)(2,1)S(1)}, u32[]{:S(2)}, u32[]{:S(2)}) collective-permute-start(bf16[384,128]{1,0:T(8,128)(2,1)S(1)} %get-tuple-element.13), channel_id=1, source_target_pairs={{0,2},{1,3},{2,0},{3,1},{4,6},{5,7},{6,4},{7,5},{8,10},{9,11},{10,... | collective-permute-start | bytes 294920 | tf_op jit(solution)/shard_map/ppermute | solution.py:222
  5.4 0.1 collective-permute-start.1
  5.5 0.0 copy-done.6
  5.5 0.0 copy-start.3
  5.5 0.0 copy-start.4
  5.5 0.0 copy-start.5
  5.5 3.5 %collective-permute-done.4.across_ref = bf16[384,128]{1,0:T(8,128)(2,1)S(1)} collective-permute-done((bf16[384,128]{1,0:T(8,128)(2,1)S(1)}, bf16[384,128]{1,0:T(8,128)(2,1)S(1)}, u32[]{:S(2)}, u32[]{:S(2)}) %collective-permute-start.4) | collective-permute-done | bytes 98336 | tf_op jit(solution)/shard_map/ppermute | solution.py:222
  9.0 0.0 collective-permute-done.2.u1
  9.0 0.0 collective-permute-done.3.d1
  9.0 0.0 copy-done
  9.0 0.0 copy-done.1
  9.0 1.1 %shard_map.97 = bf16[128,768]{1,0:T(8,128)(2,1)S(1)} custom-call(bf16[192,512]{1,0:T(8,128)(2,1)S(1)} %bitcast.10, bf16[192,512]{1,0:T(8,128)(2,1)S(1)} %collective-permute-done.beside_ref, bf16[384,128]{1,0:T(8,128)(2,1)S(1)} %collective-permute-done.4.across_ref, bf16[768,768]{1,0:T(8,128)(2,1)S(1)} %copy-done, bf16[768,768]{1,0:T(8,128)(2,1)S(1)} %copy-done.1, ...), custom_call_target="tpu_custom_call" | custom-call | flops 603979776 | bytes 4718592 | tf_op jit(solution)/shard_map/pallas_call | solution.py:20
  10.1 2.1 %collective-permute-start.5 = (bf16[128,768]{1,0:T(8,128)(2,1)S(1)}, bf16[128,768]{1,0:T(8,128)(2,1)S(1)}, u32[]{:S(2)}, u32[]{:S(2)}) collective-permute-start(bf16[128,768]{1,0:T(8,128)(2,1)S(1)} %shard_map.97), channel_id=1, source_target_pairs={{0,2},{1,3},{2,0},{3,1},{4,6},{5,7},{6,4},{7,5},{8,10},{9,11},{10,... | collective-permute-start | bytes 589832 | tf_op jit(solution)/shard_map/ppermute | solution.py:222
  12.2 0.0 collective-permute-done.1.across_ref
  12.2 0.0 copy-done.3
  12.3 0.0 copy-done.4
  12.3 0.0 copy-done.5
  12.3 1.1 %shard_map.96 = (f32[128,768]{1,0:T(8,128)S(1)}, f32[128,128]{1,0:T(8,128)S(1)}, f32[8,128]{1,0:T(8,128)S(1)}) custom-call(bf16[192,512]{1,0:T(8,128)(2,1)S(1)} %bitcast.11, bf16[192,512]{1,0:T(8,128)(2,1)S(1)} %collective-permute-done.beside_ref, bf16[384,128]{1,0:T(8,128)(2,1)S(1)} %collective-permute-done.1.across_ref, bf16[768,768]{1,0:T(8,128)(2,1)S(1)} %copy-done, ...), custom_call_target="tpu_custom_call" | custom-call | flops 10000000000 | bytes 4718592 | tf_op jit(solution)/shard_map/pallas_call | solution.py:20
  13.4 2.8 %collective-permute-done.5.came_ref = bf16[128,768]{1,0:T(8,128)(2,1)S(1)} collective-permute-done((bf16[128,768]{1,0:T(8,128)(2,1)S(1)}, bf16[128,768]{1,0:T(8,128)(2,1)S(1)}, u32[]{:S(2)}, u32[]{:S(2)}) %collective-permute-start.5) | collective-permute-done | bytes 196640 | tf_op jit(solution)/shard_map/ppermute | solution.py:222
  16.1 0.4 %shard_map.98 = bf16[8,896]{1,0:T(8,128)(2,1)S(1)} custom-call(f32[128,768]{1,0:T(8,128)S(1)} %get-tuple-element.12.kept_ref, bf16[128,768]{1,0:T(8,128)(2,1)S(1)} %collective-permute-done.5.came_ref, f32[128,128]{1,0:T(8,128)S(1)} %get-tuple-element.14.weight_ref, f32[8,128]{1,0:T(8,128)S(1)} %get-tuple-element.15.digits_ref, ...), custom_call_target="tpu_custom_call" | custom-call | tf_op jit(solution)/shard_map/pallas_call | solution.py:20
  16.6 12.6 %all_to_all.5 = bf16[16,8,896]{2,1,0:T(8,128)(2,1)S(1)} all-to-all(bf16[16,8,896]{2,1,0:T(8,128)(2,1)S(1)} %broadcast_in_dim.22), channel_id=1, replica_groups={{30,28,22,20,14,12,6,4,26,24,18,16,10,8,2,0},{31,29,23,21,15,13,7,5,27,..., dimensions={0} | all-to-all | bytes 458752 | tf_op jit(solution)/shard_map/all_to_all | solution.py:269
  29.2 0.0 collective-permute-start.6
  29.2 0.2 shard_map.99
  29.4 1.3 %collective-permute-done.6.far_ref = bf16[128,896]{1,0:T(8,128)(2,1)S(1)} collective-permute-done((bf16[128,896]{1,0:T(8,128)(2,1)S(1)}, bf16[128,896]{1,0:T(8,128)(2,1)S(1)}, u32[]{:S(2)}, u32[]{:S(2)}) %collective-permute-start.6) | collective-permute-done | bytes 229408 | tf_op jit(solution)/shard_map/ppermute | solution.py:222
  30.7 1.2 %shard_map.100 = (bf16[32,768]{1,0:T(8,128)(2,1)}, f32[8,192]{1,0:T(8,128)}, f32[2,192]{1,0:T(2,128)}) custom-call(bf16[128,896]{1,0:T(8,128)(2,1)S(1)} %bitcast.7, bf16[128,896]{1,0:T(8,128)(2,1)S(1)} %collective-permute-done.6.far_ref, f32[64,768]{1,0:T(8,128)S(1)} %get-tuple-element.16.sum_ref, bf16[64,128]{1,0:T(8,128)(2,1)S(1)} %get-tuple-element.17.picker_ref, ...), custom_call_target="tpu_custom_call" | custom-call | tf_op jit(solution)/shard_map/pallas_call | solution.py:20
  (4 shorter events, 0.1 us)
Async XLA Ops:
  0.6 1.8 %copy-start.2 = (bf16[512,192]{0,1:T(8,128)(2,1)S(1)}, bf16[512,192]{0,1:T(8,128)(2,1)}, u32[]{:S(2)}) copy-start(bf16[512,192]{0,1:T(8,128)(2,1)} %param.7) | copy-start | bytes 589828
  0.6 1.8 %collective-permute-start = (bf16[192,512]{1,0:T(8,128)(2,1)}, bf16[192,512]{1,0:T(8,128)(2,1)S(1)}, u32[]{:S(2)}, u32[]{:S(2)}) collective-permute-start(bf16[192,512]{1,0:T(8,128)(2,1)} %bitcast.8), channel_id=1, source_target_pairs={{0,1},{1,0},{2,3},{3,2},{4,5},{5,4},{6,7},{7,6},{8,9},{9,8},{10,11... | collective-permute-start | bytes 589832 | tf_op jit(solution)/shard_map/ppermute | solution.py:222
  1.2 7.8 %collective-permute-start.2 = (bf16[768,768]{1,0:T(8,128)(2,1)}, bf16[768,768]{1,0:T(8,128)(2,1)S(1)}, u32[]{:S(2)}, u32[]{:S(2)}) collective-permute-start(bf16[768,768]{1,0:T(8,128)(2,1)} %u0.3), channel_id=1, source_target_pairs={{0,1},{1,0},{2,3},{3,2},{4,5},{5,4},{6,7},{7,6},{8,9},{9,8},{10,11... | collective-permute-start | bytes 3538952 | tf_op jit(solution)/shard_map/ppermute | solution.py:222
  1.2 7.8 %collective-permute-start.3 = (bf16[768,768]{1,0:T(8,128)(2,1)}, bf16[768,768]{1,0:T(8,128)(2,1)S(1)}, u32[]{:S(2)}, u32[]{:S(2)}) collective-permute-start(bf16[768,768]{1,0:T(8,128)(2,1)} %d0.3), channel_id=1, source_target_pairs={{0,1},{1,0},{2,3},{3,2},{4,5},{5,4},{6,7},{7,6},{8,9},{9,8},{10,11... | collective-permute-start | bytes 3538952 | tf_op jit(solution)/shard_map/ppermute | solution.py:222
  1.7 3.8 %copy-start.6 = (f32[768]{0:T(1024)S(1)}, f32[768]{0:T(1024)}, u32[]{:S(2)}) copy-start(f32[768]{0:T(1024)} %param.10) | copy-start | bytes 9220
  1.7 7.3 %copy-start = (bf16[768,768]{1,0:T(8,128)(2,1)S(1)}, bf16[768,768]{1,0:T(8,128)(2,1)}, u32[]{:S(2)}) copy-start(bf16[768,768]{1,0:T(8,128)(2,1)} %u0.3) | copy-start | bytes 3538948
  1.7 7.3 %copy-start.1 = (bf16[768,768]{1,0:T(8,128)(2,1)S(1)}, bf16[768,768]{1,0:T(8,128)(2,1)}, u32[]{:S(2)}) copy-start(bf16[768,768]{1,0:T(8,128)(2,1)} %d0.3) | copy-start | bytes 3538948
  2.5 6.5 %collective-permute-start.4 = (bf16[384,128]{1,0:T(8,128)(2,1)S(1)}, bf16[384,128]{1,0:T(8,128)(2,1)S(1)}, u32[]{:S(2)}, u32[]{:S(2)}) collective-permute-start(bf16[384,128]{1,0:T(8,128)(2,1)S(1)} %get-tuple-element.13), channel_id=1, source_target_pairs={{0,2},{1,3},{2,0},{3,1},{4,6},{5,7},{6,4},{7,5},{8,10},{9,11},{10,... | collective-permute-start | bytes 294920 | tf_op jit(solution)/shard_map/ppermute | solution.py:222
  5.4 6.8 %collective-permute-start.1 = (bf16[384,128]{1,0:T(8,128)(2,1)S(1)}, bf16[384,128]{1,0:T(8,128)(2,1)S(1)}, u32[]{:S(2)}, u32[]{:S(2)}) collective-permute-start(bf16[384,128]{1,0:T(8,128)(2,1)S(1)} %get-tuple-element.11), channel_id=1, source_target_pairs={{0,2},{1,3},{2,0},{3,1},{4,6},{5,7},{6,4},{7,5},{8,10},{9,11},{10,... | collective-permute-start | bytes 294920 | tf_op jit(solution)/shard_map/ppermute | solution.py:222
  5.5 6.8 %copy-start.3 = (s32[32]{0:T(128)S(1)}, s32[32]{0:T(128)}, u32[]{:S(2)}) copy-start(s32[32]{0:T(128)} %param.11) | copy-start | bytes 388
  5.5 6.8 %copy-start.4 = (s32[32]{0:T(128)S(1)}, s32[32]{0:T(128)}, u32[]{:S(2)}) copy-start(s32[32]{0:T(128)} %param.12) | copy-start | bytes 388
  5.5 6.8 %copy-start.5 = (s32[8]{0:T(128)S(1)}, s32[8]{0:T(128)}, u32[]{:S(2)}) copy-start(s32[8]{0:T(128)} %param.13) | copy-start | bytes 100
  10.1 6.0 %collective-permute-start.5 = (bf16[128,768]{1,0:T(8,128)(2,1)S(1)}, bf16[128,768]{1,0:T(8,128)(2,1)S(1)}, u32[]{:S(2)}, u32[]{:S(2)}) collective-permute-start(bf16[128,768]{1,0:T(8,128)(2,1)S(1)} %shard_map.97), channel_id=1, source_target_pairs={{0,2},{1,3},{2,0},{3,1},{4,6},{5,7},{6,4},{7,5},{8,10},{9,11},{10,... | collective-permute-start | bytes 589832 | tf_op jit(solution)/shard_map/ppermute | solution.py:222
  29.2 1.5 %collective-permute-start.6 = (bf16[128,896]{1,0:T(8,128)(2,1)S(1)}, bf16[128,896]{1,0:T(8,128)(2,1)S(1)}, u32[]{:S(2)}, u32[]{:S(2)}) collective-permute-start(bf16[128,896]{1,0:T(8,128)(2,1)S(1)} %bitcast.5), channel_id=1, source_target_pairs={{0,1},{1,0},{2,3},{3,2},{4,5},{5,4},{6,7},{7,6},{8,9},{9,8},{10,11... | collective-permute-start | bytes 688136 | tf_op jit(solution)/shard_map/ppermute | solution.py:222

commit v5 on v4

--- a/solution.py
+++ b/solution.py
@@ -33,24 +33,29 @@
     out_ref[...] = (lax.broadcasted_iota(jnp.int32, shape, 0) % seq).astype(jnp.float32)
 
 
-def merge_kernel(hidden_ref, beside_ref, position_ref, near_ref, far_ref):
+def quarter_of(ref, owner, quarter):
+    return ref[:, pl.ds(pl.multiple_of(owner * quarter, quarter), quarter)]
+
+
+def own_kernel(hidden_ref, position_ref, near_ref):
+    near_ref[...] = quarter_of(hidden_ref, lax.axis_index("heads"), near_ref.shape[1])
+
+
+def merge_kernel(hidden_ref, beside_ref, near_ref, far_ref):
     head = lax.axis_index("heads")
-    share, quarter = hidden_ref.shape[0], near_ref.shape[1]
-    for owner, ref in ((head, near_ref), (head ^ 2, far_ref)):
-        columns = pl.ds(pl.multiple_of(owner * quarter, quarter), quarter)
-        ref[:share, :] = hidden_ref[:, columns]
-        ref[share:, :] = beside_ref[:, columns]
-
-
-def feed_forward(hidden_ref, beside_ref, across_ref, weights, gathered, owner):
+    share, quarter = near_ref.shape
+    near_ref[...] = quarter_of(beside_ref, head, quarter)
+    far_ref[:share, :] = quarter_of(hidden_ref, head ^ 2, quarter)
+    far_ref[share:, :] = quarter_of(beside_ref, head ^ 2, quarter)
+
+
+def feed_forward(hidden_ref, beside_ref, across, weights, gathered, owner):
     head = lax.axis_index("heads")
     share, quarter = hidden_ref.shape[0], gathered.shape[1]
-    columns = pl.ds(pl.multiple_of(owner * quarter, quarter), quarter)
     pieces = (
-        hidden_ref[:, columns],
-        beside_ref[:, columns],
-        across_ref[:share, :],
-        across_ref[share:, :],
+        quarter_of(hidden_ref, owner, quarter),
+        quarter_of(beside_ref, owner, quarter),
+        *across,
     )
     for flip, piece in enumerate(pieces):
         rows = pl.ds(pl.multiple_of((head ^ flip) * share, 64), share)
@@ -77,10 +82,11 @@
     return tokens, total
 
 
-def give_kernel(hidden_ref, beside_ref, across_ref, u0, d0, u1, d1, out_ref, gathered):
+def give_kernel(hidden_ref, beside_ref, across_ref, diagonal_ref, u0, d0, u1, d1, out_ref, gathered):
     owner = lax.axis_index("heads") ^ 2
     weights = ((u0, d0), (u1, d1))
-    _, total = feed_forward(hidden_ref, beside_ref, across_ref, weights, gathered, owner)
+    across = (across_ref[...], diagonal_ref[...])
+    _, total = feed_forward(hidden_ref, beside_ref, across, weights, gathered, owner)
     out_ref[...] = total.astype(jnp.bfloat16)
 
 
@@ -111,7 +117,9 @@
         digits = jnp.where(lane == 2 * at + 1, values // BASE, digits)
     digits_ref[...] = digits.astype(jnp.float32)
     weights = ((u0, d0), (u1, d1))
-    tokens, total = feed_forward(hidden_ref, beside_ref, across_ref, weights, gathered, head)
+    share = hidden_ref.shape[0]
+    across = (across_ref[:share, :], across_ref[share:, :])
+    tokens, total = feed_forward(hidden_ref, beside_ref, across, weights, gathered, head)
     out_ref[...] = tokens.astype(jnp.float32) + total
 
 
@@ -147,7 +155,7 @@
     return 2 * (half - 1 - position + (1 - odd) * half) + odd
 
 
-def near_kernel(leaf_count, near_ref, sum_ref, picker_ref, parent_ref):
+def near_kernel(heads, leaf_count, near_ref, sum_ref, share_ref, picker_ref, parent_ref):
     leaves, width = sum_ref.shape
     count = near_ref.shape[0]
     owners = leaves // leaf_count
@@ -160,7 +168,9 @@
         leaf = (turned[at : at + 1] + BASE * turned[at + 1 : at + 2]).astype(jnp.int32)
         return jnp.where(wanted == leaf, 1.0, 0.0).astype(jnp.bfloat16)
 
-    sum_ref[...] = jnp.dot(pick(0), near_ref[:, :width], preferred_element_type=jnp.float32)
+    near_sum = jnp.dot(pick(0), near_ref[:, :width], preferred_element_type=jnp.float32)
+    sum_ref[...] = near_sum
+    share_ref[...] = pick_share(near_sum, lax.axis_index("heads"), heads)
     picker_ref[...] = pick(4)
     digits = digits.reshape(owners, count // owners, LANES)[:, :leaf_count].reshape(leaves, LANES)
     parent = digits[:, 2:3] + BASE * digits[:, 3:4]
@@ -168,7 +178,7 @@
 
 
 def leaf_kernel(
-    heads, near_ref, far_ref, sum_ref, picker_ref, parent_ref,
+    heads, near_ref, far_ref, sum_ref, share_ref, picker_ref, parent_ref,
     embed_out, centers_out, parents_out, embed_ref, centers_ref, parents_ref, scratch, sems,
 ):
     head, index = lax.axis_index("heads"), lax.axis_index("labels")
@@ -186,14 +196,16 @@
     ).astype(jnp.bfloat16)
     embed_copy = pltpu.make_async_copy(embed_ref, embed_out, sems.at[0])
     embed_copy.start()
+    picker = picker_ref[...]
     leaf_sum = sum_ref[...] + jnp.dot(
-        picker_ref[...], far_ref[:, :width], preferred_element_type=jnp.float32
-    )
+        picker, far_ref[:, :width], preferred_element_type=jnp.float32
+    )
+    far_share = pick_share(far_ref[:, :width], head, heads)
+    leaf_share = share_ref[...] + jnp.dot(picker, far_share, preferred_element_type=jnp.float32)
     squares = jnp.mean(leaf_sum * leaf_sum, axis=1, keepdims=True)
-    centers = leaf_sum * lax.rsqrt(squares + 1e-05)
+    centers = leaf_share * lax.rsqrt(squares + 1e-05)
     scratch[...] = centers
-    own = scratch[pl.ds(pl.multiple_of(position * leaf_count, leaf_count), leaf_count), :]
-    centers_ref[...] = pick_share(own, head, heads)
+    centers_ref[...] = scratch[pl.ds(pl.multiple_of(position * leaf_count, leaf_count), leaf_count), :]
     centers_copy = pltpu.make_async_copy(centers_ref, centers_out, sems.at[1])
     centers_copy.start()
     parent = parent_ref[:, :1].astype(jnp.int32)
@@ -201,7 +213,7 @@
         jnp.sum(jnp.where(parent == index * PAR_DEV + p, centers, 0.0), axis=0, keepdims=True)
         for p in range(PAR_DEV)
     ]
-    parents_ref[...] = pick_share(jnp.concatenate(sums, axis=0), head, heads)
+    parents_ref[...] = jnp.concatenate(sums, axis=0)
     parents_copy = pltpu.make_async_copy(parents_ref, parents_out, sems.at[2])
     parents_copy.start()
     embed_copy.wait()
@@ -232,10 +244,17 @@
         (),
         flops=5000000000,
     )
-    merged = array(2 * share, quarter, dtype=jnp.bfloat16)
-    near, far = call(merge_kernel, (merged, merged), (hidden, beside, position), flops=10000000000)
     up_far, down_far = swap(w_up, 1), swap(w_down, 1)
-    come_give, come_keep = swap(near, 2), swap(far, 2)
+    piece = array(share, quarter, dtype=jnp.bfloat16)
+    across = swap(call(own_kernel, piece, (hidden, position), flops=5000000000), 2)
+    near, far = call(
+        merge_kernel,
+        (piece, array(2 * share, quarter, dtype=jnp.bfloat16)),
+        (hidden, beside),
+        flops=10000000000,
+    )
+    diagonal = swap(near, 2)
+    come_keep = swap(far, 2)
     weights = (w_up, w_down, up_far, down_far)
     cost = dict(
         scratch=[pltpu.VMEM((width, quarter), jnp.bfloat16)],
@@ -243,7 +262,7 @@
         moved=8 * width * units,
     )
     given = call(
-        give_kernel, array(quarter, width, dtype=jnp.bfloat16), (hidden, beside, come_give, *weights), **cost
+        give_kernel, array(quarter, width, dtype=jnp.bfloat16), (hidden, beside, across, diagonal, *weights), **cost
     )
     came = swap(given, 2)
     kept, weight, digits = call(
@@ -277,9 +296,10 @@
     far = swap(near, 1)
     leaves = owners * leaf_count
     ready = call(
-        functools.partial(near_kernel, leaf_count),
+        functools.partial(near_kernel, heads, leaf_count),
         (
             array(leaves, width),
+            array(leaves, share),
             array(leaves, members * rows, dtype=jnp.bfloat16),
             array(leaves, LANES),
         ),
@@ -296,7 +316,7 @@
         (near, far, *ready),
         out_spec=HBM,
         scratch=[pltpu.VMEM(out.shape, out.dtype) for out in outputs]
-        + [pltpu.VMEM((leaves, width), jnp.float32), pltpu.SemaphoreType.DMA((3,))],
+        + [pltpu.VMEM((leaves, share), jnp.float32), pltpu.SemaphoreType.DMA((3,))],
     )
 
 

time: 32 us -> 31.1 us (0.972)
  waiting for transfers between devices: 8.22 us -> 6.95 us
  starting transfers between devices: 6.15 us -> 7.08 us
  blocking collectives: 12.6 us -> 11.9 us
    ppermute x7 -> x8, waiting for transfers between devices: 8.22 us -> 6.95 us  [swap(): return lax.ppermute(values, 'heads', [(i, i ^ flip) for i in range(heads)])]
    ppermute x7 -> x8, starting transfers between devices: 6.15 us -> 7.08 us  [swap(): return lax.ppermute(values, 'heads', [(i, i ^ flip) for i in range(heads)])]
    all_to_all x1, blocking collectives: 12.6 us -> 11.9 us  [local(): lax.all_to_all(jnp.broadcast_to(message[None], (members,) + message.shape...]
    pallas_call x7 -> x8, Pallas kernels: 4.1 us -> 4.22 us  [call(): pl.pallas_call(kernel, out_shape=out_shape, in_specs=[VMEM] * len(operand...]
  transfers between devices with their start and end apart: 7 -> 8, of which waited for: 4 -> 3; matrix products, arithmetic and copies ran while one was open for 0% -> 0% of each run, Pallas kernels for 8% -> 9%
where the time goes in v5:
time: 31.1 us; the launch traced here: 31 us
  blocking collectives  11.9 us (38%)
  starting transfers between devices  7.08 us (23%)
  waiting for transfers between devices  6.95 us (22%)
  Pallas kernels  4.22 us (14%)
  between operations  0.77 us (2%)
    all_to_all x1, blocking collectives, local(): lax.all_to_all(jnp.broadcast_to(message[None], (members,) + message.shape...  11.9 us
    ppermute x8, starting transfers between devices, swap(): return lax.ppermute(values, 'heads', [(i, i ^ flip) for i in range(heads)])  7.08 us
    ppermute x8, waiting for transfers between devices, swap(): return lax.ppermute(values, 'heads', [(i, i ^ flip) for i in range(heads)])  6.95 us
    pallas_call x8, Pallas kernels, call(): pl.pallas_call(kernel, out_shape=out_shape, in_specs=[VMEM] * len(operand...  4.22 us
  transfers between devices with their start and end apart: 8, of which 3 were waited for; matrix products, arithmetic and copies ran while one was open for 0% of the time, Pallas kernels for 9%

profile of v5, /device:TPU:0, one launch (start us, length us, event | category | flops | bytes accessed | tf_op | source)
XLA Modules:
  0.0 31.0 jit_solution(2354909540889825686)
XLA Ops:
  0.6 0.0 copy-start.2
  0.6 0.5 %collective-permute-start = (bf16[192,512]{1,0:T(8,128)(2,1)}, bf16[192,512]{1,0:T(8,128)(2,1)S(1)}, u32[]{:S(2)}, u32[]{:S(2)}) collective-permute-start(bf16[192,512]{1,0:T(8,128)(2,1)} %bitcast.8), channel_id=1, source_target_pairs={{0,1},{1,0},{2,3},{3,2},{4,5},{5,4},{6,7},{7,6},{8,9},{9,8},{10,11... | collective-permute-start | bytes 589832 | tf_op jit(solution)/shard_map/ppermute | solution.py:234
  1.2 0.1 collective-permute-start.2
  1.2 0.4 %collective-permute-start.3 = (bf16[768,768]{1,0:T(8,128)(2,1)}, bf16[768,768]{1,0:T(8,128)(2,1)S(1)}, u32[]{:S(2)}, u32[]{:S(2)}) collective-permute-start(bf16[768,768]{1,0:T(8,128)(2,1)} %d0.3), channel_id=1, source_target_pairs={{0,1},{1,0},{2,3},{3,2},{4,5},{5,4},{6,7},{7,6},{8,9},{9,8},{10,11... | collective-permute-start | bytes 3538952 | tf_op jit(solution)/shard_map/ppermute | solution.py:234
  1.7 0.0 copy-done.2
  1.7 0.0 copy-start.6
  1.7 0.0 copy-start
  1.7 0.0 copy-start.1
  1.8 2.9 %collective-permute-start.4 = (bf16[192,128]{1,0:T(8,128)(2,1)S(1)}, bf16[192,128]{1,0:T(8,128)(2,1)S(1)}, u32[]{:S(2)}, u32[]{:S(2)}) collective-permute-start(bf16[192,128]{1,0:T(8,128)(2,1)S(1)} %shard_map.97), channel_id=1, source_target_pairs={{0,2},{1,3},{2,0},{3,1},{4,6},{5,7},{6,4},{7,5},{8,10},{9,11},{10,... | collective-permute-start | bytes 147464 | tf_op jit(solution)/shard_map/ppermute | solution.py:234
  4.6 0.0 collective-permute-done.beside_ref
  4.6 0.7 %collective-permute-start.5 = (bf16[192,128]{1,0:T(8,128)(2,1)S(1)}, bf16[192,128]{1,0:T(8,128)(2,1)S(1)}, u32[]{:S(2)}, u32[]{:S(2)}) collective-permute-start(bf16[192,128]{1,0:T(8,128)(2,1)S(1)} %get-tuple-element.14), channel_id=1, source_target_pairs={{0,2},{1,3},{2,0},{3,1},{4,6},{5,7},{6,4},{7,5},{8,10},{9,11},{10,... | collective-permute-start | bytes 147464 | tf_op jit(solution)/shard_map/ppermute | solution.py:234
  5.4 1.3 %collective-permute-start.1 = (bf16[384,128]{1,0:T(8,128)(2,1)S(1)}, bf16[384,128]{1,0:T(8,128)(2,1)S(1)}, u32[]{:S(2)}, u32[]{:S(2)}) collective-permute-start(bf16[384,128]{1,0:T(8,128)(2,1)S(1)} %get-tuple-element.12), channel_id=1, source_target_pairs={{0,2},{1,3},{2,0},{3,1},{4,6},{5,7},{6,4},{7,5},{8,10},{9,11},{10,... | collective-permute-start | bytes 294920 | tf_op jit(solution)/shard_map/ppermute | solution.py:234
  6.7 0.0 copy-done.6
  6.7 0.0 copy-start.3
  6.7 0.0 copy-start.4
  6.8 0.0 copy-start.5
  6.8 0.0 collective-permute-done.4.across_ref
  6.8 2.5 %collective-permute-done.5.diagonal_ref = bf16[192,128]{1,0:T(8,128)(2,1)S(1)} collective-permute-done((bf16[192,128]{1,0:T(8,128)(2,1)S(1)}, bf16[192,128]{1,0:T(8,128)(2,1)S(1)}, u32[]{:S(2)}, u32[]{:S(2)}) %collective-permute-start.5) | collective-permute-done | bytes 49184 | tf_op jit(solution)/shard_map/ppermute | solution.py:234
  9.2 0.0 collective-permute-done.2.u1
  9.2 0.0 collective-permute-done.3.d1
  9.2 0.0 copy-done
  9.3 0.0 copy-done.1
  9.3 1.1 %shard_map.98 = bf16[128,768]{1,0:T(8,128)(2,1)S(1)} custom-call(bf16[192,512]{1,0:T(8,128)(2,1)S(1)} %bitcast.11, bf16[192,512]{1,0:T(8,128)(2,1)S(1)} %collective-permute-done.beside_ref, bf16[192,128]{1,0:T(8,128)(2,1)S(1)} %collective-permute-done.4.across_ref, bf16[192,128]{1,0:T(8,128)(2,1)S(1)} %collective-permute-done.5.diagonal_ref, ...), custom_call_target="tpu_custom_call" | custom-call | flops 603979776 | bytes 4718592 | tf_op jit(solution)/shard_map/pallas_call | solution.py:20
  10.4 1.1 %collective-permute-start.6 = (bf16[128,768]{1,0:T(8,128)(2,1)S(1)}, bf16[128,768]{1,0:T(8,128)(2,1)S(1)}, u32[]{:S(2)}, u32[]{:S(2)}) collective-permute-start(bf16[128,768]{1,0:T(8,128)(2,1)S(1)} %shard_map.98), channel_id=1, source_target_pairs={{0,2},{1,3},{2,0},{3,1},{4,6},{5,7},{6,4},{7,5},{8,10},{9,11},{10,... | collective-permute-start | bytes 589832 | tf_op jit(solution)/shard_map/ppermute | solution.py:234
  11.5 0.0 collective-permute-done.1.across_ref
  11.5 0.0 copy-done.3
  11.5 0.0 copy-done.4
  11.5 0.0 copy-done.5
  11.5 1.1 %shard_map.96 = (f32[128,768]{1,0:T(8,128)S(1)}, f32[128,128]{1,0:T(8,128)S(1)}, f32[8,128]{1,0:T(8,128)S(1)}) custom-call(bf16[192,512]{1,0:T(8,128)(2,1)S(1)} %bitcast.12, bf16[192,512]{1,0:T(8,128)(2,1)S(1)} %collective-permute-done.beside_ref, bf16[384,128]{1,0:T(8,128)(2,1)S(1)} %collective-permute-done.1.across_ref, bf16[768,768]{1,0:T(8,128)(2,1)S(1)} %copy-done, ...), custom_call_target="tpu_custom_call" | custom-call | flops 10000000000 | bytes 4718592 | tf_op jit(solution)/shard_map/pallas_call | solution.py:20
  12.6 3.5 %collective-permute-done.6.came_ref = bf16[128,768]{1,0:T(8,128)(2,1)S(1)} collective-permute-done((bf16[128,768]{1,0:T(8,128)(2,1)S(1)}, bf16[128,768]{1,0:T(8,128)(2,1)S(1)}, u32[]{:S(2)}, u32[]{:S(2)}) %collective-permute-start.6) | collective-permute-done | bytes 196640 | tf_op jit(solution)/shard_map/ppermute | solution.py:234
  16.1 0.4 %shard_map.99 = bf16[8,896]{1,0:T(8,128)(2,1)S(1)} custom-call(f32[128,768]{1,0:T(8,128)S(1)} %get-tuple-element.13.kept_ref, bf16[128,768]{1,0:T(8,128)(2,1)S(1)} %collective-permute-done.6.came_ref, f32[128,128]{1,0:T(8,128)S(1)} %get-tuple-element.15.weight_ref, f32[8,128]{1,0:T(8,128)S(1)} %get-tuple-element.16.digits_ref, ...), custom_call_target="tpu_custom_call" | custom-call | tf_op jit(solution)/shard_map/pallas_call | solution.py:20
  16.6 11.9 %all_to_all.5 = bf16[16,8,896]{2,1,0:T(8,128)(2,1)S(1)} all-to-all(bf16[16,8,896]{2,1,0:T(8,128)(2,1)S(1)} %broadcast_in_dim.22), channel_id=1, replica_groups={{30,28,22,20,14,12,6,4,26,24,18,16,10,8,2,0},{31,29,23,21,15,13,7,5,27,..., dimensions={0} | all-to-all | bytes 458752 | tf_op jit(solution)/shard_map/all_to_all | solution.py:288
  28.5 0.0 collective-permute-start.7
  28.5 0.5 %shard_map.100 = (f32[64,768]{1,0:T(8,128)S(1)}, f32[64,192]{1,0:T(8,128)S(1)}, bf16[64,128]{1,0:T(8,128)(2,1)S(1)}, f32[64,128]{1,0:T(8,128)S(1)}) custom-call(bf16[128,896]{1,0:T(8,128)(2,1)S(1)} %bitcast.6), custom_call_target="tpu_custom_call" | custom-call | tf_op jit(solution)/shard_map/pallas_call | solution.py:20
  29.0 1.0 %collective-permute-done.7.far_ref = bf16[128,896]{1,0:T(8,128)(2,1)S(1)} collective-permute-done((bf16[128,896]{1,0:T(8,128)(2,1)S(1)}, bf16[128,896]{1,0:T(8,128)(2,1)S(1)}, u32[]{:S(2)}, u32[]{:S(2)}) %collective-permute-start.7) | collective-permute-done | bytes 229408 | tf_op jit(solution)/shard_map/ppermute | solution.py:234
  30.0 1.0 %shard_map.101 = (bf16[32,768]{1,0:T(8,128)(2,1)}, f32[8,192]{1,0:T(8,128)}, f32[2,192]{1,0:T(2,128)}) custom-call(bf16[128,896]{1,0:T(8,128)(2,1)S(1)} %bitcast.7, bf16[128,896]{1,0:T(8,128)(2,1)S(1)} %collective-permute-done.7.far_ref, f32[64,768]{1,0:T(8,128)S(1)} %get-tuple-element.17.sum_ref, f32[64,192]{1,0:T(8,128)S(1)} %get-tuple-element.18.share_ref, ...), custom_call_target="tpu_custom_call" | custom-call | tf_op jit(solution)/shard_map/pallas_call | solution.py:20
  (5 shorter events, 0.1 us)
Async XLA Ops:
  0.6 1.1 %copy-start.2 = (bf16[512,192]{0,1:T(8,128)(2,1)S(1)}, bf16[512,192]{0,1:T(8,128)(2,1)}, u32[]{:S(2)}) copy-start(bf16[512,192]{0,1:T(8,128)(2,1)} %param.7) | copy-start | bytes 589828
  0.6 4.0 %collective-permute-start = (bf16[192,512]{1,0:T(8,128)(2,1)}, bf16[192,512]{1,0:T(8,128)(2,1)S(1)}, u32[]{:S(2)}, u32[]{:S(2)}) collective-permute-start(bf16[192,512]{1,0:T(8,128)(2,1)} %bitcast.8), channel_id=1, source_target_pairs={{0,1},{1,0},{2,3},{3,2},{4,5},{5,4},{6,7},{7,6},{8,9},{9,8},{10,11... | collective-permute-start | bytes 589832 | tf_op jit(solution)/shard_map/ppermute | solution.py:234
  1.2 8.1 %collective-permute-start.2 = (bf16[768,768]{1,0:T(8,128)(2,1)}, bf16[768,768]{1,0:T(8,128)(2,1)S(1)}, u32[]{:S(2)}, u32[]{:S(2)}) collective-permute-start(bf16[768,768]{1,0:T(8,128)(2,1)} %u0.3), channel_id=1, source_target_pairs={{0,1},{1,0},{2,3},{3,2},{4,5},{5,4},{6,7},{7,6},{8,9},{9,8},{10,11... | collective-permute-start | bytes 3538952 | tf_op jit(solution)/shard_map/ppermute | solution.py:234
  1.2 8.0 %collective-permute-start.3 = (bf16[768,768]{1,0:T(8,128)(2,1)}, bf16[768,768]{1,0:T(8,128)(2,1)S(1)}, u32[]{:S(2)}, u32[]{:S(2)}) collective-permute-start(bf16[768,768]{1,0:T(8,128)(2,1)} %d0.3), channel_id=1, source_target_pairs={{0,1},{1,0},{2,3},{3,2},{4,5},{5,4},{6,7},{7,6},{8,9},{9,8},{10,11... | collective-permute-start | bytes 3538952 | tf_op jit(solution)/shard_map/ppermute | solution.py:234
  1.7 5.0 %copy-start.6 = (f32[768]{0:T(1024)S(1)}, f32[768]{0:T(1024)}, u32[]{:S(2)}) copy-start(f32[768]{0:T(1024)} %param.10) | copy-start | bytes 9220
  1.7 7.5 %copy-start = (bf16[768,768]{1,0:T(8,128)(2,1)S(1)}, bf16[768,768]{1,0:T(8,128)(2,1)}, u32[]{:S(2)}) copy-start(bf16[768,768]{1,0:T(8,128)(2,1)} %u0.3) | copy-start | bytes 3538948
  1.7 7.5 %copy-start.1 = (bf16[768,768]{1,0:T(8,128)(2,1)S(1)}, bf16[768,768]{1,0:T(8,128)(2,1)}, u32[]{:S(2)}) copy-start(bf16[768,768]{1,0:T(8,128)(2,1)} %d0.3) | copy-start | bytes 3538948
  1.8 5.0 %collective-permute-start.4 = (bf16[192,128]{1,0:T(8,128)(2,1)S(1)}, bf16[192,128]{1,0:T(8,128)(2,1)S(1)}, u32[]{:S(2)}, u32[]{:S(2)}) collective-permute-start(bf16[192,128]{1,0:T(8,128)(2,1)S(1)} %shard_map.97), channel_id=1, source_target_pairs={{0,2},{1,3},{2,0},{3,1},{4,6},{5,7},{6,4},{7,5},{8,10},{9,11},{10,... | collective-permute-start | bytes 147464 | tf_op jit(solution)/shard_map/ppermute | solution.py:234
  4.6 4.6 %collective-permute-start.5 = (bf16[192,128]{1,0:T(8,128)(2,1)S(1)}, bf16[192,128]{1,0:T(8,128)(2,1)S(1)}, u32[]{:S(2)}, u32[]{:S(2)}) collective-permute-start(bf16[192,128]{1,0:T(8,128)(2,1)S(1)} %get-tuple-element.14), channel_id=1, source_target_pairs={{0,2},{1,3},{2,0},{3,1},{4,6},{5,7},{6,4},{7,5},{8,10},{9,11},{10,... | collective-permute-start | bytes 147464 | tf_op jit(solution)/shard_map/ppermute | solution.py:234
  5.4 6.1 %collective-permute-start.1 = (bf16[384,128]{1,0:T(8,128)(2,1)S(1)}, bf16[384,128]{1,0:T(8,128)(2,1)S(1)}, u32[]{:S(2)}, u32[]{:S(2)}) collective-permute-start(bf16[384,128]{1,0:T(8,128)(2,1)S(1)} %get-tuple-element.12), channel_id=1, source_target_pairs={{0,2},{1,3},{2,0},{3,1},{4,6},{5,7},{6,4},{7,5},{8,10},{9,11},{10,... | collective-permute-start | bytes 294920 | tf_op jit(solution)/shard_map/ppermute | solution.py:234
  6.7 4.7 %copy-start.3 = (s32[32]{0:T(128)S(1)}, s32[32]{0:T(128)}, u32[]{:S(2)}) copy-start(s32[32]{0:T(128)} %param.11) | copy-start | bytes 388
  6.7 4.7 %copy-start.4 = (s32[32]{0:T(128)S(1)}, s32[32]{0:T(128)}, u32[]{:S(2)}) copy-start(s32[32]{0:T(128)} %param.12) | copy-start | bytes 388
  6.8 4.7 %copy-start.5 = (s32[8]{0:T(128)S(1)}, s32[8]{0:T(128)}, u32[]{:S(2)}) copy-start(s32[8]{0:T(128)} %param.13) | copy-start | bytes 100
  10.4 5.7 %collective-permute-start.6 = (bf16[128,768]{1,0:T(8,128)(2,1)S(1)}, bf16[128,768]{1,0:T(8,128)(2,1)S(1)}, u32[]{:S(2)}, u32[]{:S(2)}) collective-permute-start(bf16[128,768]{1,0:T(8,128)(2,1)S(1)} %shard_map.98), channel_id=1, source_target_pairs={{0,2},{1,3},{2,0},{3,1},{4,6},{5,7},{6,4},{7,5},{8,10},{9,11},{10,... | collective-permute-start | bytes 589832 | tf_op jit(solution)/shard_map/ppermute | solution.py:234
  28.5 1.5 %collective-permute-start.7 = (bf16[128,896]{1,0:T(8,128)(2,1)S(1)}, bf16[128,896]{1,0:T(8,128)(2,1)S(1)}, u32[]{:S(2)}, u32[]{:S(2)}) collective-permute-start(bf16[128,896]{1,0:T(8,128)(2,1)S(1)} %bitcast.5), channel_id=1, source_target_pairs={{0,1},{1,0},{2,3},{3,2},{4,5},{5,4},{6,7},{7,6},{8,9},{9,8},{10,11... | collective-permute-start | bytes 688136 | tf_op jit(solution)/shard_map/ppermute | solution.py:234

commit v6 on v5

--- a/solution.py
+++ b/solution.py
@@ -8,6 +8,7 @@
 from jax.sharding import PartitionSpec as P
 
 PAR_DEV = 2
+STRIDE = 5
 BASE = 128
 LANES = 128
 UNIT_TILE = 768
@@ -47,6 +48,10 @@
     near_ref[...] = quarter_of(beside_ref, head, quarter)
     far_ref[:share, :] = quarter_of(hidden_ref, head ^ 2, quarter)
     far_ref[share:, :] = quarter_of(beside_ref, head ^ 2, quarter)
+
+
+def gelu(upward):
+    return (0.5 * upward * (1.0 + lax.erf(upward * 0.7071067811865476))).astype(jnp.bfloat16)
 
 
 def feed_forward(hidden_ref, beside_ref, across, weights, gathered, owner):
@@ -70,11 +75,10 @@
             upward = jnp.dot(
                 tokens, up_ref[:, start : start + tile], preferred_element_type=jnp.float32
             )
-            activ = (0.5 * upward * (1.0 + lax.erf(upward * 0.7071067811865476))).astype(
-                jnp.bfloat16
-            )
             term = jnp.dot(
-                activ, down_ref[start : start + tile, :], preferred_element_type=jnp.float32
+                gelu(upward),
+                down_ref[start : start + tile, :],
+                preferred_element_type=jnp.float32,
             )
             part = term if part is None else part + term
         part = part.astype(jnp.bfloat16).astype(jnp.float32)
@@ -82,11 +86,41 @@
     return tokens, total
 
 
-def give_kernel(hidden_ref, beside_ref, across_ref, diagonal_ref, u0, d0, u1, d1, out_ref, gathered):
-    owner = lax.axis_index("heads") ^ 2
-    weights = ((u0, d0), (u1, d1))
-    across = (across_ref[...], diagonal_ref[...])
-    _, total = feed_forward(hidden_ref, beside_ref, across, weights, gathered, owner)
+def pair_tokens(near_ref, other_ref, columns, gathered):
+    head = lax.axis_index("heads")
+    share = near_ref.shape[0]
+    gathered[pl.ds(pl.multiple_of(head % 2 * share, 64), share), :] = near_ref[:, columns]
+    gathered[pl.ds(pl.multiple_of((head + 1) % 2 * share, 64), share), :] = other_ref[:, columns]
+    return gathered[...].T
+
+
+def pair_rows(ref, pair):
+    count = ref.shape[0] // 2
+    return ref[pl.ds(pl.multiple_of(pair * count, 128), count), :]
+
+
+def early_kernel(hidden_ref, beside_ref, u0, u1, out_ref, gathered):
+    head = lax.axis_index("heads")
+    quarter = gathered.shape[1]
+    columns = pl.ds(pl.multiple_of((head ^ 2) * quarter, quarter), quarter)
+    tokens = pair_tokens(hidden_ref, beside_ref, columns, gathered)
+    for i, up_ref in enumerate((u0, u1)):
+        out_ref[i] = jnp.dot(
+            tokens, pair_rows(up_ref, head // 2), preferred_element_type=jnp.float32
+        )
+
+
+def give_kernel(early_ref, across_ref, diagonal_ref, u0, d0, u1, d1, out_ref, gathered):
+    pair = 1 - lax.axis_index("heads") // 2
+    tokens = pair_tokens(across_ref, diagonal_ref, slice(None), gathered)
+    total = None
+    for i, (up_ref, down_ref) in enumerate(((u0, d0), (u1, d1))):
+        upward = early_ref[i] + jnp.dot(
+            tokens, pair_rows(up_ref, pair), preferred_element_type=jnp.float32
+        )
+        part = jnp.dot(gelu(upward), down_ref[...], preferred_element_type=jnp.float32)
+        part = part.astype(jnp.bfloat16).astype(jnp.float32)
+        total = part if total is None else total + part
     out_ref[...] = total.astype(jnp.bfloat16)
 
 
@@ -144,15 +178,21 @@
     return result
 
 
-def position_of(owners, owner):
+def stride_of(count):
+    return STRIDE if count % STRIDE else 1
+
+
+def position_of(owners, owner, lower):
     half = owners // 2
-    return (1 - owner % 2) * half + half - 1 - owner // 2
-
-
-def owner_at(owners, position):
+    place = 2 * ((1 - owner % 2) * half + half - 1 - owner // 2) + lower
+    return place * pow(stride_of(2 * owners), -1, 2 * owners) % (2 * owners)
+
+
+def owner_at(owners, block):
     half = owners // 2
-    odd = jnp.where(position < half, 1, 0)
-    return 2 * (half - 1 - position + (1 - odd) * half) + odd
+    place = block * stride_of(2 * owners) % owners
+    odd = jnp.where(place < half, 1, 0)
+    return 2 * (half - 1 - place + (1 - odd) * half) + odd
 
 
 def near_kernel(heads, leaf_count, near_ref, sum_ref, share_ref, picker_ref, parent_ref):
@@ -186,14 +226,18 @@
     width = embed_ref.shape[1]
     rows = embed_ref.shape[0] // heads
     leaf_count = centers_ref.shape[0]
-    position = position_of(sum_ref.shape[0] // leaf_count, index)
-    here = pl.ds(pl.multiple_of(position * 2 * rows, 2 * rows), 2 * rows)
-    near = near_ref[here, :width].astype(jnp.float32)
-    far = far_ref[here, :width].astype(jnp.float32)
-    even, odd = jnp.where(core == 0, near, far), jnp.where(core == 0, far, near)
-    embed_ref[...] = jnp.concatenate(
-        [part[i * rows : (i + 1) * rows] for i in (1, 0) for part in (even, odd)], axis=0
-    ).astype(jnp.bfloat16)
+    owners = sum_ref.shape[0] // leaf_count
+    upper, lower = position_of(owners, index, 0), position_of(owners, index, 1)
+
+    def own_rows(ref, position, half):
+        pair = pl.ds(pl.multiple_of(position // 2 * 2 * rows, 2 * rows), 2 * rows)
+        return ref[pair, :width].astype(jnp.float32)[half * rows : (half + 1) * rows]
+
+    blocks = []
+    for position, half in ((lower, 1), (upper, 0)):
+        near, far = own_rows(near_ref, position, half), own_rows(far_ref, position, half)
+        blocks += [jnp.where(core == 0, near, far), jnp.where(core == 0, far, near)]
+    embed_ref[...] = jnp.concatenate(blocks, axis=0).astype(jnp.bfloat16)
     embed_copy = pltpu.make_async_copy(embed_ref, embed_out, sems.at[0])
     embed_copy.start()
     picker = picker_ref[...]
@@ -205,7 +249,8 @@
     squares = jnp.mean(leaf_sum * leaf_sum, axis=1, keepdims=True)
     centers = leaf_share * lax.rsqrt(squares + 1e-05)
     scratch[...] = centers
-    centers_ref[...] = scratch[pl.ds(pl.multiple_of(position * leaf_count, leaf_count), leaf_count), :]
+    own = pl.ds(pl.multiple_of(upper // 2 * leaf_count, leaf_count), leaf_count)
+    centers_ref[...] = scratch[own, :]
     centers_copy = pltpu.make_async_copy(centers_ref, centers_out, sems.at[1])
     centers_copy.start()
     parent = parent_ref[:, :1].astype(jnp.int32)
@@ -261,15 +306,31 @@
         flops=8 * quarter * width * units,
         moved=8 * width * units,
     )
+    half = [pltpu.VMEM((width // 2, quarter), jnp.bfloat16)]
+    early = call(
+        early_kernel,
+        array(2, quarter, units),
+        (hidden, beside, w_up, up_far),
+        scratch=half,
+        flops=0,
+    )
     given = call(
-        give_kernel, array(quarter, width, dtype=jnp.bfloat16), (hidden, beside, across, diagonal, *weights), **cost
+        give_kernel,
+        array(quarter, width, dtype=jnp.bfloat16),
+        (early, across, diagonal, *weights),
+        scratch=half,
+        flops=8 * quarter * width * units,
+        moved=8 * width * units,
     )
     came = swap(given, 2)
     kept, weight, digits = call(
         keep_kernel,
         (array(quarter, width), array(quarter, LANES), array(rows, LANES)),
-        (hidden, beside, come_keep, *weights, position, title_length[None, :], label_leaf[None, :], leaf_parent[None, :]),
-        **dict(cost, flops=10000000000),
+        (
+            *(hidden, beside, come_keep, *weights, position),
+            *(title_length[None, :], label_leaf[None, :], leaf_parent[None, :]),
+        ),
+        **dict(cost, flops=10_000_000_000),
     )
     message = call(
         embed_kernel,
@@ -277,11 +338,10 @@
         (kept, came, weight, digits, norm_gain[None, :]),
     )
     groups = [
-        [
-            owner * heads + head
-            for owner in sorted(range(owners), key=functools.partial(position_of, owners))
-            for head in reversed(range(core, heads, 2))
-        ]
+        sorted(
+            range(core, owners * heads, 2),
+            key=lambda rank: position_of(owners, rank // heads, 1 - rank % heads // 2),
+        )
         for core in range(2)
     ]
     members = owners * heads // 2

time: 31.1 us -> 30.8 us (level)
  waiting for transfers between devices: 6.95 us -> 6.49 us
    ppermute x8, waiting for transfers between devices: 6.95 us -> 6.49 us  [swap(): return lax.ppermute(values, 'heads', [(i, i ^ flip) for i in range(heads)])]
    pallas_call x8 -> x9, Pallas kernels: 4.22 us -> 4.51 us  [call(): pl.pallas_call(kernel, out_shape=out_shape, in_specs=[VMEM] * len(operand...]
  transfers between devices with their start and end apart: 8 -> 8, of which waited for: 3 -> 3; matrix products, arithmetic and copies ran while one was open for 0% -> 0% of each run, Pallas kernels for 9% -> 10%
where the time goes in v6:
time: 30.8 us; the launch traced here: 30.6 us
  blocking collectives  11.7 us (38%)
  starting transfers between devices  7.08 us (23%)
  waiting for transfers between devices  6.49 us (21%)
  Pallas kernels  4.51 us (15%)
  between operations  0.78 us (3%)
    all_to_all x1, blocking collectives, local(): lax.all_to_all(jnp.broadcast_to(message[None], (members,) + message.shape...  11.7 us
    ppermute x8, starting transfers between devices, swap(): return lax.ppermute(values, 'heads', [(i, i ^ flip) for i in range(heads)])  7.08 us
    ppermute x8, waiting for transfers between devices, swap(): return lax.ppermute(values, 'heads', [(i, i ^ flip) for i in range(heads)])  6.49 us
    pallas_call x9, Pallas kernels, call(): pl.pallas_call(kernel, out_shape=out_shape, in_specs=[VMEM] * len(operand...  4.51 us
  transfers between devices with their start and end apart: 8, of which 3 were waited for; matrix products, arithmetic and copies ran while one was open for 0% of the time, Pallas kernels for 10%

profile of v6, /device:TPU:0, one launch (start us, length us, event | category | flops | bytes accessed | tf_op | source)
XLA Modules:
  0.0 30.6 jit_solution(16561905953996347045)
XLA Ops:
  0.6 0.0 copy-start.2
  0.6 0.5 %collective-permute-start = (bf16[192,512]{1,0:T(8,128)(2,1)}, bf16[192,512]{1,0:T(8,128)(2,1)S(1)}, u32[]{:S(2)}, u32[]{:S(2)}) collective-permute-start(bf16[192,512]{1,0:T(8,128)(2,1)} %bitcast.8), channel_id=1, source_target_pairs={{0,1},{1,0},{2,3},{3,2},{4,5},{5,4},{6,7},{7,6},{8,9},{9,8},{10,11... | collective-permute-start | bytes 589832 | tf_op jit(solution)/shard_map/ppermute | solution.py:279
  1.2 0.1 collective-permute-start.2
  1.2 0.4 %collective-permute-start.3 = (bf16[768,768]{1,0:T(8,128)(2,1)}, bf16[768,768]{1,0:T(8,128)(2,1)S(1)}, u32[]{:S(2)}, u32[]{:S(2)}) collective-permute-start(bf16[768,768]{1,0:T(8,128)(2,1)} %d0.3), channel_id=1, source_target_pairs={{0,1},{1,0},{2,3},{3,2},{4,5},{5,4},{6,7},{7,6},{8,9},{9,8},{10,11... | collective-permute-start | bytes 3538952 | tf_op jit(solution)/shard_map/ppermute | solution.py:279
  1.7 0.0 copy-done.2
  1.7 0.0 copy-start.6
  1.7 0.0 copy-start
  1.7 2.9 %collective-permute-start.4 = (bf16[192,128]{1,0:T(8,128)(2,1)S(1)}, bf16[192,128]{1,0:T(8,128)(2,1)S(1)}, u32[]{:S(2)}, u32[]{:S(2)}) collective-permute-start(bf16[192,128]{1,0:T(8,128)(2,1)S(1)} %shard_map.98), channel_id=1, source_target_pairs={{0,2},{1,3},{2,0},{3,1},{4,6},{5,7},{6,4},{7,5},{8,10},{9,11},{10,... | collective-permute-start | bytes 147464 | tf_op jit(solution)/shard_map/ppermute | solution.py:279
  4.6 0.0 collective-permute-done.beside_ref
  4.6 0.8 %collective-permute-start.5 = (bf16[192,128]{1,0:T(8,128)(2,1)S(1)}, bf16[192,128]{1,0:T(8,128)(2,1)S(1)}, u32[]{:S(2)}, u32[]{:S(2)}) collective-permute-start(bf16[192,128]{1,0:T(8,128)(2,1)S(1)} %get-tuple-element.14), channel_id=1, source_target_pairs={{0,2},{1,3},{2,0},{3,1},{4,6},{5,7},{6,4},{7,5},{8,10},{9,11},{10,... | collective-permute-start | bytes 147464 | tf_op jit(solution)/shard_map/ppermute | solution.py:279
  5.4 1.3 %collective-permute-start.1 = (bf16[384,128]{1,0:T(8,128)(2,1)S(1)}, bf16[384,128]{1,0:T(8,128)(2,1)S(1)}, u32[]{:S(2)}, u32[]{:S(2)}) collective-permute-start(bf16[384,128]{1,0:T(8,128)(2,1)S(1)} %get-tuple-element.12), channel_id=1, source_target_pairs={{0,2},{1,3},{2,0},{3,1},{4,6},{5,7},{6,4},{7,5},{8,10},{9,11},{10,... | collective-permute-start | bytes 294920 | tf_op jit(solution)/shard_map/ppermute | solution.py:279
  6.7 0.0 copy-done.6
  6.7 0.0 copy-start.1
  6.7 0.0 collective-permute-done.2.u1
  6.7 0.0 copy-done
  6.8 0.4 %shard_map.97.early_ref = f32[2,128,768]{2,1,0:T(8,128)S(1)} custom-call(bf16[192,512]{1,0:T(8,128)(2,1)S(1)} %bitcast.11, bf16[192,512]{1,0:T(8,128)(2,1)S(1)} %collective-permute-done.beside_ref, bf16[768,768]{1,0:T(8,128)(2,1)S(1)} %copy-done, bf16[768,768]{1,0:T(8,128)(2,1)S(1)} %collective-permute-done.2.u1), custom_call_target="tpu_custom_call" | custom-call | tf_op jit(solution)/shard_map/pallas_call | solution.py:21
  7.2 0.0 copy-start.3
  7.2 0.0 copy-start.4
  7.2 0.0 copy-start.5
  7.2 0.0 collective-permute-done.4.across_ref
  7.2 2.0 %collective-permute-done.5.diagonal_ref = bf16[192,128]{1,0:T(8,128)(2,1)S(1)} collective-permute-done((bf16[192,128]{1,0:T(8,128)(2,1)S(1)}, bf16[192,128]{1,0:T(8,128)(2,1)S(1)}, u32[]{:S(2)}, u32[]{:S(2)}) %collective-permute-start.5) | collective-permute-done | bytes 49184 | tf_op jit(solution)/shard_map/ppermute | solution.py:279
  9.2 0.0 collective-permute-done.3.d1
  9.2 0.0 copy-done.1
  9.2 1.0 %shard_map.99 = bf16[128,768]{1,0:T(8,128)(2,1)S(1)} custom-call(f32[2,128,768]{2,1,0:T(8,128)S(1)} %shard_map.97.early_ref, bf16[192,128]{1,0:T(8,128)(2,1)S(1)} %collective-permute-done.4.across_ref, bf16[192,128]{1,0:T(8,128)(2,1)S(1)} %collective-permute-done.5.diagonal_ref, bf16[768,768]{1,0:T(8,128)(2,1)S(1)} %copy-done, ...), custom_call_target="tpu_custom_call" | custom-call | flops 603979776 | bytes 4718592 | tf_op jit(solution)/shard_map/pallas_call | solution.py:21
  10.2 1.1 %collective-permute-start.6 = (bf16[128,768]{1,0:T(8,128)(2,1)S(1)}, bf16[128,768]{1,0:T(8,128)(2,1)S(1)}, u32[]{:S(2)}, u32[]{:S(2)}) collective-permute-start(bf16[128,768]{1,0:T(8,128)(2,1)S(1)} %shard_map.99), channel_id=1, source_target_pairs={{0,2},{1,3},{2,0},{3,1},{4,6},{5,7},{6,4},{7,5},{8,10},{9,11},{10,... | collective-permute-start | bytes 589832 | tf_op jit(solution)/shard_map/ppermute | solution.py:279
  11.3 0.0 collective-permute-done.1.across_ref
  11.3 0.0 copy-done.3
  11.3 0.0 copy-done.4
  11.3 0.0 copy-done.5
  11.3 1.1 %shard_map.96 = (f32[128,768]{1,0:T(8,128)S(1)}, f32[128,128]{1,0:T(8,128)S(1)}, f32[8,128]{1,0:T(8,128)S(1)}) custom-call(bf16[192,512]{1,0:T(8,128)(2,1)S(1)} %bitcast.12, bf16[192,512]{1,0:T(8,128)(2,1)S(1)} %collective-permute-done.beside_ref, bf16[384,128]{1,0:T(8,128)(2,1)S(1)} %collective-permute-done.1.across_ref, bf16[768,768]{1,0:T(8,128)(2,1)S(1)} %copy-done, ...), custom_call_target="tpu_custom_call" | custom-call | flops 10000000000 | bytes 4718592 | tf_op jit(solution)/shard_map/pallas_call | solution.py:21
  12.5 3.5 %collective-permute-done.6.came_ref = bf16[128,768]{1,0:T(8,128)(2,1)S(1)} collective-permute-done((bf16[128,768]{1,0:T(8,128)(2,1)S(1)}, bf16[128,768]{1,0:T(8,128)(2,1)S(1)}, u32[]{:S(2)}, u32[]{:S(2)}) %collective-permute-start.6) | collective-permute-done | bytes 196640 | tf_op jit(solution)/shard_map/ppermute | solution.py:279
  16.0 0.4 %shard_map.100 = bf16[8,896]{1,0:T(8,128)(2,1)S(1)} custom-call(f32[128,768]{1,0:T(8,128)S(1)} %get-tuple-element.13.kept_ref, bf16[128,768]{1,0:T(8,128)(2,1)S(1)} %collective-permute-done.6.came_ref, f32[128,128]{1,0:T(8,128)S(1)} %get-tuple-element.15.weight_ref, f32[8,128]{1,0:T(8,128)S(1)} %get-tuple-element.16.digits_ref, ...), custom_call_target="tpu_custom_call" | custom-call | tf_op jit(solution)/shard_map/pallas_call | solution.py:21
  16.4 11.7 %all_to_all.5 = bf16[16,8,896]{2,1,0:T(8,128)(2,1)S(1)} all-to-all(bf16[16,8,896]{2,1,0:T(8,128)(2,1)S(1)} %broadcast_in_dim.22), channel_id=1, replica_groups={{30,12,18,0,14,24,2,20,26,8,22,4,10,28,6,16},{31,13,19,1,15,25,3,21,27,..., dimensions={0} | all-to-all | bytes 458752 | tf_op jit(solution)/shard_map/all_to_all | solution.py:348
  28.1 0.0 collective-permute-start.7
  28.1 0.5 %shard_map.101 = (f32[64,768]{1,0:T(8,128)S(1)}, f32[64,192]{1,0:T(8,128)S(1)}, bf16[64,128]{1,0:T(8,128)(2,1)S(1)}, f32[64,128]{1,0:T(8,128)S(1)}) custom-call(bf16[128,896]{1,0:T(8,128)(2,1)S(1)} %bitcast.6), custom_call_target="tpu_custom_call" | custom-call | tf_op jit(solution)/shard_map/pallas_call | solution.py:21
  28.6 1.0 %collective-permute-done.7.far_ref = bf16[128,896]{1,0:T(8,128)(2,1)S(1)} collective-permute-done((bf16[128,896]{1,0:T(8,128)(2,1)S(1)}, bf16[128,896]{1,0:T(8,128)(2,1)S(1)}, u32[]{:S(2)}, u32[]{:S(2)}) %collective-permute-start.7) | collective-permute-done | bytes 229408 | tf_op jit(solution)/shard_map/ppermute | solution.py:279
  29.6 1.0 %shard_map.102 = (bf16[32,768]{1,0:T(8,128)(2,1)}, f32[8,192]{1,0:T(8,128)}, f32[2,192]{1,0:T(2,128)}) custom-call(bf16[128,896]{1,0:T(8,128)(2,1)S(1)} %bitcast.7, bf16[128,896]{1,0:T(8,128)(2,1)S(1)} %collective-permute-done.7.far_ref, f32[64,768]{1,0:T(8,128)S(1)} %get-tuple-element.17.sum_ref, f32[64,192]{1,0:T(8,128)S(1)} %get-tuple-element.18.share_ref, ...), custom_call_target="tpu_custom_call" | custom-call | tf_op jit(solution)/shard_map/pallas_call | solution.py:21
  (5 shorter events, 0.1 us)
Async XLA Ops:
  0.6 1.1 %copy-start.2 = (bf16[512,192]{0,1:T(8,128)(2,1)S(1)}, bf16[512,192]{0,1:T(8,128)(2,1)}, u32[]{:S(2)}) copy-start(bf16[512,192]{0,1:T(8,128)(2,1)} %param.7) | copy-start | bytes 589828
  0.6 4.0 %collective-permute-start = (bf16[192,512]{1,0:T(8,128)(2,1)}, bf16[192,512]{1,0:T(8,128)(2,1)S(1)}, u32[]{:S(2)}, u32[]{:S(2)}) collective-permute-start(bf16[192,512]{1,0:T(8,128)(2,1)} %bitcast.8), channel_id=1, source_target_pairs={{0,1},{1,0},{2,3},{3,2},{4,5},{5,4},{6,7},{7,6},{8,9},{9,8},{10,11... | collective-permute-start | bytes 589832 | tf_op jit(solution)/shard_map/ppermute | solution.py:279
  1.2 5.6 %collective-permute-start.2 = (bf16[768,768]{1,0:T(8,128)(2,1)}, bf16[768,768]{1,0:T(8,128)(2,1)S(1)}, u32[]{:S(2)}, u32[]{:S(2)}) collective-permute-start(bf16[768,768]{1,0:T(8,128)(2,1)} %u0.5), channel_id=1, source_target_pairs={{0,1},{1,0},{2,3},{3,2},{4,5},{5,4},{6,7},{7,6},{8,9},{9,8},{10,11... | collective-permute-start | bytes 3538952 | tf_op jit(solution)/shard_map/ppermute | solution.py:279
  1.2 8.0 %collective-permute-start.3 = (bf16[768,768]{1,0:T(8,128)(2,1)}, bf16[768,768]{1,0:T(8,128)(2,1)S(1)}, u32[]{:S(2)}, u32[]{:S(2)}) collective-permute-start(bf16[768,768]{1,0:T(8,128)(2,1)} %d0.3), channel_id=1, source_target_pairs={{0,1},{1,0},{2,3},{3,2},{4,5},{5,4},{6,7},{7,6},{8,9},{9,8},{10,11... | collective-permute-start | bytes 3538952 | tf_op jit(solution)/shard_map/ppermute | solution.py:279
  1.7 5.0 %copy-start.6 = (f32[768]{0:T(1024)S(1)}, f32[768]{0:T(1024)}, u32[]{:S(2)}) copy-start(f32[768]{0:T(1024)} %param.10) | copy-start | bytes 9220
  1.7 5.0 %copy-start = (bf16[768,768]{1,0:T(8,128)(2,1)S(1)}, bf16[768,768]{1,0:T(8,128)(2,1)}, u32[]{:S(2)}) copy-start(bf16[768,768]{1,0:T(8,128)(2,1)} %u0.5) | copy-start | bytes 3538948
  1.7 5.5 %collective-permute-start.4 = (bf16[192,128]{1,0:T(8,128)(2,1)S(1)}, bf16[192,128]{1,0:T(8,128)(2,1)S(1)}, u32[]{:S(2)}, u32[]{:S(2)}) collective-permute-start(bf16[192,128]{1,0:T(8,128)(2,1)S(1)} %shard_map.98), channel_id=1, source_target_pairs={{0,2},{1,3},{2,0},{3,1},{4,6},{5,7},{6,4},{7,5},{8,10},{9,11},{10,... | collective-permute-start | bytes 147464 | tf_op jit(solution)/shard_map/ppermute | solution.py:279
  4.6 4.6 %collective-permute-start.5 = (bf16[192,128]{1,0:T(8,128)(2,1)S(1)}, bf16[192,128]{1,0:T(8,128)(2,1)S(1)}, u32[]{:S(2)}, u32[]{:S(2)}) collective-permute-start(bf16[192,128]{1,0:T(8,128)(2,1)S(1)} %get-tuple-element.14), channel_id=1, source_target_pairs={{0,2},{1,3},{2,0},{3,1},{4,6},{5,7},{6,4},{7,5},{8,10},{9,11},{10,... | collective-permute-start | bytes 147464 | tf_op jit(solution)/shard_map/ppermute | solution.py:279
  5.4 5.9 %collective-permute-start.1 = (bf16[384,128]{1,0:T(8,128)(2,1)S(1)}, bf16[384,128]{1,0:T(8,128)(2,1)S(1)}, u32[]{:S(2)}, u32[]{:S(2)}) collective-permute-start(bf16[384,128]{1,0:T(8,128)(2,1)S(1)} %get-tuple-element.12), channel_id=1, source_target_pairs={{0,2},{1,3},{2,0},{3,1},{4,6},{5,7},{6,4},{7,5},{8,10},{9,11},{10,... | collective-permute-start | bytes 294920 | tf_op jit(solution)/shard_map/ppermute | solution.py:279
  6.7 2.5 %copy-start.1 = (bf16[768,768]{1,0:T(8,128)(2,1)S(1)}, bf16[768,768]{1,0:T(8,128)(2,1)}, u32[]{:S(2)}) copy-start(bf16[768,768]{1,0:T(8,128)(2,1)} %d0.3) | copy-start | bytes 3538948
  7.2 4.2 %copy-start.3 = (s32[32]{0:T(128)S(1)}, s32[32]{0:T(128)}, u32[]{:S(2)}) copy-start(s32[32]{0:T(128)} %param.11) | copy-start | bytes 388
  7.2 4.1 %copy-start.4 = (s32[32]{0:T(128)S(1)}, s32[32]{0:T(128)}, u32[]{:S(2)}) copy-start(s32[32]{0:T(128)} %param.12) | copy-start | bytes 388
  7.2 4.1 %copy-start.5 = (s32[8]{0:T(128)S(1)}, s32[8]{0:T(128)}, u32[]{:S(2)}) copy-start(s32[8]{0:T(128)} %param.13) | copy-start | bytes 100
  10.2 5.7 %collective-permute-start.6 = (bf16[128,768]{1,0:T(8,128)(2,1)S(1)}, bf16[128,768]{1,0:T(8,128)(2,1)S(1)}, u32[]{:S(2)}, u32[]{:S(2)}) collective-permute-start(bf16[128,768]{1,0:T(8,128)(2,1)S(1)} %shard_map.99), channel_id=1, source_target_pairs={{0,2},{1,3},{2,0},{3,1},{4,6},{5,7},{6,4},{7,5},{8,10},{9,11},{10,... | collective-permute-start | bytes 589832 | tf_op jit(solution)/shard_map/ppermute | solution.py:279
  28.1 1.5 %collective-permute-start.7 = (bf16[128,896]{1,0:T(8,128)(2,1)S(1)}, bf16[128,896]{1,0:T(8,128)(2,1)S(1)}, u32[]{:S(2)}, u32[]{:S(2)}) collective-permute-start(bf16[128,896]{1,0:T(8,128)(2,1)S(1)} %bitcast.5), channel_id=1, source_target_pairs={{0,1},{1,0},{2,3},{3,2},{4,5},{5,4},{6,7},{7,6},{8,9},{9,8},{10,11... | collective-permute-start | bytes 688136 | tf_op jit(solution)/shard_map/ppermute | solution.py:279

commit v7 on v6

--- a/solution.py
+++ b/solution.py
@@ -86,38 +86,43 @@
     return tokens, total
 
 
-def pair_tokens(near_ref, other_ref, columns, gathered):
-    head = lax.axis_index("heads")
-    share = near_ref.shape[0]
-    gathered[pl.ds(pl.multiple_of(head % 2 * share, 64), share), :] = near_ref[:, columns]
-    gathered[pl.ds(pl.multiple_of((head + 1) % 2 * share, 64), share), :] = other_ref[:, columns]
-    return gathered[...].T
-
-
 def pair_rows(ref, pair):
     count = ref.shape[0] // 2
     return ref[pl.ds(pl.multiple_of(pair * count, 128), count), :]
 
 
+def head_rows(ref, head, share):
+    return ref[pl.ds(pl.multiple_of(head * share, 64), share), :]
+
+
 def early_kernel(hidden_ref, beside_ref, u0, u1, out_ref, gathered):
     head = lax.axis_index("heads")
-    quarter = gathered.shape[1]
-    columns = pl.ds(pl.multiple_of((head ^ 2) * quarter, quarter), quarter)
-    tokens = pair_tokens(hidden_ref, beside_ref, columns, gathered)
+    share, quarter = hidden_ref.shape[0], gathered.shape[1]
+    for source, ref in ((head, hidden_ref), (head ^ 1, beside_ref)):
+        rows = pl.ds(pl.multiple_of(source % 2 * share, 64), share)
+        gathered[rows, :] = quarter_of(ref, head ^ 2, quarter)
+    tokens = gathered[...].T
     for i, up_ref in enumerate((u0, u1)):
         out_ref[i] = jnp.dot(
             tokens, pair_rows(up_ref, head // 2), preferred_element_type=jnp.float32
         )
 
 
-def give_kernel(early_ref, across_ref, diagonal_ref, u0, d0, u1, d1, out_ref, gathered):
-    pair = 1 - lax.axis_index("heads") // 2
-    tokens = pair_tokens(across_ref, diagonal_ref, slice(None), gathered)
+def across_kernel(early_ref, across_ref, u0, u1, out_ref):
+    head = lax.axis_index("heads")
+    tokens = across_ref[...].T
+    for i, up_ref in enumerate((u0, u1)):
+        rows = head_rows(up_ref, head ^ 2, tokens.shape[1])
+        out_ref[i] = early_ref[i] + jnp.dot(tokens, rows, preferred_element_type=jnp.float32)
+
+
+def give_kernel(early_ref, diagonal_ref, u0, d0, u1, d1, out_ref):
+    head = lax.axis_index("heads")
+    tokens = diagonal_ref[...].T
     total = None
     for i, (up_ref, down_ref) in enumerate(((u0, d0), (u1, d1))):
-        upward = early_ref[i] + jnp.dot(
-            tokens, pair_rows(up_ref, pair), preferred_element_type=jnp.float32
-        )
+        rows = head_rows(up_ref, head ^ 3, tokens.shape[1])
+        upward = early_ref[i] + jnp.dot(tokens, rows, preferred_element_type=jnp.float32)
         part = jnp.dot(gelu(upward), down_ref[...], preferred_element_type=jnp.float32)
         part = part.astype(jnp.bfloat16).astype(jnp.float32)
         total = part if total is None else total + part
@@ -163,7 +168,8 @@
     as_float = mixed.astype(jnp.float32)
     centred = as_float - jnp.mean(as_float, axis=1, keepdims=True)
     variance = jnp.mean(centred * centred, axis=1, keepdims=True)
-    weighted = centred * (lax.rsqrt(variance + 1e-05) * weight_ref[:, :1])
+    weight = jnp.concatenate([weight_ref[...]] * (width // LANES), axis=1)
+    weighted = centred * weight * lax.rsqrt(variance + 1e-05)
     pooled = jnp.sum(weighted.reshape(rows, -1, width), axis=1) * gain_ref[...]
     scale = lax.rsqrt(jnp.mean(pooled * pooled, axis=1, keepdims=True) + 1e-05)
     both = jnp.concatenate([pooled * scale, digits_ref[...]], axis=1)
@@ -306,19 +312,18 @@
         flops=8 * quarter * width * units,
         moved=8 * width * units,
     )
-    half = [pltpu.VMEM((width // 2, quarter), jnp.bfloat16)]
+    upward = array(2, quarter, units)
     early = call(
         early_kernel,
-        array(2, quarter, units),
+        upward,
         (hidden, beside, w_up, up_far),
-        scratch=half,
-        flops=0,
-    )
+        scratch=[pltpu.VMEM((width // 2, quarter), jnp.bfloat16)],
+    )
+    early = call(across_kernel, upward, (early, across, w_up, up_far), flops=0)
     given = call(
         give_kernel,
         array(quarter, width, dtype=jnp.bfloat16),
-        (early, across, diagonal, *weights),
-        scratch=half,
+        (early, diagonal, *weights),
         flops=8 * quarter * width * units,
         moved=8 * width * units,
     )

time: 30.8 us -> 30.6 us (level)
    pallas_call x9 -> x10, Pallas kernels: 4.51 us -> 4.59 us  [call(): pl.pallas_call(kernel, out_shape=out_shape, in_specs=[VMEM] * len(operand...]
  transfers between devices with their start and end apart: 8 -> 8, of which waited for: 3 -> 3; matrix products, arithmetic and copies ran while one was open for 0% -> 0% of each run, Pallas kernels for 10% -> 11%
where the time goes in v7:
time: 30.6 us; the launch traced here: 30.4 us
  blocking collectives  11.7 us (38%)
  starting transfers between devices  7.08 us (23%)
  waiting for transfers between devices  6.19 us (20%)
  Pallas kernels  4.59 us (15%)
  between operations  0.79 us (3%)
    all_to_all x1, blocking collectives, local(): lax.all_to_all(jnp.broadcast_to(message[None], (members,) + message.shape...  11.7 us
    ppermute x8, starting transfers between devices, swap(): return lax.ppermute(values, 'heads', [(i, i ^ flip) for i in range(heads)])  7.08 us
    ppermute x8, waiting for transfers between devices, swap(): return lax.ppermute(values, 'heads', [(i, i ^ flip) for i in range(heads)])  6.19 us
    pallas_call x10, Pallas kernels, call(): pl.pallas_call(kernel, out_shape=out_shape, in_specs=[VMEM] * len(operand...  4.59 us
  transfers between devices with their start and end apart: 8, of which 3 were waited for; matrix products, arithmetic and copies ran while one was open for 0% of the time, Pallas kernels for 11%

profile of v7, /device:TPU:0, one launch (start us, length us, event | category | flops | bytes accessed | tf_op | source)
XLA Modules:
  0.0 30.4 jit_solution(593730122294701502)
XLA Ops:
  0.6 0.0 copy-start.2
  0.6 0.5 %collective-permute-start = (bf16[192,512]{1,0:T(8,128)(2,1)}, bf16[192,512]{1,0:T(8,128)(2,1)S(1)}, u32[]{:S(2)}, u32[]{:S(2)}) collective-permute-start(bf16[192,512]{1,0:T(8,128)(2,1)} %bitcast.8), channel_id=1, source_target_pairs={{0,1},{1,0},{2,3},{3,2},{4,5},{5,4},{6,7},{7,6},{8,9},{9,8},{10,11... | collective-permute-start | bytes 589832 | tf_op jit(solution)/shard_map/ppermute | solution.py:285
  1.2 0.1 collective-permute-start.2
  1.2 0.4 %collective-permute-start.3 = (bf16[768,768]{1,0:T(8,128)(2,1)}, bf16[768,768]{1,0:T(8,128)(2,1)S(1)}, u32[]{:S(2)}, u32[]{:S(2)}) collective-permute-start(bf16[768,768]{1,0:T(8,128)(2,1)} %d0.3), channel_id=1, source_target_pairs={{0,1},{1,0},{2,3},{3,2},{4,5},{5,4},{6,7},{7,6},{8,9},{9,8},{10,11... | collective-permute-start | bytes 3538952 | tf_op jit(solution)/shard_map/ppermute | solution.py:285
  1.7 0.0 copy-done.2
  1.7 0.0 copy-start.6
  1.7 0.0 copy-start
  1.7 2.9 %collective-permute-start.4 = (bf16[192,128]{1,0:T(8,128)(2,1)S(1)}, bf16[192,128]{1,0:T(8,128)(2,1)S(1)}, u32[]{:S(2)}, u32[]{:S(2)}) collective-permute-start(bf16[192,128]{1,0:T(8,128)(2,1)S(1)} %shard_map.98), channel_id=1, source_target_pairs={{0,2},{1,3},{2,0},{3,1},{4,6},{5,7},{6,4},{7,5},{8,10},{9,11},{10,... | collective-permute-start | bytes 147464 | tf_op jit(solution)/shard_map/ppermute | solution.py:285
  4.6 0.0 collective-permute-done.beside_ref
  4.6 0.8 %collective-permute-start.5 = (bf16[192,128]{1,0:T(8,128)(2,1)S(1)}, bf16[192,128]{1,0:T(8,128)(2,1)S(1)}, u32[]{:S(2)}, u32[]{:S(2)}) collective-permute-start(bf16[192,128]{1,0:T(8,128)(2,1)S(1)} %get-tuple-element.14), channel_id=1, source_target_pairs={{0,2},{1,3},{2,0},{3,1},{4,6},{5,7},{6,4},{7,5},{8,10},{9,11},{10,... | collective-permute-start | bytes 147464 | tf_op jit(solution)/shard_map/ppermute | solution.py:285
  5.4 1.3 %collective-permute-start.1 = (bf16[384,128]{1,0:T(8,128)(2,1)S(1)}, bf16[384,128]{1,0:T(8,128)(2,1)S(1)}, u32[]{:S(2)}, u32[]{:S(2)}) collective-permute-start(bf16[384,128]{1,0:T(8,128)(2,1)S(1)} %get-tuple-element.12), channel_id=1, source_target_pairs={{0,2},{1,3},{2,0},{3,1},{4,6},{5,7},{6,4},{7,5},{8,10},{9,11},{10,... | collective-permute-start | bytes 294920 | tf_op jit(solution)/shard_map/ppermute | solution.py:285
  6.7 0.0 copy-done.6
  6.7 0.0 collective-permute-done.2.u1
  6.7 0.0 copy-done
  6.7 0.4 %shard_map.97.early_ref = f32[2,128,768]{2,1,0:T(8,128)S(1)} custom-call(bf16[192,512]{1,0:T(8,128)(2,1)S(1)} %bitcast.11, bf16[192,512]{1,0:T(8,128)(2,1)S(1)} %collective-permute-done.beside_ref, bf16[768,768]{1,0:T(8,128)(2,1)S(1)} %copy-done, bf16[768,768]{1,0:T(8,128)(2,1)S(1)} %collective-permute-done.2.u1), custom_call_target="tpu_custom_call" | custom-call | tf_op jit(solution)/shard_map/pallas_call | solution.py:21
  7.2 0.0 copy-start.1
  7.2 0.0 collective-permute-done.4.across_ref
  7.2 0.3 shard_map.99.early_ref
  7.5 0.0 copy-start.3
  7.5 0.0 copy-start.4
  7.5 0.0 copy-start.5
  7.5 1.7 %collective-permute-done.5.diagonal_ref = bf16[192,128]{1,0:T(8,128)(2,1)S(1)} collective-permute-done((bf16[192,128]{1,0:T(8,128)(2,1)S(1)}, bf16[192,128]{1,0:T(8,128)(2,1)S(1)}, u32[]{:S(2)}, u32[]{:S(2)}) %collective-permute-start.5) | collective-permute-done | bytes 49184 | tf_op jit(solution)/shard_map/ppermute | solution.py:285
  9.2 0.0 collective-permute-done.3.d1
  9.2 0.0 copy-done.1
  9.2 0.9 %shard_map.100 = bf16[128,768]{1,0:T(8,128)(2,1)S(1)} custom-call(f32[2,128,768]{2,1,0:T(8,128)S(1)} %shard_map.99.early_ref, bf16[192,128]{1,0:T(8,128)(2,1)S(1)} %collective-permute-done.5.diagonal_ref, bf16[768,768]{1,0:T(8,128)(2,1)S(1)} %copy-done, bf16[768,768]{1,0:T(8,128)(2,1)S(1)} %copy-done.1, bf16[768,768]{1,0:T(8,128)(2,1)S(1)} %collective-permute-done.2.u1, ...), custom_call_target="tpu_custom_call" | custom-call | flops 603979776 | bytes 4718592 | tf_op jit(solution)/shard_map/pallas_call | solution.py:21
  10.1 1.1 %collective-permute-start.6 = (bf16[128,768]{1,0:T(8,128)(2,1)S(1)}, bf16[128,768]{1,0:T(8,128)(2,1)S(1)}, u32[]{:S(2)}, u32[]{:S(2)}) collective-permute-start(bf16[128,768]{1,0:T(8,128)(2,1)S(1)} %shard_map.100), channel_id=1, source_target_pairs={{0,2},{1,3},{2,0},{3,1},{4,6},{5,7},{6,4},{7,5},{8,10},{9,11},{10,... | collective-permute-start | bytes 589832 | tf_op jit(solution)/shard_map/ppermute | solution.py:285
  11.2 0.0 collective-permute-done.1.across_ref
  11.2 0.0 copy-done.3
  11.2 0.0 copy-done.4
  11.2 0.0 copy-done.5
  11.2 1.1 %shard_map.96 = (f32[128,768]{1,0:T(8,128)S(1)}, f32[128,128]{1,0:T(8,128)S(1)}, f32[8,128]{1,0:T(8,128)S(1)}) custom-call(bf16[192,512]{1,0:T(8,128)(2,1)S(1)} %bitcast.12, bf16[192,512]{1,0:T(8,128)(2,1)S(1)} %collective-permute-done.beside_ref, bf16[384,128]{1,0:T(8,128)(2,1)S(1)} %collective-permute-done.1.across_ref, bf16[768,768]{1,0:T(8,128)(2,1)S(1)} %copy-done, ...), custom_call_target="tpu_custom_call" | custom-call | flops 10000000000 | bytes 4718592 | tf_op jit(solution)/shard_map/pallas_call | solution.py:21
  12.3 3.5 %collective-permute-done.6.came_ref = bf16[128,768]{1,0:T(8,128)(2,1)S(1)} collective-permute-done((bf16[128,768]{1,0:T(8,128)(2,1)S(1)}, bf16[128,768]{1,0:T(8,128)(2,1)S(1)}, u32[]{:S(2)}, u32[]{:S(2)}) %collective-permute-start.6) | collective-permute-done | bytes 196640 | tf_op jit(solution)/shard_map/ppermute | solution.py:285
  15.8 0.3 %shard_map.101 = bf16[8,896]{1,0:T(8,128)(2,1)S(1)} custom-call(f32[128,768]{1,0:T(8,128)S(1)} %get-tuple-element.13.kept_ref, bf16[128,768]{1,0:T(8,128)(2,1)S(1)} %collective-permute-done.6.came_ref, f32[128,128]{1,0:T(8,128)S(1)} %get-tuple-element.15.weight_ref, f32[8,128]{1,0:T(8,128)S(1)} %get-tuple-element.16.digits_ref, ...), custom_call_target="tpu_custom_call" | custom-call | tf_op jit(solution)/shard_map/pallas_call | solution.py:21
  16.2 11.7 %all_to_all.5 = bf16[16,8,896]{2,1,0:T(8,128)(2,1)S(1)} all-to-all(bf16[16,8,896]{2,1,0:T(8,128)(2,1)S(1)} %broadcast_in_dim.22), channel_id=1, replica_groups={{30,12,18,0,14,24,2,20,26,8,22,4,10,28,6,16},{31,13,19,1,15,25,3,21,27,..., dimensions={0} | all-to-all | bytes 458752 | tf_op jit(solution)/shard_map/all_to_all | solution.py:353
  27.9 0.0 collective-permute-start.7
  27.9 0.5 %shard_map.102 = (f32[64,768]{1,0:T(8,128)S(1)}, f32[64,192]{1,0:T(8,128)S(1)}, bf16[64,128]{1,0:T(8,128)(2,1)S(1)}, f32[64,128]{1,0:T(8,128)S(1)}) custom-call(bf16[128,896]{1,0:T(8,128)(2,1)S(1)} %bitcast.6), custom_call_target="tpu_custom_call" | custom-call | tf_op jit(solution)/shard_map/pallas_call | solution.py:21
  28.4 1.0 %collective-permute-done.7.far_ref = bf16[128,896]{1,0:T(8,128)(2,1)S(1)} collective-permute-done((bf16[128,896]{1,0:T(8,128)(2,1)S(1)}, bf16[128,896]{1,0:T(8,128)(2,1)S(1)}, u32[]{:S(2)}, u32[]{:S(2)}) %collective-permute-start.7) | collective-permute-done | bytes 229408 | tf_op jit(solution)/shard_map/ppermute | solution.py:285
  29.4 1.0 %shard_map.103 = (bf16[32,768]{1,0:T(8,128)(2,1)}, f32[8,192]{1,0:T(8,128)}, f32[2,192]{1,0:T(2,128)}) custom-call(bf16[128,896]{1,0:T(8,128)(2,1)S(1)} %bitcast.7, bf16[128,896]{1,0:T(8,128)(2,1)S(1)} %collective-permute-done.7.far_ref, f32[64,768]{1,0:T(8,128)S(1)} %get-tuple-element.17.sum_ref, f32[64,192]{1,0:T(8,128)S(1)} %get-tuple-element.18.share_ref, ...), custom_call_target="tpu_custom_call" | custom-call | tf_op jit(solution)/shard_map/pallas_call | solution.py:21
  (5 shorter events, 0.1 us)
Async XLA Ops:
  0.6 1.1 %copy-start.2 = (bf16[512,192]{0,1:T(8,128)(2,1)S(1)}, bf16[512,192]{0,1:T(8,128)(2,1)}, u32[]{:S(2)}) copy-start(bf16[512,192]{0,1:T(8,128)(2,1)} %param.7) | copy-start | bytes 589828
  0.6 4.0 %collective-permute-start = (bf16[192,512]{1,0:T(8,128)(2,1)}, bf16[192,512]{1,0:T(8,128)(2,1)S(1)}, u32[]{:S(2)}, u32[]{:S(2)}) collective-permute-start(bf16[192,512]{1,0:T(8,128)(2,1)} %bitcast.8), channel_id=1, source_target_pairs={{0,1},{1,0},{2,3},{3,2},{4,5},{5,4},{6,7},{7,6},{8,9},{9,8},{10,11... | collective-permute-start | bytes 589832 | tf_op jit(solution)/shard_map/ppermute | solution.py:285
  1.2 5.6 %collective-permute-start.2 = (bf16[768,768]{1,0:T(8,128)(2,1)}, bf16[768,768]{1,0:T(8,128)(2,1)S(1)}, u32[]{:S(2)}, u32[]{:S(2)}) collective-permute-start(bf16[768,768]{1,0:T(8,128)(2,1)} %u0.7), channel_id=1, source_target_pairs={{0,1},{1,0},{2,3},{3,2},{4,5},{5,4},{6,7},{7,6},{8,9},{9,8},{10,11... | collective-permute-start | bytes 3538952 | tf_op jit(solution)/shard_map/ppermute | solution.py:285
  1.2 8.0 %collective-permute-start.3 = (bf16[768,768]{1,0:T(8,128)(2,1)}, bf16[768,768]{1,0:T(8,128)(2,1)S(1)}, u32[]{:S(2)}, u32[]{:S(2)}) collective-permute-start(bf16[768,768]{1,0:T(8,128)(2,1)} %d0.3), channel_id=1, source_target_pairs={{0,1},{1,0},{2,3},{3,2},{4,5},{5,4},{6,7},{7,6},{8,9},{9,8},{10,11... | collective-permute-start | bytes 3538952 | tf_op jit(solution)/shard_map/ppermute | solution.py:285
  1.7 5.0 %copy-start.6 = (f32[768]{0:T(1024)S(1)}, f32[768]{0:T(1024)}, u32[]{:S(2)}) copy-start(f32[768]{0:T(1024)} %param.10) | copy-start | bytes 9220
  1.7 5.0 %copy-start = (bf16[768,768]{1,0:T(8,128)(2,1)S(1)}, bf16[768,768]{1,0:T(8,128)(2,1)}, u32[]{:S(2)}) copy-start(bf16[768,768]{1,0:T(8,128)(2,1)} %u0.7) | copy-start | bytes 3538948
  1.7 5.4 %collective-permute-start.4 = (bf16[192,128]{1,0:T(8,128)(2,1)S(1)}, bf16[192,128]{1,0:T(8,128)(2,1)S(1)}, u32[]{:S(2)}, u32[]{:S(2)}) collective-permute-start(bf16[192,128]{1,0:T(8,128)(2,1)S(1)} %shard_map.98), channel_id=1, source_target_pairs={{0,2},{1,3},{2,0},{3,1},{4,6},{5,7},{6,4},{7,5},{8,10},{9,11},{10,... | collective-permute-start | bytes 147464 | tf_op jit(solution)/shard_map/ppermute | solution.py:285
  4.6 4.6 %collective-permute-start.5 = (bf16[192,128]{1,0:T(8,128)(2,1)S(1)}, bf16[192,128]{1,0:T(8,128)(2,1)S(1)}, u32[]{:S(2)}, u32[]{:S(2)}) collective-permute-start(bf16[192,128]{1,0:T(8,128)(2,1)S(1)} %get-tuple-element.14), channel_id=1, source_target_pairs={{0,2},{1,3},{2,0},{3,1},{4,6},{5,7},{6,4},{7,5},{8,10},{9,11},{10,... | collective-permute-start | bytes 147464 | tf_op jit(solution)/shard_map/ppermute | solution.py:285
  5.4 5.8 %collective-permute-start.1 = (bf16[384,128]{1,0:T(8,128)(2,1)S(1)}, bf16[384,128]{1,0:T(8,128)(2,1)S(1)}, u32[]{:S(2)}, u32[]{:S(2)}) collective-permute-start(bf16[384,128]{1,0:T(8,128)(2,1)S(1)} %get-tuple-element.12), channel_id=1, source_target_pairs={{0,2},{1,3},{2,0},{3,1},{4,6},{5,7},{6,4},{7,5},{8,10},{9,11},{10,... | collective-permute-start | bytes 294920 | tf_op jit(solution)/shard_map/ppermute | solution.py:285
  7.2 2.1 %copy-start.1 = (bf16[768,768]{1,0:T(8,128)(2,1)S(1)}, bf16[768,768]{1,0:T(8,128)(2,1)}, u32[]{:S(2)}) copy-start(bf16[768,768]{1,0:T(8,128)(2,1)} %d0.3) | copy-start | bytes 3538948
  7.5 3.7 %copy-start.3 = (s32[32]{0:T(128)S(1)}, s32[32]{0:T(128)}, u32[]{:S(2)}) copy-start(s32[32]{0:T(128)} %param.11) | copy-start | bytes 388
  7.5 3.7 %copy-start.4 = (s32[32]{0:T(128)S(1)}, s32[32]{0:T(128)}, u32[]{:S(2)}) copy-start(s32[32]{0:T(128)} %param.12) | copy-start | bytes 388
  7.5 3.7 %copy-start.5 = (s32[8]{0:T(128)S(1)}, s32[8]{0:T(128)}, u32[]{:S(2)}) copy-start(s32[8]{0:T(128)} %param.13) | copy-start | bytes 100
  10.1 5.7 %collective-permute-start.6 = (bf16[128,768]{1,0:T(8,128)(2,1)S(1)}, bf16[128,768]{1,0:T(8,128)(2,1)S(1)}, u32[]{:S(2)}, u32[]{:S(2)}) collective-permute-start(bf16[128,768]{1,0:T(8,128)(2,1)S(1)} %shard_map.100), channel_id=1, source_target_pairs={{0,2},{1,3},{2,0},{3,1},{4,6},{5,7},{6,4},{7,5},{8,10},{9,11},{10,... | collective-permute-start | bytes 589832 | tf_op jit(solution)/shard_map/ppermute | solution.py:285
  27.9 1.5 %collective-permute-start.7 = (bf16[128,896]{1,0:T(8,128)(2,1)S(1)}, bf16[128,896]{1,0:T(8,128)(2,1)S(1)}, u32[]{:S(2)}, u32[]{:S(2)}) collective-permute-start(bf16[128,896]{1,0:T(8,128)(2,1)S(1)} %bitcast.5), channel_id=1, source_target_pairs={{0,1},{1,0},{2,3},{3,2},{4,5},{5,4},{6,7},{7,6},{8,9},{9,8},{10,11... | collective-permute-start | bytes 688136 | tf_op jit(solution)/shard_map/ppermute | solution.py:285

commit v8 on v7

--- a/solution.py
+++ b/solution.py
@@ -173,7 +173,9 @@
     pooled = jnp.sum(weighted.reshape(rows, -1, width), axis=1) * gain_ref[...]
     scale = lax.rsqrt(jnp.mean(pooled * pooled, axis=1, keepdims=True) + 1e-05)
     both = jnp.concatenate([pooled * scale, digits_ref[...]], axis=1)
-    out_ref[...] = both.astype(jnp.bfloat16)
+    both = both.astype(jnp.bfloat16)
+    for i in range(out_ref.shape[0]):
+        out_ref[i] = both
 
 
 def pick_share(values, head, heads):
@@ -339,7 +341,7 @@
     )
     message = call(
         embed_kernel,
-        array(rows, width + LANES, dtype=jnp.bfloat16),
+        array(owners * heads // 2, rows, width + LANES, dtype=jnp.bfloat16),
         (kept, came, weight, digits, norm_gain[None, :]),
     )
     groups = [
@@ -351,7 +353,7 @@
     ]
     members = owners * heads // 2
     near = lax.all_to_all(
-        jnp.broadcast_to(message[None], (members,) + message.shape),
+        message,
         ("labels", "heads"),
         split_axis=0,
         concat_axis=0,

time: 30.6 us -> 30.6 us (level)
  no operation moved by 1% of the time
where the time goes in v8:
time: 30.6 us; the launch traced here: 30.4 us
  blocking collectives  11.7 us (38%)
  starting transfers between devices  7.08 us (23%)
  waiting for transfers between devices  6.19 us (20%)
  Pallas kernels  4.6 us (15%)
  between operations  0.79 us (3%)
    all_to_all x1, blocking collectives, local(): lax.all_to_all(message, ('labels', 'heads'), split_axis=0, concat_axis=0,...  11.7 us
    ppermute x8, starting transfers between devices, swap(): return lax.ppermute(values, 'heads', [(i, i ^ flip) for i in range(heads)])  7.08 us
    ppermute x8, waiting for transfers between devices, swap(): return lax.ppermute(values, 'heads', [(i, i ^ flip) for i in range(heads)])  6.19 us
    pallas_call x10, Pallas kernels, call(): pl.pallas_call(kernel, out_shape=out_shape, in_specs=[VMEM] * len(operand...  4.6 us
  transfers between devices with their start and end apart: 8, of which 3 were waited for; matrix products, arithmetic and copies ran while one was open for 0% of the time, Pallas kernels for 11%

profile of v8, /device:TPU:0, one launch (start us, length us, event | category | flops | bytes accessed | tf_op | source)
XLA Modules:
  0.0 30.4 jit_solution(3143710110986292775)
XLA Ops:
  0.6 0.0 copy-start.2
  0.6 0.5 %collective-permute-start = (bf16[192,512]{1,0:T(8,128)(2,1)}, bf16[192,512]{1,0:T(8,128)(2,1)S(1)}, u32[]{:S(2)}, u32[]{:S(2)}) collective-permute-start(bf16[192,512]{1,0:T(8,128)(2,1)} %bitcast.8), channel_id=1, source_target_pairs={{0,1},{1,0},{2,3},{3,2},{4,5},{5,4},{6,7},{7,6},{8,9},{9,8},{10,11... | collective-permute-start | bytes 589832 | tf_op jit(solution)/shard_map/ppermute | solution.py:287
  1.2 0.1 collective-permute-start.2
  1.2 0.4 %collective-permute-start.3 = (bf16[768,768]{1,0:T(8,128)(2,1)}, bf16[768,768]{1,0:T(8,128)(2,1)S(1)}, u32[]{:S(2)}, u32[]{:S(2)}) collective-permute-start(bf16[768,768]{1,0:T(8,128)(2,1)} %d0.3), channel_id=1, source_target_pairs={{0,1},{1,0},{2,3},{3,2},{4,5},{5,4},{6,7},{7,6},{8,9},{9,8},{10,11... | collective-permute-start | bytes 3538952 | tf_op jit(solution)/shard_map/ppermute | solution.py:287
  1.7 0.0 copy-done.2
  1.7 0.0 copy-start.6
  1.7 0.0 copy-start
  1.7 2.9 %collective-permute-start.4 = (bf16[192,128]{1,0:T(8,128)(2,1)S(1)}, bf16[192,128]{1,0:T(8,128)(2,1)S(1)}, u32[]{:S(2)}, u32[]{:S(2)}) collective-permute-start(bf16[192,128]{1,0:T(8,128)(2,1)S(1)} %shard_map.98), channel_id=1, source_target_pairs={{0,2},{1,3},{2,0},{3,1},{4,6},{5,7},{6,4},{7,5},{8,10},{9,11},{10,... | collective-permute-start | bytes 147464 | tf_op jit(solution)/shard_map/ppermute | solution.py:287
  4.6 0.0 collective-permute-done.beside_ref
  4.6 0.8 %collective-permute-start.5 = (bf16[192,128]{1,0:T(8,128)(2,1)S(1)}, bf16[192,128]{1,0:T(8,128)(2,1)S(1)}, u32[]{:S(2)}, u32[]{:S(2)}) collective-permute-start(bf16[192,128]{1,0:T(8,128)(2,1)S(1)} %get-tuple-element.14), channel_id=1, source_target_pairs={{0,2},{1,3},{2,0},{3,1},{4,6},{5,7},{6,4},{7,5},{8,10},{9,11},{10,... | collective-permute-start | bytes 147464 | tf_op jit(solution)/shard_map/ppermute | solution.py:287
  5.4 1.3 %collective-permute-start.1 = (bf16[384,128]{1,0:T(8,128)(2,1)S(1)}, bf16[384,128]{1,0:T(8,128)(2,1)S(1)}, u32[]{:S(2)}, u32[]{:S(2)}) collective-permute-start(bf16[384,128]{1,0:T(8,128)(2,1)S(1)} %get-tuple-element.12), channel_id=1, source_target_pairs={{0,2},{1,3},{2,0},{3,1},{4,6},{5,7},{6,4},{7,5},{8,10},{9,11},{10,... | collective-permute-start | bytes 294920 | tf_op jit(solution)/shard_map/ppermute | solution.py:287
  6.7 0.0 copy-done.6
  6.7 0.0 collective-permute-done.2.u1
  6.7 0.0 copy-done
  6.7 0.4 %shard_map.97.early_ref = f32[2,128,768]{2,1,0:T(8,128)S(1)} custom-call(bf16[192,512]{1,0:T(8,128)(2,1)S(1)} %bitcast.11, bf16[192,512]{1,0:T(8,128)(2,1)S(1)} %collective-permute-done.beside_ref, bf16[768,768]{1,0:T(8,128)(2,1)S(1)} %copy-done, bf16[768,768]{1,0:T(8,128)(2,1)S(1)} %collective-permute-done.2.u1), custom_call_target="tpu_custom_call" | custom-call | tf_op jit(solution)/shard_map/pallas_call | solution.py:21
  7.2 0.0 copy-start.1
  7.2 0.0 collective-permute-done.4.across_ref
  7.2 0.3 shard_map.99.early_ref
  7.5 0.0 copy-start.3
  7.5 0.0 copy-start.4
  7.5 0.0 copy-start.5
  7.5 1.7 %collective-permute-done.5.diagonal_ref = bf16[192,128]{1,0:T(8,128)(2,1)S(1)} collective-permute-done((bf16[192,128]{1,0:T(8,128)(2,1)S(1)}, bf16[192,128]{1,0:T(8,128)(2,1)S(1)}, u32[]{:S(2)}, u32[]{:S(2)}) %collective-permute-start.5) | collective-permute-done | bytes 49184 | tf_op jit(solution)/shard_map/ppermute | solution.py:287
  9.2 0.0 collective-permute-done.3.d1
  9.2 0.0 copy-done.1
  9.2 0.9 %shard_map.100 = bf16[128,768]{1,0:T(8,128)(2,1)S(1)} custom-call(f32[2,128,768]{2,1,0:T(8,128)S(1)} %shard_map.99.early_ref, bf16[192,128]{1,0:T(8,128)(2,1)S(1)} %collective-permute-done.5.diagonal_ref, bf16[768,768]{1,0:T(8,128)(2,1)S(1)} %copy-done, bf16[768,768]{1,0:T(8,128)(2,1)S(1)} %copy-done.1, bf16[768,768]{1,0:T(8,128)(2,1)S(1)} %collective-permute-done.2.u1, ...), custom_call_target="tpu_custom_call" | custom-call | flops 603979776 | bytes 4718592 | tf_op jit(solution)/shard_map/pallas_call | solution.py:21
  10.1 1.1 %collective-permute-start.6 = (bf16[128,768]{1,0:T(8,128)(2,1)S(1)}, bf16[128,768]{1,0:T(8,128)(2,1)S(1)}, u32[]{:S(2)}, u32[]{:S(2)}) collective-permute-start(bf16[128,768]{1,0:T(8,128)(2,1)S(1)} %shard_map.100), channel_id=1, source_target_pairs={{0,2},{1,3},{2,0},{3,1},{4,6},{5,7},{6,4},{7,5},{8,10},{9,11},{10,... | collective-permute-start | bytes 589832 | tf_op jit(solution)/shard_map/ppermute | solution.py:287
  11.2 0.0 collective-permute-done.1.across_ref
  11.2 0.0 copy-done.3
  11.2 0.0 copy-done.4
  11.2 0.0 copy-done.5
  11.2 1.1 %shard_map.96 = (f32[128,768]{1,0:T(8,128)S(1)}, f32[128,128]{1,0:T(8,128)S(1)}, f32[8,128]{1,0:T(8,128)S(1)}) custom-call(bf16[192,512]{1,0:T(8,128)(2,1)S(1)} %bitcast.12, bf16[192,512]{1,0:T(8,128)(2,1)S(1)} %collective-permute-done.beside_ref, bf16[384,128]{1,0:T(8,128)(2,1)S(1)} %collective-permute-done.1.across_ref, bf16[768,768]{1,0:T(8,128)(2,1)S(1)} %copy-done, ...), custom_call_target="tpu_custom_call" | custom-call | flops 10000000000 | bytes 4718592 | tf_op jit(solution)/shard_map/pallas_call | solution.py:21
  12.3 3.5 %collective-permute-done.6.came_ref = bf16[128,768]{1,0:T(8,128)(2,1)S(1)} collective-permute-done((bf16[128,768]{1,0:T(8,128)(2,1)S(1)}, bf16[128,768]{1,0:T(8,128)(2,1)S(1)}, u32[]{:S(2)}, u32[]{:S(2)}) %collective-permute-start.6) | collective-permute-done | bytes 196640 | tf_op jit(solution)/shard_map/ppermute | solution.py:287
  15.8 0.4 %shard_map.101 = bf16[16,8,896]{2,1,0:T(8,128)(2,1)S(1)} custom-call(f32[128,768]{1,0:T(8,128)S(1)} %get-tuple-element.13.kept_ref, bf16[128,768]{1,0:T(8,128)(2,1)S(1)} %collective-permute-done.6.came_ref, f32[128,128]{1,0:T(8,128)S(1)} %get-tuple-element.15.weight_ref, f32[8,128]{1,0:T(8,128)S(1)} %get-tuple-element.16.digits_ref, ...), custom_call_target="tpu_custom_call" | custom-call | tf_op jit(solution)/shard_map/pallas_call | solution.py:21
  16.2 11.7 %all_to_all.5 = bf16[16,8,896]{2,1,0:T(8,128)(2,1)S(1)} all-to-all(bf16[16,8,896]{2,1,0:T(8,128)(2,1)S(1)} %shard_map.101), channel_id=1, replica_groups={{30,12,18,0,14,24,2,20,26,8,22,4,10,28,6,16},{31,13,19,1,15,25,3,21,27,..., dimensions={0} | all-to-all | bytes 458752 | tf_op jit(solution)/shard_map/all_to_all | solution.py:355
  27.9 0.0 collective-permute-start.7
  27.9 0.5 %shard_map.102 = (f32[64,768]{1,0:T(8,128)S(1)}, f32[64,192]{1,0:T(8,128)S(1)}, bf16[64,128]{1,0:T(8,128)(2,1)S(1)}, f32[64,128]{1,0:T(8,128)S(1)}) custom-call(bf16[128,896]{1,0:T(8,128)(2,1)S(1)} %bitcast.6), custom_call_target="tpu_custom_call" | custom-call | tf_op jit(solution)/shard_map/pallas_call | solution.py:21
  28.4 1.0 %collective-permute-done.7.far_ref = bf16[128,896]{1,0:T(8,128)(2,1)S(1)} collective-permute-done((bf16[128,896]{1,0:T(8,128)(2,1)S(1)}, bf16[128,896]{1,0:T(8,128)(2,1)S(1)}, u32[]{:S(2)}, u32[]{:S(2)}) %collective-permute-start.7) | collective-permute-done | bytes 229408 | tf_op jit(solution)/shard_map/ppermute | solution.py:287
  29.4 1.0 %shard_map.103 = (bf16[32,768]{1,0:T(8,128)(2,1)}, f32[8,192]{1,0:T(8,128)}, f32[2,192]{1,0:T(2,128)}) custom-call(bf16[128,896]{1,0:T(8,128)(2,1)S(1)} %bitcast.7, bf16[128,896]{1,0:T(8,128)(2,1)S(1)} %collective-permute-done.7.far_ref, f32[64,768]{1,0:T(8,128)S(1)} %get-tuple-element.17.sum_ref, f32[64,192]{1,0:T(8,128)S(1)} %get-tuple-element.18.share_ref, ...), custom_call_target="tpu_custom_call" | custom-call | tf_op jit(solution)/shard_map/pallas_call | solution.py:21
  (4 shorter events, 0.1 us)
Async XLA Ops:
  0.6 1.1 %copy-start.2 = (bf16[512,192]{0,1:T(8,128)(2,1)S(1)}, bf16[512,192]{0,1:T(8,128)(2,1)}, u32[]{:S(2)}) copy-start(bf16[512,192]{0,1:T(8,128)(2,1)} %param.7) | copy-start | bytes 589828
  0.6 4.0 %collective-permute-start = (bf16[192,512]{1,0:T(8,128)(2,1)}, bf16[192,512]{1,0:T(8,128)(2,1)S(1)}, u32[]{:S(2)}, u32[]{:S(2)}) collective-permute-start(bf16[192,512]{1,0:T(8,128)(2,1)} %bitcast.8), channel_id=1, source_target_pairs={{0,1},{1,0},{2,3},{3,2},{4,5},{5,4},{6,7},{7,6},{8,9},{9,8},{10,11... | collective-permute-start | bytes 589832 | tf_op jit(solution)/shard_map/ppermute | solution.py:287
  1.2 5.6 %collective-permute-start.2 = (bf16[768,768]{1,0:T(8,128)(2,1)}, bf16[768,768]{1,0:T(8,128)(2,1)S(1)}, u32[]{:S(2)}, u32[]{:S(2)}) collective-permute-start(bf16[768,768]{1,0:T(8,128)(2,1)} %u0.7), channel_id=1, source_target_pairs={{0,1},{1,0},{2,3},{3,2},{4,5},{5,4},{6,7},{7,6},{8,9},{9,8},{10,11... | collective-permute-start | bytes 3538952 | tf_op jit(solution)/shard_map/ppermute | solution.py:287
  1.2 8.0 %collective-permute-start.3 = (bf16[768,768]{1,0:T(8,128)(2,1)}, bf16[768,768]{1,0:T(8,128)(2,1)S(1)}, u32[]{:S(2)}, u32[]{:S(2)}) collective-permute-start(bf16[768,768]{1,0:T(8,128)(2,1)} %d0.3), channel_id=1, source_target_pairs={{0,1},{1,0},{2,3},{3,2},{4,5},{5,4},{6,7},{7,6},{8,9},{9,8},{10,11... | collective-permute-start | bytes 3538952 | tf_op jit(solution)/shard_map/ppermute | solution.py:287
  1.7 5.0 %copy-start.6 = (f32[768]{0:T(1024)S(1)}, f32[768]{0:T(1024)}, u32[]{:S(2)}) copy-start(f32[768]{0:T(1024)} %param.10) | copy-start | bytes 9220
  1.7 5.0 %copy-start = (bf16[768,768]{1,0:T(8,128)(2,1)S(1)}, bf16[768,768]{1,0:T(8,128)(2,1)}, u32[]{:S(2)}) copy-start(bf16[768,768]{1,0:T(8,128)(2,1)} %u0.7) | copy-start | bytes 3538948
  1.7 5.4 %collective-permute-start.4 = (bf16[192,128]{1,0:T(8,128)(2,1)S(1)}, bf16[192,128]{1,0:T(8,128)(2,1)S(1)}, u32[]{:S(2)}, u32[]{:S(2)}) collective-permute-start(bf16[192,128]{1,0:T(8,128)(2,1)S(1)} %shard_map.98), channel_id=1, source_target_pairs={{0,2},{1,3},{2,0},{3,1},{4,6},{5,7},{6,4},{7,5},{8,10},{9,11},{10,... | collective-permute-start | bytes 147464 | tf_op jit(solution)/shard_map/ppermute | solution.py:287
  4.6 4.6 %collective-permute-start.5 = (bf16[192,128]{1,0:T(8,128)(2,1)S(1)}, bf16[192,128]{1,0:T(8,128)(2,1)S(1)}, u32[]{:S(2)}, u32[]{:S(2)}) collective-permute-start(bf16[192,128]{1,0:T(8,128)(2,1)S(1)} %get-tuple-element.14), channel_id=1, source_target_pairs={{0,2},{1,3},{2,0},{3,1},{4,6},{5,7},{6,4},{7,5},{8,10},{9,11},{10,... | collective-permute-start | bytes 147464 | tf_op jit(solution)/shard_map/ppermute | solution.py:287
  5.4 5.8 %collective-permute-start.1 = (bf16[384,128]{1,0:T(8,128)(2,1)S(1)}, bf16[384,128]{1,0:T(8,128)(2,1)S(1)}, u32[]{:S(2)}, u32[]{:S(2)}) collective-permute-start(bf16[384,128]{1,0:T(8,128)(2,1)S(1)} %get-tuple-element.12), channel_id=1, source_target_pairs={{0,2},{1,3},{2,0},{3,1},{4,6},{5,7},{6,4},{7,5},{8,10},{9,11},{10,... | collective-permute-start | bytes 294920 | tf_op jit(solution)/shard_map/ppermute | solution.py:287
  7.2 2.1 %copy-start.1 = (bf16[768,768]{1,0:T(8,128)(2,1)S(1)}, bf16[768,768]{1,0:T(8,128)(2,1)}, u32[]{:S(2)}) copy-start(bf16[768,768]{1,0:T(8,128)(2,1)} %d0.3) | copy-start | bytes 3538948
  7.5 3.7 %copy-start.3 = (s32[32]{0:T(128)S(1)}, s32[32]{0:T(128)}, u32[]{:S(2)}) copy-start(s32[32]{0:T(128)} %param.11) | copy-start | bytes 388
  7.5 3.7 %copy-start.4 = (s32[32]{0:T(128)S(1)}, s32[32]{0:T(128)}, u32[]{:S(2)}) copy-start(s32[32]{0:T(128)} %param.12) | copy-start | bytes 388
  7.5 3.7 %copy-start.5 = (s32[8]{0:T(128)S(1)}, s32[8]{0:T(128)}, u32[]{:S(2)}) copy-start(s32[8]{0:T(128)} %param.13) | copy-start | bytes 100
  10.1 5.7 %collective-permute-start.6 = (bf16[128,768]{1,0:T(8,128)(2,1)S(1)}, bf16[128,768]{1,0:T(8,128)(2,1)S(1)}, u32[]{:S(2)}, u32[]{:S(2)}) collective-permute-start(bf16[128,768]{1,0:T(8,128)(2,1)S(1)} %shard_map.100), channel_id=1, source_target_pairs={{0,2},{1,3},{2,0},{3,1},{4,6},{5,7},{6,4},{7,5},{8,10},{9,11},{10,... | collective-permute-start | bytes 589832 | tf_op jit(solution)/shard_map/ppermute | solution.py:287
  27.9 1.5 %collective-permute-start.7 = (bf16[128,896]{1,0:T(8,128)(2,1)S(1)}, bf16[128,896]{1,0:T(8,128)(2,1)S(1)}, u32[]{:S(2)}, u32[]{:S(2)}) collective-permute-start(bf16[128,896]{1,0:T(8,128)(2,1)S(1)} %bitcast.5), channel_id=1, source_target_pairs={{0,1},{1,0},{2,3},{3,2},{4,5},{5,4},{6,7},{7,6},{8,9},{9,8},{10,11... | collective-permute-start | bytes 688136 | tf_op jit(solution)/shard_map/ppermute | solution.py:287

commit v9 on v8

--- a/solution.py
+++ b/solution.py
@@ -203,7 +203,14 @@
     return 2 * (half - 1 - place + (1 - odd) * half) + odd
 
 
-def near_kernel(heads, leaf_count, near_ref, sum_ref, share_ref, picker_ref, parent_ref):
+def own_rows(ref, position, half, rows, width):
+    pair = pl.ds(pl.multiple_of(position // 2 * 2 * rows, 2 * rows), 2 * rows)
+    return ref[pair, :width].astype(jnp.float32)[half * rows : (half + 1) * rows]
+
+
+def near_kernel(
+    heads, leaf_count, near_ref, sum_ref, share_ref, picker_ref, parent_ref, own_ref
+):
     leaves, width = sum_ref.shape
     count = near_ref.shape[0]
     owners = leaves // leaf_count
@@ -223,10 +230,14 @@
     digits = digits.reshape(owners, count // owners, LANES)[:, :leaf_count].reshape(leaves, LANES)
     parent = digits[:, 2:3] + BASE * digits[:, 3:4]
     parent_ref[...] = jnp.broadcast_to(parent, parent_ref.shape)
+    rows = own_ref.shape[0] // 2
+    for i in range(2):
+        position = position_of(owners, lax.axis_index("labels"), 1 - i)
+        own_ref[i * rows : (i + 1) * rows, :] = own_rows(near_ref, position, 1 - i, rows, width)
 
 
 def leaf_kernel(
-    heads, near_ref, far_ref, sum_ref, share_ref, picker_ref, parent_ref,
+    heads, far_ref, sum_ref, share_ref, picker_ref, parent_ref, own_ref,
     embed_out, centers_out, parents_out, embed_ref, centers_ref, parents_ref, scratch, sems,
 ):
     head, index = lax.axis_index("heads"), lax.axis_index("labels")
@@ -237,13 +248,10 @@
     owners = sum_ref.shape[0] // leaf_count
     upper, lower = position_of(owners, index, 0), position_of(owners, index, 1)
 
-    def own_rows(ref, position, half):
-        pair = pl.ds(pl.multiple_of(position // 2 * 2 * rows, 2 * rows), 2 * rows)
-        return ref[pair, :width].astype(jnp.float32)[half * rows : (half + 1) * rows]
-
     blocks = []
-    for position, half in ((lower, 1), (upper, 0)):
-        near, far = own_rows(near_ref, position, half), own_rows(far_ref, position, half)
+    for i, position in enumerate((lower, upper)):
+        near = own_ref[i * rows : (i + 1) * rows, :]
+        far = own_rows(far_ref, position, 1 - i, rows, width)
         blocks += [jnp.where(core == 0, near, far), jnp.where(core == 0, far, near)]
     embed_ref[...] = jnp.concatenate(blocks, axis=0).astype(jnp.bfloat16)
     embed_copy = pltpu.make_async_copy(embed_ref, embed_out, sems.at[0])
@@ -369,6 +377,7 @@
             array(leaves, share),
             array(leaves, members * rows, dtype=jnp.bfloat16),
             array(leaves, LANES),
+            array(2 * rows, width),
         ),
         (near,),
     )
@@ -380,7 +389,7 @@
     return call(
         functools.partial(leaf_kernel, heads),
         outputs,
-        (near, far, *ready),
+        (far, *ready),
         out_spec=HBM,
         scratch=[pltpu.VMEM(out.shape, out.dtype) for out in outputs]
         + [pltpu.VMEM((leaves, share), jnp.float32), pltpu.SemaphoreType.DMA((3,))],

time: 30.6 us -> 30.6 us (level)
  no operation moved by 1% of the time
where the time goes in v9:
time: 30.6 us; the launch traced here: 30.4 us
  blocking collectives  11.7 us (38%)
  starting transfers between devices  7.08 us (23%)
  waiting for transfers between devices  6.19 us (20%)
  Pallas kernels  4.6 us (15%)
  between operations  0.79 us (3%)
    all_to_all x1, blocking collectives, local(): lax.all_to_all(message, ('labels', 'heads'), split_axis=0, concat_axis=0,...  11.7 us
    ppermute x8, starting transfers between devices, swap(): return lax.ppermute(values, 'heads', [(i, i ^ flip) for i in range(heads)])  7.08 us
    ppermute x8, waiting for transfers between devices, swap(): return lax.ppermute(values, 'heads', [(i, i ^ flip) for i in range(heads)])  6.19 us
    pallas_call x10, Pallas kernels, call(): pl.pallas_call(kernel, out_shape=out_shape, in_specs=[VMEM] * len(operand...  4.6 us
  transfers between devices with their start and end apart: 8, of which 3 were waited for; matrix products, arithmetic and copies ran while one was open for 0% of the time, Pallas kernels for 11%

profile of v9, /device:TPU:0, one launch (start us, length us, event | category | flops | bytes accessed | tf_op | source)
XLA Modules:
  0.0 30.4 jit_solution(18371287488023569321)
XLA Ops:
  0.6 0.0 copy-start.2
  0.6 0.5 %collective-permute-start = (bf16[192,512]{1,0:T(8,128)(2,1)}, bf16[192,512]{1,0:T(8,128)(2,1)S(1)}, u32[]{:S(2)}, u32[]{:S(2)}) collective-permute-start(bf16[192,512]{1,0:T(8,128)(2,1)} %bitcast.7), channel_id=1, source_target_pairs={{0,1},{1,0},{2,3},{3,2},{4,5},{5,4},{6,7},{7,6},{8,9},{9,8},{10,11... | collective-permute-start | bytes 589832 | tf_op jit(solution)/shard_map/ppermute | solution.py:295
  1.2 0.1 collective-permute-start.2
  1.2 0.4 %collective-permute-start.3 = (bf16[768,768]{1,0:T(8,128)(2,1)}, bf16[768,768]{1,0:T(8,128)(2,1)S(1)}, u32[]{:S(2)}, u32[]{:S(2)}) collective-permute-start(bf16[768,768]{1,0:T(8,128)(2,1)} %d0.3), channel_id=1, source_target_pairs={{0,1},{1,0},{2,3},{3,2},{4,5},{5,4},{6,7},{7,6},{8,9},{9,8},{10,11... | collective-permute-start | bytes 3538952 | tf_op jit(solution)/shard_map/ppermute | solution.py:295
  1.7 0.0 copy-done.2
  1.7 0.0 copy-start.6
  1.7 0.0 copy-start
  1.7 2.9 %collective-permute-start.4 = (bf16[192,128]{1,0:T(8,128)(2,1)S(1)}, bf16[192,128]{1,0:T(8,128)(2,1)S(1)}, u32[]{:S(2)}, u32[]{:S(2)}) collective-permute-start(bf16[192,128]{1,0:T(8,128)(2,1)S(1)} %shard_map.98), channel_id=1, source_target_pairs={{0,2},{1,3},{2,0},{3,1},{4,6},{5,7},{6,4},{7,5},{8,10},{9,11},{10,... | collective-permute-start | bytes 147464 | tf_op jit(solution)/shard_map/ppermute | solution.py:295
  4.6 0.0 collective-permute-done.beside_ref
  4.6 0.8 %collective-permute-start.5 = (bf16[192,128]{1,0:T(8,128)(2,1)S(1)}, bf16[192,128]{1,0:T(8,128)(2,1)S(1)}, u32[]{:S(2)}, u32[]{:S(2)}) collective-permute-start(bf16[192,128]{1,0:T(8,128)(2,1)S(1)} %get-tuple-element.15), channel_id=1, source_target_pairs={{0,2},{1,3},{2,0},{3,1},{4,6},{5,7},{6,4},{7,5},{8,10},{9,11},{10,... | collective-permute-start | bytes 147464 | tf_op jit(solution)/shard_map/ppermute | solution.py:295
  5.4 1.3 %collective-permute-start.1 = (bf16[384,128]{1,0:T(8,128)(2,1)S(1)}, bf16[384,128]{1,0:T(8,128)(2,1)S(1)}, u32[]{:S(2)}, u32[]{:S(2)}) collective-permute-start(bf16[384,128]{1,0:T(8,128)(2,1)S(1)} %get-tuple-element.13), channel_id=1, source_target_pairs={{0,2},{1,3},{2,0},{3,1},{4,6},{5,7},{6,4},{7,5},{8,10},{9,11},{10,... | collective-permute-start | bytes 294920 | tf_op jit(solution)/shard_map/ppermute | solution.py:295
  6.7 0.0 copy-done.6
  6.7 0.0 collective-permute-done.2.u1
  6.7 0.0 copy-done
  6.7 0.4 %shard_map.97.early_ref = f32[2,128,768]{2,1,0:T(8,128)S(1)} custom-call(bf16[192,512]{1,0:T(8,128)(2,1)S(1)} %bitcast.10, bf16[192,512]{1,0:T(8,128)(2,1)S(1)} %collective-permute-done.beside_ref, bf16[768,768]{1,0:T(8,128)(2,1)S(1)} %copy-done, bf16[768,768]{1,0:T(8,128)(2,1)S(1)} %collective-permute-done.2.u1), custom_call_target="tpu_custom_call" | custom-call | tf_op jit(solution)/shard_map/pallas_call | solution.py:21
  7.2 0.0 copy-start.1
  7.2 0.0 collective-permute-done.4.across_ref
  7.2 0.3 shard_map.99.early_ref
  7.5 0.0 copy-start.3
  7.5 0.0 copy-start.4
  7.5 0.0 copy-start.5
  7.5 1.7 %collective-permute-done.5.diagonal_ref = bf16[192,128]{1,0:T(8,128)(2,1)S(1)} collective-permute-done((bf16[192,128]{1,0:T(8,128)(2,1)S(1)}, bf16[192,128]{1,0:T(8,128)(2,1)S(1)}, u32[]{:S(2)}, u32[]{:S(2)}) %collective-permute-start.5) | collective-permute-done | bytes 49184 | tf_op jit(solution)/shard_map/ppermute | solution.py:295
  9.2 0.0 collective-permute-done.3.d1
  9.2 0.0 copy-done.1
  9.2 0.9 %shard_map.100 = bf16[128,768]{1,0:T(8,128)(2,1)S(1)} custom-call(f32[2,128,768]{2,1,0:T(8,128)S(1)} %shard_map.99.early_ref, bf16[192,128]{1,0:T(8,128)(2,1)S(1)} %collective-permute-done.5.diagonal_ref, bf16[768,768]{1,0:T(8,128)(2,1)S(1)} %copy-done, bf16[768,768]{1,0:T(8,128)(2,1)S(1)} %copy-done.1, bf16[768,768]{1,0:T(8,128)(2,1)S(1)} %collective-permute-done.2.u1, ...), custom_call_target="tpu_custom_call" | custom-call | flops 603979776 | bytes 4718592 | tf_op jit(solution)/shard_map/pallas_call | solution.py:21
  10.1 1.1 %collective-permute-start.6 = (bf16[128,768]{1,0:T(8,128)(2,1)S(1)}, bf16[128,768]{1,0:T(8,128)(2,1)S(1)}, u32[]{:S(2)}, u32[]{:S(2)}) collective-permute-start(bf16[128,768]{1,0:T(8,128)(2,1)S(1)} %shard_map.100), channel_id=1, source_target_pairs={{0,2},{1,3},{2,0},{3,1},{4,6},{5,7},{6,4},{7,5},{8,10},{9,11},{10,... | collective-permute-start | bytes 589832 | tf_op jit(solution)/shard_map/ppermute | solution.py:295
  11.2 0.0 collective-permute-done.1.across_ref
  11.2 0.0 copy-done.3
  11.2 0.0 copy-done.4
  11.2 0.0 copy-done.5
  11.2 1.1 %shard_map.96 = (f32[128,768]{1,0:T(8,128)S(1)}, f32[128,128]{1,0:T(8,128)S(1)}, f32[8,128]{1,0:T(8,128)S(1)}) custom-call(bf16[192,512]{1,0:T(8,128)(2,1)S(1)} %bitcast.11, bf16[192,512]{1,0:T(8,128)(2,1)S(1)} %collective-permute-done.beside_ref, bf16[384,128]{1,0:T(8,128)(2,1)S(1)} %collective-permute-done.1.across_ref, bf16[768,768]{1,0:T(8,128)(2,1)S(1)} %copy-done, ...), custom_call_target="tpu_custom_call" | custom-call | flops 10000000000 | bytes 4718592 | tf_op jit(solution)/shard_map/pallas_call | solution.py:21
  12.3 3.5 %collective-permute-done.6.came_ref = bf16[128,768]{1,0:T(8,128)(2,1)S(1)} collective-permute-done((bf16[128,768]{1,0:T(8,128)(2,1)S(1)}, bf16[128,768]{1,0:T(8,128)(2,1)S(1)}, u32[]{:S(2)}, u32[]{:S(2)}) %collective-permute-start.6) | collective-permute-done | bytes 196640 | tf_op jit(solution)/shard_map/ppermute | solution.py:295
  15.8 0.4 %shard_map.101 = bf16[16,8,896]{2,1,0:T(8,128)(2,1)S(1)} custom-call(f32[128,768]{1,0:T(8,128)S(1)} %get-tuple-element.14.kept_ref, bf16[128,768]{1,0:T(8,128)(2,1)S(1)} %collective-permute-done.6.came_ref, f32[128,128]{1,0:T(8,128)S(1)} %get-tuple-element.16.weight_ref, f32[8,128]{1,0:T(8,128)S(1)} %get-tuple-element.17.digits_ref, ...), custom_call_target="tpu_custom_call" | custom-call | tf_op jit(solution)/shard_map/pallas_call | solution.py:21
  16.2 11.7 %all_to_all.5 = bf16[16,8,896]{2,1,0:T(8,128)(2,1)S(1)} all-to-all(bf16[16,8,896]{2,1,0:T(8,128)(2,1)S(1)} %shard_map.101), channel_id=1, replica_groups={{30,12,18,0,14,24,2,20,26,8,22,4,10,28,6,16},{31,13,19,1,15,25,3,21,27,..., dimensions={0} | all-to-all | bytes 458752 | tf_op jit(solution)/shard_map/all_to_all | solution.py:363
  27.9 0.0 collective-permute-start.7
  27.9 0.5 %shard_map.102 = (f32[64,768]{1,0:T(8,128)S(1)}, f32[64,192]{1,0:T(8,128)S(1)}, bf16[64,128]{1,0:T(8,128)(2,1)S(1)}, f32[64,128]{1,0:T(8,128)S(1)}, f32[16,768]{1,0:T(8,128)S(1)}) custom-call(bf16[128,896]{1,0:T(8,128)(2,1)S(1)} %bitcast.6), custom_call_target="tpu_custom_call" | custom-call | tf_op jit(solution)/shard_map/pallas_call | solution.py:21
  28.4 1.0 %collective-permute-done.7.far_ref = bf16[128,896]{1,0:T(8,128)(2,1)S(1)} collective-permute-done((bf16[128,896]{1,0:T(8,128)(2,1)S(1)}, bf16[128,896]{1,0:T(8,128)(2,1)S(1)}, u32[]{:S(2)}, u32[]{:S(2)}) %collective-permute-start.7) | collective-permute-done | bytes 229408 | tf_op jit(solution)/shard_map/ppermute | solution.py:295
  29.4 1.0 %shard_map.103 = (bf16[32,768]{1,0:T(8,128)(2,1)}, f32[8,192]{1,0:T(8,128)}, f32[2,192]{1,0:T(2,128)}) custom-call(bf16[128,896]{1,0:T(8,128)(2,1)S(1)} %collective-permute-done.7.far_ref, f32[64,768]{1,0:T(8,128)S(1)} %get-tuple-element.18.sum_ref, f32[64,192]{1,0:T(8,128)S(1)} %get-tuple-element.19.share_ref, ...), custom_call_target="tpu_custom_call" | custom-call | tf_op jit(solution)/shard_map/pallas_call | solution.py:21
  (4 shorter events, 0.1 us)
Async XLA Ops:
  0.6 1.1 %copy-start.2 = (bf16[512,192]{0,1:T(8,128)(2,1)S(1)}, bf16[512,192]{0,1:T(8,128)(2,1)}, u32[]{:S(2)}) copy-start(bf16[512,192]{0,1:T(8,128)(2,1)} %param.7) | copy-start | bytes 589828
  0.6 4.0 %collective-permute-start = (bf16[192,512]{1,0:T(8,128)(2,1)}, bf16[192,512]{1,0:T(8,128)(2,1)S(1)}, u32[]{:S(2)}, u32[]{:S(2)}) collective-permute-start(bf16[192,512]{1,0:T(8,128)(2,1)} %bitcast.7), channel_id=1, source_target_pairs={{0,1},{1,0},{2,3},{3,2},{4,5},{5,4},{6,7},{7,6},{8,9},{9,8},{10,11... | collective-permute-start | bytes 589832 | tf_op jit(solution)/shard_map/ppermute | solution.py:295
  1.2 5.6 %collective-permute-start.2 = (bf16[768,768]{1,0:T(8,128)(2,1)}, bf16[768,768]{1,0:T(8,128)(2,1)S(1)}, u32[]{:S(2)}, u32[]{:S(2)}) collective-permute-start(bf16[768,768]{1,0:T(8,128)(2,1)} %u0.7), channel_id=1, source_target_pairs={{0,1},{1,0},{2,3},{3,2},{4,5},{5,4},{6,7},{7,6},{8,9},{9,8},{10,11... | collective-permute-start | bytes 3538952 | tf_op jit(solution)/shard_map/ppermute | solution.py:295
  1.2 8.0 %collective-permute-start.3 = (bf16[768,768]{1,0:T(8,128)(2,1)}, bf16[768,768]{1,0:T(8,128)(2,1)S(1)}, u32[]{:S(2)}, u32[]{:S(2)}) collective-permute-start(bf16[768,768]{1,0:T(8,128)(2,1)} %d0.3), channel_id=1, source_target_pairs={{0,1},{1,0},{2,3},{3,2},{4,5},{5,4},{6,7},{7,6},{8,9},{9,8},{10,11... | collective-permute-start | bytes 3538952 | tf_op jit(solution)/shard_map/ppermute | solution.py:295
  1.7 5.0 %copy-start.6 = (f32[768]{0:T(1024)S(1)}, f32[768]{0:T(1024)}, u32[]{:S(2)}) copy-start(f32[768]{0:T(1024)} %param.10) | copy-start | bytes 9220
  1.7 5.0 %copy-start = (bf16[768,768]{1,0:T(8,128)(2,1)S(1)}, bf16[768,768]{1,0:T(8,128)(2,1)}, u32[]{:S(2)}) copy-start(bf16[768,768]{1,0:T(8,128)(2,1)} %u0.7) | copy-start | bytes 3538948
  1.7 5.4 %collective-permute-start.4 = (bf16[192,128]{1,0:T(8,128)(2,1)S(1)}, bf16[192,128]{1,0:T(8,128)(2,1)S(1)}, u32[]{:S(2)}, u32[]{:S(2)}) collective-permute-start(bf16[192,128]{1,0:T(8,128)(2,1)S(1)} %shard_map.98), channel_id=1, source_target_pairs={{0,2},{1,3},{2,0},{3,1},{4,6},{5,7},{6,4},{7,5},{8,10},{9,11},{10,... | collective-permute-start | bytes 147464 | tf_op jit(solution)/shard_map/ppermute | solution.py:295
  4.6 4.6 %collective-permute-start.5 = (bf16[192,128]{1,0:T(8,128)(2,1)S(1)}, bf16[192,128]{1,0:T(8,128)(2,1)S(1)}, u32[]{:S(2)}, u32[]{:S(2)}) collective-permute-start(bf16[192,128]{1,0:T(8,128)(2,1)S(1)} %get-tuple-element.15), channel_id=1, source_target_pairs={{0,2},{1,3},{2,0},{3,1},{4,6},{5,7},{6,4},{7,5},{8,10},{9,11},{10,... | collective-permute-start | bytes 147464 | tf_op jit(solution)/shard_map/ppermute | solution.py:295
  5.4 5.8 %collective-permute-start.1 = (bf16[384,128]{1,0:T(8,128)(2,1)S(1)}, bf16[384,128]{1,0:T(8,128)(2,1)S(1)}, u32[]{:S(2)}, u32[]{:S(2)}) collective-permute-start(bf16[384,128]{1,0:T(8,128)(2,1)S(1)} %get-tuple-element.13), channel_id=1, source_target_pairs={{0,2},{1,3},{2,0},{3,1},{4,6},{5,7},{6,4},{7,5},{8,10},{9,11},{10,... | collective-permute-start | bytes 294920 | tf_op jit(solution)/shard_map/ppermute | solution.py:295
  7.2 2.1 %copy-start.1 = (bf16[768,768]{1,0:T(8,128)(2,1)S(1)}, bf16[768,768]{1,0:T(8,128)(2,1)}, u32[]{:S(2)}) copy-start(bf16[768,768]{1,0:T(8,128)(2,1)} %d0.3) | copy-start | bytes 3538948
  7.5 3.7 %copy-start.3 = (s32[32]{0:T(128)S(1)}, s32[32]{0:T(128)}, u32[]{:S(2)}) copy-start(s32[32]{0:T(128)} %param.11) | copy-start | bytes 388
  7.5 3.7 %copy-start.4 = (s32[32]{0:T(128)S(1)}, s32[32]{0:T(128)}, u32[]{:S(2)}) copy-start(s32[32]{0:T(128)} %param.12) | copy-start | bytes 388
  7.5 3.7 %copy-start.5 = (s32[8]{0:T(128)S(1)}, s32[8]{0:T(128)}, u32[]{:S(2)}) copy-start(s32[8]{0:T(128)} %param.13) | copy-start | bytes 100
  10.1 5.7 %collective-permute-start.6 = (bf16[128,768]{1,0:T(8,128)(2,1)S(1)}, bf16[128,768]{1,0:T(8,128)(2,1)S(1)}, u32[]{:S(2)}, u32[]{:S(2)}) collective-permute-start(bf16[128,768]{1,0:T(8,128)(2,1)S(1)} %shard_map.100), channel_id=1, source_target_pairs={{0,2},{1,3},{2,0},{3,1},{4,6},{5,7},{6,4},{7,5},{8,10},{9,11},{10,... | collective-permute-start | bytes 589832 | tf_op jit(solution)/shard_map/ppermute | solution.py:295
  27.9 1.5 %collective-permute-start.7 = (bf16[128,896]{1,0:T(8,128)(2,1)S(1)}, bf16[128,896]{1,0:T(8,128)(2,1)S(1)}, u32[]{:S(2)}, u32[]{:S(2)}) collective-permute-start(bf16[128,896]{1,0:T(8,128)(2,1)S(1)} %bitcast.5), channel_id=1, source_target_pairs={{0,1},{1,0},{2,3},{3,2},{4,5},{5,4},{6,7},{7,6},{8,9},{9,8},{10,11... | collective-permute-start | bytes 688136 | tf_op jit(solution)/shard_map/ppermute | solution.py:295

commit v10 on v9

--- a/solution.py
+++ b/solution.py
@@ -264,11 +264,6 @@
     leaf_share = share_ref[...] + jnp.dot(picker, far_share, preferred_element_type=jnp.float32)
     squares = jnp.mean(leaf_sum * leaf_sum, axis=1, keepdims=True)
     centers = leaf_share * lax.rsqrt(squares + 1e-05)
-    scratch[...] = centers
-    own = pl.ds(pl.multiple_of(upper // 2 * leaf_count, leaf_count), leaf_count)
-    centers_ref[...] = scratch[own, :]
-    centers_copy = pltpu.make_async_copy(centers_ref, centers_out, sems.at[1])
-    centers_copy.start()
     parent = parent_ref[:, :1].astype(jnp.int32)
     sums = [
         jnp.sum(jnp.where(parent == index * PAR_DEV + p, centers, 0.0), axis=0, keepdims=True)
@@ -277,6 +272,11 @@
     parents_ref[...] = jnp.concatenate(sums, axis=0)
     parents_copy = pltpu.make_async_copy(parents_ref, parents_out, sems.at[2])
     parents_copy.start()
+    scratch[...] = centers
+    own = pl.ds(pl.multiple_of(upper // 2 * leaf_count, leaf_count), leaf_count)
+    centers_ref[...] = scratch[own, :]
+    centers_copy = pltpu.make_async_copy(centers_ref, centers_out, sems.at[1])
+    centers_copy.start()
     embed_copy.wait()
     centers_copy.wait()
     parents_copy.wait()

time: 30.6 us -> 30.6 us (level)
  no operation moved by 1% of the time
where the time goes in v10:
time: 30.6 us; the launch traced here: 30.4 us
  blocking collectives  11.7 us (38%)
  starting transfers between devices  7.08 us (23%)
  waiting for transfers between devices  6.19 us (20%)
  Pallas kernels  4.61 us (15%)
  between operations  0.79 us (3%)
    all_to_all x1, blocking collectives, local(): lax.all_to_all(message, ('labels', 'heads'), split_axis=0, concat_axis=0,...  11.7 us
    ppermute x8, starting transfers between devices, swap(): return lax.ppermute(values, 'heads', [(i, i ^ flip) for i in range(heads)])  7.08 us
    ppermute x8, waiting for transfers between devices, swap(): return lax.ppermute(values, 'heads', [(i, i ^ flip) for i in range(heads)])  6.19 us
    pallas_call x10, Pallas kernels, call(): pl.pallas_call(kernel, out_shape=out_shape, in_specs=[VMEM] * len(operand...  4.61 us
  transfers between devices with their start and end apart: 8, of which 3 were waited for; matrix products, arithmetic and copies ran while one was open for 0% of the time, Pallas kernels for 11%

profile of v10, /device:TPU:0, one launch (start us, length us, event | category | flops | bytes accessed | tf_op | source)
XLA Modules:
  0.0 30.4 jit_solution(17735906959571747478)
XLA Ops:
  0.6 0.0 copy-start.2
  0.6 0.5 %collective-permute-start = (bf16[192,512]{1,0:T(8,128)(2,1)}, bf16[192,512]{1,0:T(8,128)(2,1)S(1)}, u32[]{:S(2)}, u32[]{:S(2)}) collective-permute-start(bf16[192,512]{1,0:T(8,128)(2,1)} %bitcast.7), channel_id=1, source_target_pairs={{0,1},{1,0},{2,3},{3,2},{4,5},{5,4},{6,7},{7,6},{8,9},{9,8},{10,11... | collective-permute-start | bytes 589832 | tf_op jit(solution)/shard_map/ppermute | solution.py:295
  1.2 0.1 collective-permute-start.2
  1.2 0.4 %collective-permute-start.3 = (bf16[768,768]{1,0:T(8,128)(2,1)}, bf16[768,768]{1,0:T(8,128)(2,1)S(1)}, u32[]{:S(2)}, u32[]{:S(2)}) collective-permute-start(bf16[768,768]{1,0:T(8,128)(2,1)} %d0.3), channel_id=1, source_target_pairs={{0,1},{1,0},{2,3},{3,2},{4,5},{5,4},{6,7},{7,6},{8,9},{9,8},{10,11... | collective-permute-start | bytes 3538952 | tf_op jit(solution)/shard_map/ppermute | solution.py:295
  1.7 0.0 copy-done.2
  1.7 0.0 copy-start.6
  1.7 0.0 copy-start
  1.7 2.9 %collective-permute-start.4 = (bf16[192,128]{1,0:T(8,128)(2,1)S(1)}, bf16[192,128]{1,0:T(8,128)(2,1)S(1)}, u32[]{:S(2)}, u32[]{:S(2)}) collective-permute-start(bf16[192,128]{1,0:T(8,128)(2,1)S(1)} %shard_map.98), channel_id=1, source_target_pairs={{0,2},{1,3},{2,0},{3,1},{4,6},{5,7},{6,4},{7,5},{8,10},{9,11},{10,... | collective-permute-start | bytes 147464 | tf_op jit(solution)/shard_map/ppermute | solution.py:295
  4.6 0.0 collective-permute-done.beside_ref
  4.6 0.8 %collective-permute-start.5 = (bf16[192,128]{1,0:T(8,128)(2,1)S(1)}, bf16[192,128]{1,0:T(8,128)(2,1)S(1)}, u32[]{:S(2)}, u32[]{:S(2)}) collective-permute-start(bf16[192,128]{1,0:T(8,128)(2,1)S(1)} %get-tuple-element.15), channel_id=1, source_target_pairs={{0,2},{1,3},{2,0},{3,1},{4,6},{5,7},{6,4},{7,5},{8,10},{9,11},{10,... | collective-permute-start | bytes 147464 | tf_op jit(solution)/shard_map/ppermute | solution.py:295
  5.4 1.3 %collective-permute-start.1 = (bf16[384,128]{1,0:T(8,128)(2,1)S(1)}, bf16[384,128]{1,0:T(8,128)(2,1)S(1)}, u32[]{:S(2)}, u32[]{:S(2)}) collective-permute-start(bf16[384,128]{1,0:T(8,128)(2,1)S(1)} %get-tuple-element.13), channel_id=1, source_target_pairs={{0,2},{1,3},{2,0},{3,1},{4,6},{5,7},{6,4},{7,5},{8,10},{9,11},{10,... | collective-permute-start | bytes 294920 | tf_op jit(solution)/shard_map/ppermute | solution.py:295
  6.7 0.0 copy-done.6
  6.7 0.0 collective-permute-done.2.u1
  6.7 0.0 copy-done
  6.7 0.4 %shard_map.97.early_ref = f32[2,128,768]{2,1,0:T(8,128)S(1)} custom-call(bf16[192,512]{1,0:T(8,128)(2,1)S(1)} %bitcast.10, bf16[192,512]{1,0:T(8,128)(2,1)S(1)} %collective-permute-done.beside_ref, bf16[768,768]{1,0:T(8,128)(2,1)S(1)} %copy-done, bf16[768,768]{1,0:T(8,128)(2,1)S(1)} %collective-permute-done.2.u1), custom_call_target="tpu_custom_call" | custom-call | tf_op jit(solution)/shard_map/pallas_call | solution.py:21
  7.2 0.0 copy-start.1
  7.2 0.0 collective-permute-done.4.across_ref
  7.2 0.3 shard_map.99.early_ref
  7.5 0.0 copy-start.3
  7.5 0.0 copy-start.4
  7.5 0.0 copy-start.5
  7.5 1.7 %collective-permute-done.5.diagonal_ref = bf16[192,128]{1,0:T(8,128)(2,1)S(1)} collective-permute-done((bf16[192,128]{1,0:T(8,128)(2,1)S(1)}, bf16[192,128]{1,0:T(8,128)(2,1)S(1)}, u32[]{:S(2)}, u32[]{:S(2)}) %collective-permute-start.5) | collective-permute-done | bytes 49184 | tf_op jit(solution)/shard_map/ppermute | solution.py:295
  9.2 0.0 collective-permute-done.3.d1
  9.2 0.0 copy-done.1
  9.2 0.9 %shard_map.100 = bf16[128,768]{1,0:T(8,128)(2,1)S(1)} custom-call(f32[2,128,768]{2,1,0:T(8,128)S(1)} %shard_map.99.early_ref, bf16[192,128]{1,0:T(8,128)(2,1)S(1)} %collective-permute-done.5.diagonal_ref, bf16[768,768]{1,0:T(8,128)(2,1)S(1)} %copy-done, bf16[768,768]{1,0:T(8,128)(2,1)S(1)} %copy-done.1, bf16[768,768]{1,0:T(8,128)(2,1)S(1)} %collective-permute-done.2.u1, ...), custom_call_target="tpu_custom_call" | custom-call | flops 603979776 | bytes 4718592 | tf_op jit(solution)/shard_map/pallas_call | solution.py:21
  10.1 1.1 %collective-permute-start.6 = (bf16[128,768]{1,0:T(8,128)(2,1)S(1)}, bf16[128,768]{1,0:T(8,128)(2,1)S(1)}, u32[]{:S(2)}, u32[]{:S(2)}) collective-permute-start(bf16[128,768]{1,0:T(8,128)(2,1)S(1)} %shard_map.100), channel_id=1, source_target_pairs={{0,2},{1,3},{2,0},{3,1},{4,6},{5,7},{6,4},{7,5},{8,10},{9,11},{10,... | collective-permute-start | bytes 589832 | tf_op jit(solution)/shard_map/ppermute | solution.py:295
  11.2 0.0 collective-permute-done.1.across_ref
  11.2 0.0 copy-done.3
  11.2 0.0 copy-done.4
  11.2 0.0 copy-done.5
  11.2 1.1 %shard_map.96 = (f32[128,768]{1,0:T(8,128)S(1)}, f32[128,128]{1,0:T(8,128)S(1)}, f32[8,128]{1,0:T(8,128)S(1)}) custom-call(bf16[192,512]{1,0:T(8,128)(2,1)S(1)} %bitcast.11, bf16[192,512]{1,0:T(8,128)(2,1)S(1)} %collective-permute-done.beside_ref, bf16[384,128]{1,0:T(8,128)(2,1)S(1)} %collective-permute-done.1.across_ref, bf16[768,768]{1,0:T(8,128)(2,1)S(1)} %copy-done, ...), custom_call_target="tpu_custom_call" | custom-call | flops 10000000000 | bytes 4718592 | tf_op jit(solution)/shard_map/pallas_call | solution.py:21
  12.3 3.5 %collective-permute-done.6.came_ref = bf16[128,768]{1,0:T(8,128)(2,1)S(1)} collective-permute-done((bf16[128,768]{1,0:T(8,128)(2,1)S(1)}, bf16[128,768]{1,0:T(8,128)(2,1)S(1)}, u32[]{:S(2)}, u32[]{:S(2)}) %collective-permute-start.6) | collective-permute-done | bytes 196640 | tf_op jit(solution)/shard_map/ppermute | solution.py:295
  15.8 0.4 %shard_map.101 = bf16[16,8,896]{2,1,0:T(8,128)(2,1)S(1)} custom-call(f32[128,768]{1,0:T(8,128)S(1)} %get-tuple-element.14.kept_ref, bf16[128,768]{1,0:T(8,128)(2,1)S(1)} %collective-permute-done.6.came_ref, f32[128,128]{1,0:T(8,128)S(1)} %get-tuple-element.16.weight_ref, f32[8,128]{1,0:T(8,128)S(1)} %get-tuple-element.17.digits_ref, ...), custom_call_target="tpu_custom_call" | custom-call | tf_op jit(solution)/shard_map/pallas_call | solution.py:21
  16.2 11.7 %all_to_all.5 = bf16[16,8,896]{2,1,0:T(8,128)(2,1)S(1)} all-to-all(bf16[16,8,896]{2,1,0:T(8,128)(2,1)S(1)} %shard_map.101), channel_id=1, replica_groups={{30,12,18,0,14,24,2,20,26,8,22,4,10,28,6,16},{31,13,19,1,15,25,3,21,27,..., dimensions={0} | all-to-all | bytes 458752 | tf_op jit(solution)/shard_map/all_to_all | solution.py:363
  27.9 0.0 collective-permute-start.7
  27.9 0.5 %shard_map.102 = (f32[64,768]{1,0:T(8,128)S(1)}, f32[64,192]{1,0:T(8,128)S(1)}, bf16[64,128]{1,0:T(8,128)(2,1)S(1)}, f32[64,128]{1,0:T(8,128)S(1)}, f32[16,768]{1,0:T(8,128)S(1)}) custom-call(bf16[128,896]{1,0:T(8,128)(2,1)S(1)} %bitcast.6), custom_call_target="tpu_custom_call" | custom-call | tf_op jit(solution)/shard_map/pallas_call | solution.py:21
  28.4 1.0 %collective-permute-done.7.far_ref = bf16[128,896]{1,0:T(8,128)(2,1)S(1)} collective-permute-done((bf16[128,896]{1,0:T(8,128)(2,1)S(1)}, bf16[128,896]{1,0:T(8,128)(2,1)S(1)}, u32[]{:S(2)}, u32[]{:S(2)}) %collective-permute-start.7) | collective-permute-done | bytes 229408 | tf_op jit(solution)/shard_map/ppermute | solution.py:295
  29.4 1.0 %shard_map.103 = (bf16[32,768]{1,0:T(8,128)(2,1)}, f32[8,192]{1,0:T(8,128)}, f32[2,192]{1,0:T(2,128)}) custom-call(bf16[128,896]{1,0:T(8,128)(2,1)S(1)} %collective-permute-done.7.far_ref, f32[64,768]{1,0:T(8,128)S(1)} %get-tuple-element.18.sum_ref, f32[64,192]{1,0:T(8,128)S(1)} %get-tuple-element.19.share_ref, ...), custom_call_target="tpu_custom_call" | custom-call | tf_op jit(solution)/shard_map/pallas_call | solution.py:21
  (4 shorter events, 0.1 us)
Async XLA Ops:
  0.6 1.1 %copy-start.2 = (bf16[512,192]{0,1:T(8,128)(2,1)S(1)}, bf16[512,192]{0,1:T(8,128)(2,1)}, u32[]{:S(2)}) copy-start(bf16[512,192]{0,1:T(8,128)(2,1)} %param.7) | copy-start | bytes 589828
  0.6 4.0 %collective-permute-start = (bf16[192,512]{1,0:T(8,128)(2,1)}, bf16[192,512]{1,0:T(8,128)(2,1)S(1)}, u32[]{:S(2)}, u32[]{:S(2)}) collective-permute-start(bf16[192,512]{1,0:T(8,128)(2,1)} %bitcast.7), channel_id=1, source_target_pairs={{0,1},{1,0},{2,3},{3,2},{4,5},{5,4},{6,7},{7,6},{8,9},{9,8},{10,11... | collective-permute-start | bytes 589832 | tf_op jit(solution)/shard_map/ppermute | solution.py:295
  1.2 5.6 %collective-permute-start.2 = (bf16[768,768]{1,0:T(8,128)(2,1)}, bf16[768,768]{1,0:T(8,128)(2,1)S(1)}, u32[]{:S(2)}, u32[]{:S(2)}) collective-permute-start(bf16[768,768]{1,0:T(8,128)(2,1)} %u0.7), channel_id=1, source_target_pairs={{0,1},{1,0},{2,3},{3,2},{4,5},{5,4},{6,7},{7,6},{8,9},{9,8},{10,11... | collective-permute-start | bytes 3538952 | tf_op jit(solution)/shard_map/ppermute | solution.py:295
  1.2 8.0 %collective-permute-start.3 = (bf16[768,768]{1,0:T(8,128)(2,1)}, bf16[768,768]{1,0:T(8,128)(2,1)S(1)}, u32[]{:S(2)}, u32[]{:S(2)}) collective-permute-start(bf16[768,768]{1,0:T(8,128)(2,1)} %d0.3), channel_id=1, source_target_pairs={{0,1},{1,0},{2,3},{3,2},{4,5},{5,4},{6,7},{7,6},{8,9},{9,8},{10,11... | collective-permute-start | bytes 3538952 | tf_op jit(solution)/shard_map/ppermute | solution.py:295
  1.7 5.0 %copy-start.6 = (f32[768]{0:T(1024)S(1)}, f32[768]{0:T(1024)}, u32[]{:S(2)}) copy-start(f32[768]{0:T(1024)} %param.10) | copy-start | bytes 9220
  1.7 5.0 %copy-start = (bf16[768,768]{1,0:T(8,128)(2,1)S(1)}, bf16[768,768]{1,0:T(8,128)(2,1)}, u32[]{:S(2)}) copy-start(bf16[768,768]{1,0:T(8,128)(2,1)} %u0.7) | copy-start | bytes 3538948
  1.7 5.4 %collective-permute-start.4 = (bf16[192,128]{1,0:T(8,128)(2,1)S(1)}, bf16[192,128]{1,0:T(8,128)(2,1)S(1)}, u32[]{:S(2)}, u32[]{:S(2)}) collective-permute-start(bf16[192,128]{1,0:T(8,128)(2,1)S(1)} %shard_map.98), channel_id=1, source_target_pairs={{0,2},{1,3},{2,0},{3,1},{4,6},{5,7},{6,4},{7,5},{8,10},{9,11},{10,... | collective-permute-start | bytes 147464 | tf_op jit(solution)/shard_map/ppermute | solution.py:295
  4.6 4.6 %collective-permute-start.5 = (bf16[192,128]{1,0:T(8,128)(2,1)S(1)}, bf16[192,128]{1,0:T(8,128)(2,1)S(1)}, u32[]{:S(2)}, u32[]{:S(2)}) collective-permute-start(bf16[192,128]{1,0:T(8,128)(2,1)S(1)} %get-tuple-element.15), channel_id=1, source_target_pairs={{0,2},{1,3},{2,0},{3,1},{4,6},{5,7},{6,4},{7,5},{8,10},{9,11},{10,... | collective-permute-start | bytes 147464 | tf_op jit(solution)/shard_map/ppermute | solution.py:295
  5.4 5.8 %collective-permute-start.1 = (bf16[384,128]{1,0:T(8,128)(2,1)S(1)}, bf16[384,128]{1,0:T(8,128)(2,1)S(1)}, u32[]{:S(2)}, u32[]{:S(2)}) collective-permute-start(bf16[384,128]{1,0:T(8,128)(2,1)S(1)} %get-tuple-element.13), channel_id=1, source_target_pairs={{0,2},{1,3},{2,0},{3,1},{4,6},{5,7},{6,4},{7,5},{8,10},{9,11},{10,... | collective-permute-start | bytes 294920 | tf_op jit(solution)/shard_map/ppermute | solution.py:295
  7.2 2.1 %copy-start.1 = (bf16[768,768]{1,0:T(8,128)(2,1)S(1)}, bf16[768,768]{1,0:T(8,128)(2,1)}, u32[]{:S(2)}) copy-start(bf16[768,768]{1,0:T(8,128)(2,1)} %d0.3) | copy-start | bytes 3538948
  7.5 3.7 %copy-start.3 = (s32[32]{0:T(128)S(1)}, s32[32]{0:T(128)}, u32[]{:S(2)}) copy-start(s32[32]{0:T(128)} %param.11) | copy-start | bytes 388
  7.5 3.7 %copy-start.4 = (s32[32]{0:T(128)S(1)}, s32[32]{0:T(128)}, u32[]{:S(2)}) copy-start(s32[32]{0:T(128)} %param.12) | copy-start | bytes 388
  7.5 3.7 %copy-start.5 = (s32[8]{0:T(128)S(1)}, s32[8]{0:T(128)}, u32[]{:S(2)}) copy-start(s32[8]{0:T(128)} %param.13) | copy-start | bytes 100
  10.1 5.7 %collective-permute-start.6 = (bf16[128,768]{1,0:T(8,128)(2,1)S(1)}, bf16[128,768]{1,0:T(8,128)(2,1)S(1)}, u32[]{:S(2)}, u32[]{:S(2)}) collective-permute-start(bf16[128,768]{1,0:T(8,128)(2,1)S(1)} %shard_map.100), channel_id=1, source_target_pairs={{0,2},{1,3},{2,0},{3,1},{4,6},{5,7},{6,4},{7,5},{8,10},{9,11},{10,... | collective-permute-start | bytes 589832 | tf_op jit(solution)/shard_map/ppermute | solution.py:295
  27.9 1.5 %collective-permute-start.7 = (bf16[128,896]{1,0:T(8,128)(2,1)S(1)}, bf16[128,896]{1,0:T(8,128)(2,1)S(1)}, u32[]{:S(2)}, u32[]{:S(2)}) collective-permute-start(bf16[128,896]{1,0:T(8,128)(2,1)S(1)} %bitcast.5), channel_id=1, source_target_pairs={{0,1},{1,0},{2,3},{3,2},{4,5},{5,4},{6,7},{7,6},{8,9},{9,8},{10,11... | collective-permute-start | bytes 688136 | tf_op jit(solution)/shard_map/ppermute | solution.py:295
